TPU v7x, 32 devices: a whole 2x2x4 slice. The times are simulated.
32 devices in a mesh: dp: 16 (over z, x, core), tensor: 2 (over y).
Axes of the slice: x: 2, y: 2, z: 4, core: 2. Of those that a mesh axis runs over, the one named last changes fastest.
Arguments:
- tokens: bfloat16 [5120, 2048], P('dp'), may hold values from -6 to 6
- cotangent: bfloat16 [5120, 2048], P('dp'), may hold values from -6 to 6
- route_ids: int32 [5120, 6], P('dp'), may hold values from 0 to 15, all different within a row; in each aligned block of 320 rows (0 to 319, 320 to 639, ...) at most 160 rows name the same one
- route_gates: float32 [5120, 6], P('dp'), may hold values from 0.08 to 0.32
- gain_first: bfloat16 [2048], P('dp'), may hold values from 0.5 to 1.5
- w_query: bfloat16 [2048, 2048], P('dp', 'tensor'), may hold values from -0.125 to 0.125
- w_key: bfloat16 [2048, 2048], P('dp', 'tensor'), may hold values from -0.125 to 0.125
- w_value: bfloat16 [2048, 2048], P('dp', 'tensor'), may hold values from -0.125 to 0.125
- w_output: bfloat16 [2048, 2048], P('dp', 'tensor'), may hold values from -0.5 to 0.5
- gain_second: bfloat16 [2048], P('dp'), may hold values from 0.5 to 1.5
- shared_gate: bfloat16 [2048, 2816], P('dp', 'tensor'), may hold values from -0.125 to 0.125
- shared_up: bfloat16 [2048, 2816], P('dp', 'tensor'), may hold values from -0.125 to 0.125
- shared_down: bfloat16 [2048, 2816], P('dp', 'tensor'), may hold values from -0.109375 to 0.109375
- expert_gate: bfloat16 [16, 2048, 1408], P('dp', None, 'tensor'), may hold values from -0.125 to 0.125
- expert_up: bfloat16 [16, 2048, 1408], P('dp', None, 'tensor'), may hold values from -0.125 to 0.125
- expert_down: bfloat16 [16, 1408, 2048], P('dp', 'tensor'), may hold values from -0.15625 to 0.15625
Outputs:
- layer_out: bfloat16 [5120, 2048], P('dp')
- tokens_grad: bfloat16 [5120, 2048], P('dp')
- gain_first_grad: float32 [2048], P('dp')
- query_grad: float32 [2048, 2048], P('dp', 'tensor')
- key_grad: float32 [2048, 2048], P('dp', 'tensor')
- value_grad: float32 [2048, 2048], P('dp', 'tensor')
- output_grad: float32 [2048, 2048], P('dp', 'tensor')
- gain_second_grad: float32 [2048], P('dp')
- shared_gate_grad: float32 [2048, 2816], P('dp', 'tensor')
- shared_up_grad: float32 [2048, 2816], P('dp', 'tensor')
- shared_down_grad: float32 [2048, 2816], P('dp', 'tensor')
- expert_gate_grad: float32 [16, 2048, 1408], P('dp', None, 'tensor')
- expert_up_grad: float32 [16, 2048, 1408], P('dp', None, 'tensor')
- expert_down_grad: float32 [16, 1408, 2048], P('dp', 'tensor')
Inputs may be any that keep to these rules, and one draw needn't show every extreme that they name: `route_ids`: each row names 6 different experts. Among the 320 rows of one index of dp no expert is named by more than 160 rows, and in the rows of some index one expert is named by exactly 160.
All inputs are finite; a program needn't handle non-finite values.
Results may differ from a plain program's by a relative error of at most 0.014.
Values may be sent and summed in bfloat16 or wider, within the bound.
A program may use at most 320 MiB of HBM per device.

v0:
```python
import functools

import jax
import jax.numpy as jnp
from jax import lax
from jax.experimental import pallas as pl
from jax.experimental.pallas import tpu as pltpu
from jax.sharding import PartitionSpec as P

HD = 128
MESH = pl.DeviceIdType.MESH


EPS = 1e-06


def rms_norm(values, gain):
    mean_square = jnp.mean(values * values, axis=-1, keepdims=True)
    return values * lax.rsqrt(mean_square + EPS) * gain


def rotate(values, positions):
    head = values.shape[-1]
    half = head // 2
    freqs = 10000.0 ** (-2.0 * jnp.arange(half, dtype=jnp.float32) / head)
    angles = positions[:, None] * freqs[None, :]
    cosine = jnp.cos(angles)[:, None, :]
    sine = jnp.sin(angles)[:, None, :]
    first = values[..., :half]
    second = values[..., half:]
    return jnp.concatenate(
        [first * cosine - second * sine, second * cosine + first * sine], axis=-1
    )


def gated(gate_pre, up_pre):
    return gate_pre * jax.nn.sigmoid(gate_pre) * up_pre


def contract_last(left, right):
    return lax.dot_general(
        left, right, (((1,), (1,)), ((), ())), preferred_element_type=jnp.float32
    )


def contract_first(left, right):
    return lax.dot_general(
        left, right, (((0,), (0,)), ((), ())), preferred_element_type=jnp.float32
    )


def masked_scores(query_rot, key_rot, causal, scale):
    scores = (
        jnp.einsum("qhc,khc->hqk", query_rot, key_rot, preferred_element_type=jnp.float32) * scale
    )
    return jnp.where(causal[None], scores, -1e30)


def on_device_plain(
    tokens,
    cotangent,
    route_ids,
    route_gates,
    gain_first,
    w_query,
    w_key,
    w_value,
    w_output,
    gain_second,
    shared_gate,
    shared_up,
    shared_down,
    expert_gate,
    expert_up,
    expert_down,
):
    rows_dev, width = tokens.shape
    topk = route_ids.shape[1]
    experts = lax.axis_size("dp")
    capacity = rows_dev * topk * 4 // (3 * experts)
    slots = experts * capacity
    scale = HD ** (-0.5)
    positions = jnp.arange(rows_dev, dtype=jnp.float32)
    causal = jnp.arange(rows_dev)[:, None] >= jnp.arange(rows_dev)[None, :]
    gain_one, query_whole, key_whole, value_whole, output_whole = (
        lax.all_gather(gain_first, "dp", axis=0, tiled=True),
        lax.all_gather(w_query, "dp", axis=0, tiled=True),
        lax.all_gather(w_key, "dp", axis=0, tiled=True),
        lax.all_gather(w_value, "dp", axis=0, tiled=True),
        lax.all_gather(w_output, "dp", axis=0, tiled=True),
    )
    gain_two, common_gate, common_up, common_down = (
        lax.all_gather(gain_second, "dp", axis=0, tiled=True),
        lax.all_gather(shared_gate, "dp", axis=0, tiled=True),
        lax.all_gather(shared_up, "dp", axis=0, tiled=True),
        lax.all_gather(shared_down, "dp", axis=0, tiled=True),
    )
    gain_one = gain_one.astype(jnp.float32)
    gain_two = gain_two.astype(jnp.float32)
    x_in = tokens.astype(jnp.float32)
    act_one = rms_norm(x_in, gain_one).astype(jnp.bfloat16)
    heads_dev = query_whole.shape[1] // HD
    query_pre = jnp.dot(act_one, query_whole, preferred_element_type=jnp.float32).reshape(
        rows_dev, heads_dev, HD
    )
    key_pre = jnp.dot(act_one, key_whole, preferred_element_type=jnp.float32).reshape(
        rows_dev, heads_dev, HD
    )
    query_rot = rotate(query_pre, positions).astype(jnp.bfloat16)
    key_rot = rotate(key_pre, positions).astype(jnp.bfloat16)
    value_low = (
        jnp.dot(act_one, value_whole, preferred_element_type=jnp.float32)
        .astype(jnp.bfloat16)
        .reshape(rows_dev, heads_dev, HD)
    )
    scores = masked_scores(query_rot, key_rot, causal, scale)
    top = jnp.max(scores, axis=-1, keepdims=True)
    expo = jnp.exp(scores - top)
    total = jnp.sum(expo, axis=-1, keepdims=True)
    probs = expo / total
    log_total = top + jnp.log(total)
    mixed = jnp.einsum(
        "hqk,khc->qhc", probs.astype(jnp.bfloat16), value_low, preferred_element_type=jnp.float32
    )
    mixed = mixed.reshape(rows_dev, heads_dev * HD).astype(jnp.bfloat16)
    attn = lax.psum(contract_last(mixed, output_whole), "tensor")
    x_mid = x_in + attn
    act_two = rms_norm(x_mid, gain_two).astype(jnp.bfloat16)
    gate_pre = jnp.dot(act_two, common_gate, preferred_element_type=jnp.float32)
    up_pre = jnp.dot(act_two, common_up, preferred_element_type=jnp.float32)
    hidden_common = gated(gate_pre, up_pre).astype(jnp.bfloat16)
    common_out = contract_last(hidden_common, common_down)
    flat_ids = route_ids.reshape(-1)
    onehot = (flat_ids[:, None] == jnp.arange(experts, dtype=jnp.int32)[None, :]).astype(jnp.int32)
    ranks = jnp.sum(onehot * jnp.cumsum(onehot, axis=0), axis=1) - 1
    dest = flat_ids * capacity + ranks
    token_of = jnp.arange(rows_dev * topk, dtype=jnp.int32) // topk
    source = jnp.zeros((slots,), jnp.int32).at[dest].set(token_of)
    weight_of = jnp.zeros((slots,), jnp.float32).at[dest].set(route_gates.reshape(-1))
    filled = jnp.zeros((slots,), jnp.bool_).at[dest].set(True)
    outgoing = jnp.where(filled[:, None], act_two[source], jnp.zeros((), jnp.bfloat16)).reshape(
        experts, capacity, width
    )
    exp_gate = expert_gate[0]
    exp_up = expert_up[0]
    exp_down = expert_down[0]
    received = lax.all_to_all(outgoing, "dp", split_axis=0, concat_axis=0, tiled=True)
    sources = received.shape[0]
    count = received.shape[1]
    rows = received.reshape(sources * count, width)
    gate_rows = jnp.dot(rows, exp_gate, preferred_element_type=jnp.float32)
    up_rows = jnp.dot(rows, exp_up, preferred_element_type=jnp.float32)
    hidden_rows = gated(gate_rows, up_rows).astype(jnp.bfloat16)
    partial_value = jnp.dot(hidden_rows, exp_down, preferred_element_type=jnp.float32).reshape(
        sources, count, width
    )
    returned = lax.all_to_all(
        partial_value.astype(jnp.bfloat16), "dp", split_axis=0, concat_axis=0, tiled=True
    ).astype(partial_value.dtype)
    returned, kept_rows, kept_gate, kept_up = (
        returned,
        received,
        gate_rows.reshape(sources, count, -1),
        up_rows.reshape(sources, count, -1),
    )
    picked = returned.reshape(slots, width)[dest].reshape(rows_dev, topk, width)
    routed_part = jnp.sum(picked * route_gates[:, :, None], axis=1)
    ffn = lax.psum((common_out + routed_part).astype(jnp.bfloat16), "tensor").astype(jnp.float32)
    layer_out = (x_mid + ffn).astype(jnp.bfloat16)
    grad_out = cotangent.astype(jnp.float32)
    hidden_grad = jnp.dot(cotangent, common_down, preferred_element_type=jnp.float32)
    dummy_common, common_vjp = jax.vjp(gated, gate_pre, up_pre)
    gate_grad, up_grad = common_vjp(hidden_grad)
    gate_grad = gate_grad.astype(jnp.bfloat16)
    up_grad = up_grad.astype(jnp.bfloat16)
    common_gate_grad = contract_first(act_two, gate_grad)
    common_up_grad = contract_first(act_two, up_grad)
    common_down_grad = contract_first(cotangent, hidden_common)
    act_two_grad = contract_last(gate_grad, common_gate) + contract_last(up_grad, common_up)
    outgoing_grad = (
        (weight_of[:, None] * grad_out[source])
        .astype(jnp.bfloat16)
        .reshape(experts, capacity, width)
    )
    incoming_grad = lax.all_to_all(outgoing_grad, "dp", split_axis=0, concat_axis=0, tiled=True)
    hidden_width = kept_gate.shape[2]
    rows = kept_rows.reshape(-1, width)
    rows_out_grad = incoming_grad.reshape(-1, width)
    hidden_rows, expert_vjp = jax.vjp(
        gated, kept_gate.reshape(-1, hidden_width), kept_up.reshape(-1, hidden_width)
    )
    hidden_rows = hidden_rows.astype(jnp.bfloat16)
    hidden_rows_grad = contract_last(rows_out_grad, exp_down)
    gate_rows_grad, up_rows_grad = expert_vjp(hidden_rows_grad)
    gate_rows_grad = gate_rows_grad.astype(jnp.bfloat16)
    up_rows_grad = up_rows_grad.astype(jnp.bfloat16)
    expert_gate_grad = contract_first(rows, gate_rows_grad)[None]
    expert_up_grad = contract_first(rows, up_rows_grad)[None]
    expert_down_grad = contract_first(hidden_rows, rows_out_grad)[None]
    rows_in_grad = (
        contract_last(gate_rows_grad, exp_gate) + contract_last(up_rows_grad, exp_up)
    ).reshape(experts, capacity, width)
    returned_grad = lax.all_to_all(rows_in_grad, "dp", split_axis=0, concat_axis=0, tiled=True)
    routed_grad = jnp.sum(
        returned_grad.reshape(slots, width)[dest].reshape(rows_dev, topk, width), axis=1
    )
    act_two_total = lax.psum(act_two_grad + routed_grad, "tensor")
    dummy_second, second_vjp = jax.vjp(rms_norm, x_mid, gain_two)
    mid_norm_grad, gain_two_grad = second_vjp(act_two_total)
    mid_grad = grad_out + mid_norm_grad
    ffn_sums = (gain_two_grad, common_gate_grad, common_up_grad, common_down_grad)
    attn_grad = mid_grad.astype(jnp.bfloat16)
    output_w_grad = contract_first(attn_grad, mixed)
    mixed_grad = (
        jnp.dot(attn_grad, output_whole, preferred_element_type=jnp.float32)
        .astype(jnp.bfloat16)
        .reshape(rows_dev, heads_dev, HD)
    )
    probs_again = jnp.exp(masked_scores(query_rot, key_rot, causal, scale) - log_total)
    value_grad = jnp.einsum(
        "hqk,qhc->khc",
        probs_again.astype(jnp.bfloat16),
        mixed_grad,
        preferred_element_type=jnp.float32,
    ).astype(jnp.bfloat16)
    prob_grad = jnp.einsum(
        "qhc,khc->hqk", mixed_grad, value_low, preferred_element_type=jnp.float32
    )
    delta = jnp.sum(probs_again * prob_grad, axis=-1, keepdims=True)
    score_grad = (probs_again * (prob_grad - delta)).astype(jnp.bfloat16)
    query_rot_grad = (
        jnp.einsum("hqk,khc->qhc", score_grad, key_rot, preferred_element_type=jnp.float32) * scale
    )
    key_rot_grad = (
        jnp.einsum("hqk,qhc->khc", score_grad, query_rot, preferred_element_type=jnp.float32)
        * scale
    )

    def turn(values):
        return rotate(values, positions)

    dummy_turn, turn_vjp = jax.vjp(turn, query_pre)
    query_grad = turn_vjp(query_rot_grad)[0].reshape(rows_dev, heads_dev * HD).astype(jnp.bfloat16)
    key_grad = turn_vjp(key_rot_grad)[0].reshape(rows_dev, heads_dev * HD).astype(jnp.bfloat16)
    value_flat = value_grad.reshape(rows_dev, heads_dev * HD)
    query_w_grad = contract_first(act_one, query_grad)
    key_w_grad = contract_first(act_one, key_grad)
    value_w_grad = contract_first(act_one, value_flat)
    act_one_grad = (
        contract_last(query_grad, query_whole)
        + contract_last(key_grad, key_whole)
        + contract_last(value_flat, value_whole)
    )
    act_one_total = lax.psum(act_one_grad, "tensor")
    dummy_first, first_vjp = jax.vjp(rms_norm, x_in, gain_one)
    in_norm_grad, gain_one_grad = first_vjp(act_one_total)
    tokens_grad = (mid_grad + in_norm_grad).astype(jnp.bfloat16)
    every = (
        lax.psum_scatter(gain_one_grad, "dp", scatter_dimension=0, tiled=True),
        lax.psum_scatter(query_w_grad, "dp", scatter_dimension=0, tiled=True),
        lax.psum_scatter(key_w_grad, "dp", scatter_dimension=0, tiled=True),
        lax.psum_scatter(value_w_grad, "dp", scatter_dimension=0, tiled=True),
        lax.psum_scatter(output_w_grad, "dp", scatter_dimension=0, tiled=True),
        lax.psum_scatter(ffn_sums[0], "dp", scatter_dimension=0, tiled=True),
        lax.psum_scatter(ffn_sums[1], "dp", scatter_dimension=0, tiled=True),
        lax.psum_scatter(ffn_sums[2], "dp", scatter_dimension=0, tiled=True),
        lax.psum_scatter(ffn_sums[3], "dp", scatter_dimension=0, tiled=True),
    )
    attn_sums = every[:5]
    ffn_sums = every[5:]
    return (
        layer_out,
        tokens_grad,
        attn_sums[0],
        attn_sums[1],
        attn_sums[2],
        attn_sums[3],
        attn_sums[4],
        ffn_sums[0],
        ffn_sums[1],
        ffn_sums[2],
        ffn_sums[3],
        expert_gate_grad,
        expert_up_grad,
        expert_down_grad,
    )


def place():
    d = lax.axis_index("dp"); y = lax.axis_index("tensor")
    c = lax.rem(d, 2); x = lax.rem(lax.div(d, 2), 2); z = lax.div(d, 4)
    return z, x, y, c

def dev(z, x, y, c):
    return ((z * 2 + x) * 2 + c, y)

def blk(z, x, y, c):
    return ((z * 2 + x) * 2 + c) * 2 + y

def greet(z, x, y, c):
    bar = pltpu.get_barrier_semaphore()
    for other in (dev(z, 1 - x, y, c), dev(z, x, 1 - y, c), dev(z, x, y, 1 - c)):
        pl.semaphore_signal(bar, inc=1, device_id=other, device_id_type=MESH)
    @pl.when(z > 0)
    def _():
        pl.semaphore_signal(bar, inc=1, device_id=dev(z - 1, x, y, c), device_id_type=MESH)
    @pl.when(z < 3)
    def _():
        pl.semaphore_signal(bar, inc=1, device_id=dev(z + 1, x, y, c), device_id_type=MESH)
    pl.semaphore_wait(bar, 3 + (z > 0).astype(jnp.int32) + (z < 3).astype(jnp.int32))

def rcopy(src, dst, ssem, rsem, device):
    return pltpu.make_async_remote_copy(src_ref=src, dst_ref=dst, send_sem=ssem, recv_sem=rsem, device_id=device, device_id_type=MESH)

def gather_kernel(x_ref, o_ref, zs, zr, x0s, x0r, x1s, x1r, y0s, y0r, y1s, y1r, cs, cr, lsem):
    z, x, y, c = place()
    rows = x_ref.shape[0]; h = rows // 2
    lo, hi = pl.ds(0, h), pl.ds(h, h)
    part = (lo, hi)
    xn, yn, cn = dev(z, 1 - x, y, c), dev(z, x, 1 - y, c), dev(z, x, y, 1 - c)
    greet(z, x, y, c)
    mine = blk(z, x, y, c)
    own = pltpu.make_async_copy(x_ref, o_ref.at[mine], lsem)
    own.start()

    def zcopy(s, up):
        src = o_ref.at[blk(s, x, y, c)]
        return rcopy(src, o_ref.at[blk(s, x, y, c)], zs.at[s, up], zr.at[s], dev(z + (1 if up else -1), x, y, c))
    def x0(s):
        b = blk(s, x, y, c)
        return rcopy(o_ref.at[b, lo], o_ref.at[b, lo], x0s.at[s], x0r.at[s], xn)
    def y1(s):
        b = blk(s, x, y, c)
        return rcopy(o_ref.at[b, hi], o_ref.at[b, hi], y1s.at[s], y1r.at[s], yn)
    def y0(s, xx):
        b = blk(s, xx, y, c)
        return rcopy(o_ref.at[b, lo], o_ref.at[b, lo], y0s.at[s, xx], y0r.at[s, xx], yn)
    def x1(s, yy):
        b = blk(s, x, yy, c)
        return rcopy(o_ref.at[b, hi], o_ref.at[b, hi], x1s.at[s, yy], x1r.at[s, yy], xn)
    def cc(s, xx, yy, p):
        b = blk(s, xx, yy, c)
        i = (s * 2 + xx) * 2 + yy
        return rcopy(o_ref.at[b, part[p]], o_ref.at[b, part[p]], cs.at[i, p], cr.at[i, p], cn)
    def column(s):
        x0(s).start(); y1(s).start(); y0(s, x).start(); x1(s, y).start()
        cc(s, x, y, 0).start(); cc(s, x, y, 1).start()
    def middle(s):
        x0(s).wait_recv()
        y0(s, 1 - x).start(); cc(s, 1 - x, y, 0).start()
        y1(s).wait_recv()
        x1(s, 1 - y).start(); cc(s, x, 1 - y, 1).start()
    def last(s):
        for q in (0, 1):
            y0(s, q).wait_recv(); cc(s, q, 1 - y, 0).start()
            x1(s, q).wait_recv(); cc(s, 1 - x, q, 1).start()

    own.wait()
    @pl.when(z < 3)
    def _(): zcopy(z, 1).start()
    @pl.when(z > 0)
    def _(): zcopy(z, 0).start()
    column(z)
    def each(k, fn):
        if k == 0:
            fn(z)
            return
        for sign in (-1, 1):
            s = z + sign * k
            @pl.when((s >= 0) & (s <= 3))
            def _(s=s): fn(s)
    for k in range(1, 4):
        for sign in (-1, 1):
            s = z + sign * k
            @pl.when((s >= 0) & (s <= 3))
            def _(s=s, sign=sign):
                up = 1 if sign < 0 else 0
                zcopy(s, up).wait_recv()
                @pl.when((z + (1 if up else -1) >= 0) & (z + (1 if up else -1) <= 3))
                def _(): zcopy(s, up).start()
                column(s)
        each(k - 1, middle)
        if k >= 2: each(k - 2, last)
    each(3, middle); each(2, last); each(3, last)
    for s in range(4):
        for xx in (0, 1):
            for yy in (0, 1):
                for p in (0, 1):
                    cc(s, xx, yy, p).wait_recv()
    for s in range(4):
        x0(s).wait_send(); y1(s).wait_send()
        for q in (0, 1):
            y0(s, q).wait_send(); x1(s, q).wait_send()
            for r in (0, 1):
                for p in (0, 1): cc(s, q, r, p).wait_send()
        @pl.when((z < 3) & (s <= z))
        def _(): zcopy(s, 1).wait_send()
        @pl.when((z > 0) & (s >= z))
        def _(): zcopy(s, 0).wait_send()

def gather_rows(x, cid, name):
    rows, width = x.shape
    D = pltpu.SemaphoreType.DMA
    out = pl.pallas_call(gather_kernel, out_shape=jax.ShapeDtypeStruct((32, rows, width), x.dtype),
        in_specs=[pl.BlockSpec(memory_space=pl.ANY)], out_specs=pl.BlockSpec(memory_space=pl.ANY),
        scratch_shapes=[D((4, 2)), D((4,)), D((4,)), D((4,)), D((4, 2)), D((4, 2)), D((4, 2)), D((4, 2)), D((4,)), D((4,)), D((16, 2)), D((16, 2)), D],
        compiler_params=pltpu.CompilerParams(collective_id=cid, has_side_effects=True), name=name)(x)
    return out.reshape(32 * rows, width)

def scatter_kernel(p_ref, o_ref, acc, ic, iy0, ix0, ix1, iy1, izu, izd, ls, cs, cr, y0s, y0r, x0s, x0r, x1s, x1r, y1s, y1r, zus, zur, zds, zdr):
    z, x, y, c = place()
    rows = p_ref.shape[1]; h = rows // 2
    lo, hi = pl.ds(0, h), pl.ds(h, h)
    xn, yn, cn = dev(z, 1 - x, y, c), dev(z, x, 1 - y, c), dev(z, x, y, 1 - c)
    greet(z, x, y, c)
    def at(s, xx, yy): return (s * 2 + xx) * 2 + yy
    def load(s, xx, yy):
        return pltpu.make_async_copy(p_ref.at[blk(s, xx, yy, c)], acc.at[at(s, xx, yy)], ls.at[at(s, xx, yy)])
    def cc(s, xx, yy):
        i = at(s, xx, yy)
        return rcopy(p_ref.at[blk(s, xx, yy, 1 - c)], ic.at[i], cs.at[i], cr.at[i], cn)
    def y0(s, xx):
        return rcopy(acc.at[at(s, xx, 1 - y), lo], iy0.at[s * 2 + xx], y0s.at[s, xx], y0r.at[s, xx], yn)
    def x1(s, yy):
        return rcopy(acc.at[at(s, 1 - x, yy), hi], ix1.at[s * 2 + yy], x1s.at[s, yy], x1r.at[s, yy], xn)
    def x0(s):
        return rcopy(acc.at[at(s, 1 - x, y), lo], ix0.at[s], x0s.at[s], x0r.at[s], xn)
    def y1(s):
        return rcopy(acc.at[at(s, x, 1 - y), hi], iy1.at[s], y1s.at[s], y1r.at[s], yn)
    def zu(s):
        return rcopy(acc.at[at(s, x, y)], izu.at[s], zus.at[s], zur.at[s], dev(z + 1, x, y, c))
    def zd(s):
        return rcopy(acc.at[at(s, x, y)], izd.at[s], zds.at[s], zdr.at[s], dev(z - 1, x, y, c))
    def add(i, start, count, src, j):
        step = 16
        @pl.loop(0, count // step)
        def _(r):
            a = pl.ds(pl.multiple_of(start + r * step, step), step)
            b = pl.ds(pl.multiple_of(r * step, step), step)
            acc[i, a] = acc[i, a] + src[j, b]
    def order(fn, k):
        if k == 0:
            fn(z); return
        for sign in (-1, 1):
            s = z + sign * k
            @pl.when((s >= 0) & (s <= 3))
            def _(s=s): fn(s)
    def start(s):
        for xx in (0, 1):
            for yy in (0, 1):
                cc(s, xx, yy).start(); load(s, xx, yy).start()
    def first(s):
        for xx in (0, 1):
            for yy in (0, 1):
                load(s, xx, yy).wait(); cc(s, xx, yy).wait_recv()
                add(at(s, xx, yy), 0, rows, ic, at(s, xx, yy))
                @pl.when(yy != y)
                def _(): y0(s, xx).start()
                @pl.when(xx != x)
                def _(): x1(s, yy).start()
    def second(s):
        y0(s, 1 - x).wait_recv(); add(at(s, 1 - x, y), 0, h, iy0, s * 2 + 1 - x); x0(s).start()
        x1(s, 1 - y).wait_recv(); add(at(s, x, 1 - y), h, h, ix1, s * 2 + 1 - y); y1(s).start()
        y0(s, x).wait_recv(); add(at(s, x, y), 0, h, iy0, s * 2 + x)
        x1(s, y).wait_recv(); add(at(s, x, y), h, h, ix1, s * 2 + y)
    def third(s):
        me = at(s, x, y)
        x0(s).wait_recv(); add(me, 0, h, ix0, s)
        y1(s).wait_recv(); add(me, h, h, iy1, s)
        @pl.when((s >= z) & (z > 0))
        def _():
            zu(s).wait_recv(); add(me, 0, rows, izu, s)
        @pl.when((s <= z) & (z < 3))
        def _():
            zd(s).wait_recv(); add(me, 0, rows, izd, s)
        @pl.when(s > z)
        def _(): zu(s).start()
        @pl.when(s < z)
        def _(): zd(s).start()
    for k in (3, 2, 1, 0): order(start, k)
    for k in (3, 2, 1, 0):
        order(first, k)
        if k + 1 <= 3: order(second, k + 1)
        if k + 2 <= 3: order(third, k + 2)
    order(second, 0); order(third, 1); order(third, 0)
    o_ref[...] = acc[at(z, x, y)]
    for s in range(4):
        for q in (0, 1):
            for r in (0, 1): cc(s, q, r).wait_send()
            y0(s, q).wait_send(); x1(s, q).wait_send()
        x0(s).wait_send(); y1(s).wait_send()
        @pl.when(s > z)
        def _(): zu(s).wait_send()
        @pl.when(s < z)
        def _(): zd(s).wait_send()

def scatter_rows(p, cid, name):
    total, width = p.shape
    rows = total // 32; h = rows // 2
    D = pltpu.SemaphoreType.DMA
    V = lambda n, r: pltpu.VMEM((n, r, width), p.dtype)
    return pl.pallas_call(scatter_kernel, out_shape=jax.ShapeDtypeStruct((rows, width), p.dtype),
        in_specs=[pl.BlockSpec(memory_space=pl.ANY)], out_specs=pl.BlockSpec(memory_space=pltpu.VMEM),
        scratch_shapes=[V(16, rows), V(16, rows), V(8, h), V(4, h), V(8, h), V(4, h), V(4, rows), V(4, rows),
            D((16,)), D((16,)), D((16,)), D((4, 2)), D((4, 2)), D((4,)), D((4,)), D((4, 2)), D((4, 2)), D((4,)), D((4,)), D((4,)), D((4,)), D((4,)), D((4,))],
        compiler_params=pltpu.CompilerParams(collective_id=cid, has_side_effects=True, vmem_limit_bytes=56 << 20), name=name)(p.reshape(32, rows, width))


def start_kernel(n, *refs):
    ins, g_in = refs[:n], refs[n]
    outs, g_out = refs[n + 1:2 * n + 1], refs[2 * n + 1]
    zs, zr, xs, xr, cs, cr, ls = refs[2 * n + 2:2 * n + 9]
    gzs, gzr, gxs, gxr, gys, gyr, gcs, gcr, gl = refs[2 * n + 9:]
    z, x, y, c = place()
    xn, yn, cn = dev(z, 1 - x, y, c), dev(z, x, 1 - y, c), dev(z, x, y, 1 - c)
    greet(z, x, y, c)
    def pos(s, xx, cc_): return (s * 2 + xx) * 2 + cc_
    me = pos(z, x, c)
    owns = [pltpu.make_async_copy(ins[a], outs[a].at[me], ls.at[a]) for a in range(n)]
    owns.append(pltpu.make_async_copy(g_in, g_out.at[blk(z, x, y, c)], gl))
    for o in owns: o.start()
    def wz(a, s, up):
        r = outs[a].at[pos(s, x, c)]
        return rcopy(r, r, zs.at[a, s, up], zr.at[a, s], dev(z + (1 if up else -1), x, y, c))
    def wx(a, s):
        r = outs[a].at[pos(s, x, c)]
        return rcopy(r, r, xs.at[a, s], xr.at[a, s], xn)
    def wc(a, s, xx):
        r = outs[a].at[pos(s, xx, c)]
        return rcopy(r, r, cs.at[a, s * 2 + xx], cr.at[a, s * 2 + xx], cn)
    def gz(s, up):
        r = g_out.at[blk(s, x, y, c)]
        return rcopy(r, r, gzs.at[s, up], gzr.at[s], dev(z + (1 if up else -1), x, y, c))
    def gx(s):
        r = g_out.at[blk(s, x, y, c)]
        return rcopy(r, r, gxs.at[s], gxr.at[s], xn)
    def gy(s, xx):
        r = g_out.at[blk(s, xx, y, c)]
        return rcopy(r, r, gys.at[s, xx], gyr.at[s, xx], yn)
    def gc(s, xx, yy):
        r = g_out.at[blk(s, xx, yy, c)]
        return rcopy(r, r, gcs.at[s * 2 + xx, yy], gcr.at[s * 2 + xx, yy], cn)
    for o in owns: o.wait()
    def inside(v): return (v >= 0) & (v <= 3)
    def each(k, fn):
        if k == 0:
            fn(z); return
        for sign in (-1, 1):
            s = z + sign * k
            @pl.when(inside(s))
            def _(s=s): fn(s)
    def column(s):
        for a in range(n):
            wx(a, s).start(); wc(a, s, x).start()
    def gcolumn(s):
        gx(s).start(); gy(s, x).start(); gc(s, x, y).start()
    def middle(s):
        for a in range(n):
            wx(a, s).wait_recv(); wc(a, s, 1 - x).start()
    def gmiddle(s):
        gx(s).wait_recv(); gy(s, 1 - x).start(); gc(s, 1 - x, y).start()
    def glast(s):
        for q in (0, 1):
            gy(s, q).wait_recv(); gc(s, q, 1 - y).start()
    def launch(fn):
        @pl.when(z < 3)
        def _(): fn(1)
        @pl.when(z > 0)
        def _(): fn(0)
    launch(lambda up: [wz(a, z, up).start() for a in range(n)])
    column(z)
    launch(lambda up: gz(z, up).start())
    gcolumn(z)
    def arrive(k, recv, go, then):
        for sign in (-1, 1):
            s = z + sign * k
            @pl.when(inside(s))
            def _(s=s, sign=sign):
                up = 1 if sign < 0 else 0
                nxt = inside(z - sign)
                recv(s, up)
                @pl.when(nxt)
                def _(): go(s, up)
                then(s)
    for k in range(1, 4):
        arrive(k, lambda s, up: [wz(a, s, up).wait_recv() for a in range(n)], lambda s, up: [wz(a, s, up).start() for a in range(n)], column)
        each(k - 1, middle)
        arrive(k, lambda s, up: gz(s, up).wait_recv(), lambda s, up: gz(s, up).start(), gcolumn)
        each(k - 1, gmiddle)
    each(3, middle); each(3, gmiddle)
    for k in range(4): each(k, glast)
    for s in range(4):
        for q in (0, 1):
            for a in range(n): wc(a, s, q).wait_recv()
            for r in (0, 1): gc(s, q, r).wait_recv()
    for s in range(4):
        for a in range(n):
            wx(a, s).wait_send()
            for q in (0, 1): wc(a, s, q).wait_send()
        gx(s).wait_send()
        for q in (0, 1):
            gy(s, q).wait_send()
            for r in (0, 1): gc(s, q, r).wait_send()
        @pl.when((z < 3) & (s <= z))
        def _():
            gz(s, 1).wait_send()
            for a in range(n): wz(a, s, 1).wait_send()
        @pl.when((z > 0) & (s >= z))
        def _():
            gz(s, 0).wait_send()
            for a in range(n): wz(a, s, 0).wait_send()

def start_gather(arrays, rows, cid, name):
    n = len(arrays)
    D = pltpu.SemaphoreType.DMA
    any_ = pl.BlockSpec(memory_space=pl.ANY)
    outs = pl.pallas_call(functools.partial(start_kernel, n),
        out_shape=[jax.ShapeDtypeStruct((16,) + a.shape, a.dtype) for a in arrays] + [jax.ShapeDtypeStruct((32,) + rows.shape, rows.dtype)],
        in_specs=[any_] * (n + 1), out_specs=[any_] * (n + 1),
        scratch_shapes=[D((n, 4, 2)), D((n, 4)), D((n, 4)), D((n, 4)), D((n, 8)), D((n, 8)), D((n,)),
            D((4, 2)), D((4,)), D((4,)), D((4,)), D((4, 2)), D((4, 2)), D((8, 2)), D((8, 2)), D],
        compiler_params=pltpu.CompilerParams(collective_id=cid, has_side_effects=True), name=name)(*arrays, rows)
    return outs

def wsum_kernel(n, *refs):
    ins, outs = refs[:n], refs[n:2 * n]
    acc, ic, ix, izu, izd, ls, cs, cr, xs, xr, zus, zur, zds, zdr = refs[2 * n:]
    z, x, y, c = place()
    depth = ins[0].shape[1]
    xn, cn = dev(z, 1 - x, y, c), dev(z, x, y, 1 - c)
    greet_plane(z, x, y, c)
    def at(s, xx): return s * 2 + xx
    def pos(s, xx, cc_): return (s * 2 + xx) * 2 + cc_
    def load(a, s, xx):
        i = at(s, xx)
        return pltpu.make_async_copy(ins[a].at[pos(s, xx, c)], acc.at[a, i], ls.at[a, i])
    def wc(a, s, xx):
        i = at(s, xx)
        return rcopy(ins[a].at[pos(s, xx, 1 - c)], ic.at[a, i], cs.at[a, i], cr.at[a, i], cn)
    def wx(a, s):
        return rcopy(acc.at[a, at(s, 1 - x)], ix.at[a, s], xs.at[a, s], xr.at[a, s], xn)
    def zu(a, s):
        return rcopy(acc.at[a, at(s, x)], izu.at[a, s], zus.at[a, s], zur.at[a, s], dev(z + 1, x, y, c))
    def zd(a, s):
        return rcopy(acc.at[a, at(s, x)], izd.at[a, s], zds.at[a, s], zdr.at[a, s], dev(z - 1, x, y, c))
    def add(a, i, src, j):
        step = 16
        @pl.loop(0, depth // step)
        def _(r):
            b = pl.ds(pl.multiple_of(r * step, step), step)
            acc[a, i, b] = acc[a, i, b] + src[a, j, b]
    def order(fn, k):
        if k == 0:
            fn(z); return
        for sign in (-1, 1):
            s = z + sign * k
            @pl.when((s >= 0) & (s <= 3))
            def _(s=s): fn(s)
    def start(s):
        for a in range(n):
            for q in (0, 1):
                wc(a, s, q).start(); load(a, s, q).start()
    def first(s):
        for a in range(n):
            for q in (0, 1):
                load(a, s, q).wait(); wc(a, s, q).wait_recv()
                add(a, at(s, q), ic, at(s, q))
            wx(a, s).start()
    def second(s):
        for a in range(n):
            wx(a, s).wait_recv(); add(a, at(s, x), ix, s)
            @pl.when((s >= z) & (z > 0))
            def _():
                zu(a, s).wait_recv(); add(a, at(s, x), izu, s)
            @pl.when((s <= z) & (z < 3))
            def _():
                zd(a, s).wait_recv(); add(a, at(s, x), izd, s)
            @pl.when(s > z)
            def _(): zu(a, s).start()
            @pl.when(s < z)
            def _(): zd(a, s).start()
    for k in (3, 2, 1, 0): order(start, k)
    for k in (3, 2, 1, 0):
        order(first, k)
        if k + 1 <= 3: order(second, k + 1)
    order(second, 0)
    for a in range(n):
        outs[a][...] = acc[a, at(z, x)].astype(jnp.float32)
    for s in range(4):
        for a in range(n):
            for q in (0, 1): wc(a, s, q).wait_send()
            wx(a, s).wait_send()
            @pl.when(s > z)
            def _(): zu(a, s).wait_send()
            @pl.when(s < z)
            def _(): zd(a, s).wait_send()

def greet_plane(z, x, y, c):
    bar = pltpu.get_barrier_semaphore()
    for other in (dev(z, 1 - x, y, c), dev(z, x, y, 1 - c)):
        pl.semaphore_signal(bar, inc=1, device_id=other, device_id_type=MESH)
    @pl.when(z > 0)
    def _():
        pl.semaphore_signal(bar, inc=1, device_id=dev(z - 1, x, y, c), device_id_type=MESH)
    @pl.when(z < 3)
    def _():
        pl.semaphore_signal(bar, inc=1, device_id=dev(z + 1, x, y, c), device_id_type=MESH)
    pl.semaphore_wait(bar, 2 + (z > 0).astype(jnp.int32) + (z < 3).astype(jnp.int32))

def weight_sums(arrays, cid, name):
    n = len(arrays); total, width = arrays[0].shape; depth = total // 16
    D = pltpu.SemaphoreType.DMA
    V = lambda k: pltpu.VMEM((n, k, depth, width), arrays[0].dtype)
    return pl.pallas_call(functools.partial(wsum_kernel, n),
        out_shape=[jax.ShapeDtypeStruct((depth, width), jnp.float32)] * n,
        in_specs=[pl.BlockSpec(memory_space=pl.ANY)] * n, out_specs=[pl.BlockSpec(memory_space=pltpu.VMEM)] * n,
        scratch_shapes=[V(8), V(8), V(4), V(4), V(4), D((n, 8)), D((n, 8)), D((n, 8)), D((n, 4)), D((n, 4)), D((n, 4)), D((n, 4)), D((n, 4)), D((n, 4))],
        compiler_params=pltpu.CompilerParams(collective_id=cid, has_side_effects=True, vmem_limit_bytes=56 << 20), name=name)(*[a.reshape(16, depth, width) for a in arrays])


def routing_tables(gate_table, capacity):
    member = gate_table > 0.0
    ranks = jnp.cumsum(member.astype(jnp.int32), axis=1) - 1
    slot = jnp.arange(capacity, dtype=jnp.int32)
    pick = (ranks[:, None, :] == slot[None, :, None]) & member[:, None, :]
    slot_gate = jnp.sum(jnp.where(pick, gate_table[:, None, :], 0.0), axis=2)
    return pick.astype(jnp.bfloat16), slot_gate


def on_device(
    tokens,
    cotangent,
    route_ids,
    route_gates,
    gain_first,
    w_query,
    w_key,
    w_value,
    w_output,
    gain_second,
    shared_gate,
    shared_up,
    shared_down,
    expert_gate,
    expert_up,
    expert_down,
):
    f32, bf16 = jnp.float32, jnp.bfloat16
    rows_dev, width = tokens.shape
    topk = route_ids.shape[1]
    experts = lax.axis_size("dp")
    splits = lax.axis_size("tensor")
    half = rows_dev // splits
    mine = lax.axis_index("tensor") * half
    capacity = rows_dev * topk * 4 // (3 * experts)
    slots = experts * capacity
    scale = HD ** (-0.5)
    positions = jnp.arange(rows_dev, dtype=f32)
    causal = jnp.arange(rows_dev)[:, None] >= jnp.arange(rows_dev)[None, :]
    grad_half = lax.dynamic_slice_in_dim(cotangent, mine, half, axis=0)
    chosen = route_ids[:, :, None] == jnp.arange(experts, dtype=jnp.int32)[None, None, :]
    table = jnp.sum(jnp.where(chosen, route_gates[:, :, None], 0.0), axis=1)
    gains = jnp.concatenate([gain_first[None], gain_second[None], jnp.zeros((14, gain_first.shape[0]), bf16)])
    query_whole, key_whole, value_whole, output_whole, gains, tables, grad_all = start_gather(
        [w_query, w_key, w_value, w_output, gains, table.T], grad_half, 0, "gather_weights"
    )
    query_whole, key_whole, value_whole, output_whole = [
        w.reshape(width, -1) for w in (query_whole, key_whole, value_whole, output_whole)
    ]
    grad_all = grad_all.reshape(-1, width)
    gain_one = gains[:, 0].reshape(-1).astype(f32)
    gain_two = gains[:, 1].reshape(-1).astype(f32)

    depth, common_width = shared_gate.shape
    common_dev = common_width // experts
    packed = jnp.stack([shared_gate, shared_up, shared_down])
    packed = packed.reshape(3, depth, experts, common_dev).transpose(2, 0, 1, 3)
    packed = lax.all_to_all(packed, "dp", split_axis=0, concat_axis=0, tiled=True)
    packed = packed.transpose(1, 0, 2, 3).reshape(3, width, common_dev)
    common_gu = jnp.concatenate([packed[0], packed[1]], axis=1)
    common_down = packed[2]

    table = lax.dynamic_index_in_dim(tables, lax.axis_index("dp"), axis=1, keepdims=False)
    pick, slot_gate = routing_tables(table, capacity)

    x_in = tokens.astype(f32)
    act_one = rms_norm(x_in, gain_one).astype(bf16)
    heads_dev = query_whole.shape[1] // HD
    query_pre = jnp.dot(act_one, query_whole, preferred_element_type=f32).reshape(
        rows_dev, heads_dev, HD
    )
    key_pre = jnp.dot(act_one, key_whole, preferred_element_type=f32).reshape(
        rows_dev, heads_dev, HD
    )
    query_rot = rotate(query_pre, positions).astype(bf16)
    key_rot = rotate(key_pre, positions).astype(bf16)
    value_low = (
        jnp.dot(act_one, value_whole, preferred_element_type=f32)
        .astype(bf16)
        .reshape(rows_dev, heads_dev, HD)
    )
    scores = masked_scores(query_rot, key_rot, causal, scale)
    top = jnp.max(scores, axis=-1, keepdims=True)
    expo = jnp.exp(scores - top)
    total = jnp.sum(expo, axis=-1, keepdims=True)
    probs = expo / total
    log_total = top + jnp.log(total)
    mixed = jnp.einsum("hqk,khc->qhc", probs.astype(bf16), value_low, preferred_element_type=f32)
    mixed = mixed.reshape(rows_dev, heads_dev * HD).astype(bf16)
    attn = lax.psum_scatter(
        contract_last(mixed, output_whole), "tensor", scatter_dimension=0, tiled=True
    )
    x_half = lax.dynamic_slice_in_dim(tokens, mine, half, axis=0).astype(f32)
    x_mid = x_half + attn
    act_two = rms_norm(x_mid, gain_two).astype(bf16)

    act_all = gather_rows(act_two, 1, "gather_act")
    act_blocks = act_all.reshape(experts, rows_dev, width)
    grad_blocks = grad_all.reshape(experts, rows_dev, width)
    exp_gate, exp_up, exp_down = expert_gate[0], expert_up[0], expert_down[0]

    def select(blocks):
        return jnp.einsum("jst,jtd->jsd", pick, blocks, preferred_element_type=f32)

    def spread(rows):
        return jnp.einsum(
            "jst,jsd->jtd", pick, rows.reshape(experts, capacity, width), preferred_element_type=f32
        ).reshape(experts * rows_dev, width)

    weight = slot_gate.reshape(slots, 1)
    rows = select(act_blocks).astype(bf16).reshape(slots, width)
    rows_out_grad = (weight * select(grad_blocks).reshape(slots, width)).astype(bf16)
    gate_rows = jnp.dot(rows, exp_gate, preferred_element_type=f32)
    up_rows = jnp.dot(rows, exp_up, preferred_element_type=f32)
    hidden_rows, expert_vjp = jax.vjp(gated, gate_rows, up_rows)
    hidden_rows = hidden_rows.astype(bf16)
    hidden_rows_grad = contract_last(rows_out_grad, exp_down)
    gate_rows_grad, up_rows_grad = expert_vjp(hidden_rows_grad)
    gate_rows_grad = gate_rows_grad.astype(bf16)
    up_rows_grad = up_rows_grad.astype(bf16)
    rows_in_grad = contract_last(gate_rows_grad, exp_gate) + contract_last(up_rows_grad, exp_up)

    common_pre = jnp.dot(act_all, common_gu, preferred_element_type=f32)
    common_hidden, common_vjp = jax.vjp(
        gated, common_pre[:, :common_dev], common_pre[:, common_dev:]
    )
    common_hidden = common_hidden.astype(bf16)
    common_hidden_grad = jnp.dot(grad_all, common_down, preferred_element_type=f32)
    common_gu_grad = jnp.concatenate(common_vjp(common_hidden_grad), axis=1).astype(bf16)
    act_grad = spread(rows_in_grad.astype(bf16)) + contract_last(common_gu_grad, common_gu)
    act_two_total = scatter_rows(act_grad.astype(bf16), 2, "sum_act_grad").astype(f32)

    rows_out = jnp.dot(hidden_rows, exp_down, preferred_element_type=f32) * weight
    ffn = spread(rows_out.astype(bf16)) + contract_last(common_hidden, common_down)
    ffn = scatter_rows(ffn.astype(bf16), 3, "sum_ffn").astype(f32)
    layer_out = lax.all_gather((x_mid + ffn).astype(bf16), "tensor", axis=0, tiled=True)

    expert_gate_grad = contract_first(rows, gate_rows_grad)[None]
    expert_up_grad = contract_first(rows, up_rows_grad)[None]
    expert_down_grad = contract_first(hidden_rows, rows_out_grad)[None]
    common_w_grad = jnp.concatenate(
        [contract_first(act_all, common_gu_grad), contract_first(grad_all, common_hidden)], axis=1
    )
    common_w_grad = common_w_grad.astype(bf16).reshape(experts, depth, 3 * common_dev)
    common_w_grad = lax.all_to_all(common_w_grad, "dp", split_axis=0, concat_axis=0, tiled=True)
    common_w_grad = common_w_grad.astype(f32).reshape(experts, depth, 3, common_dev)
    common_w_grad = common_w_grad.transpose(2, 1, 0, 3).reshape(3, depth, common_width)

    dummy_second, second_vjp = jax.vjp(rms_norm, x_mid, gain_two)
    mid_norm_grad, gain_two_grad = second_vjp(act_two_total)
    mid_grad = grad_half.astype(f32) + mid_norm_grad
    attn_grad = lax.all_gather(mid_grad.astype(bf16), "tensor", axis=0, tiled=True)

    mixed_grad = (
        jnp.dot(attn_grad, output_whole, preferred_element_type=f32)
        .astype(bf16)
        .reshape(rows_dev, heads_dev, HD)
    )
    probs_again = jnp.exp(masked_scores(query_rot, key_rot, causal, scale) - log_total)
    value_grad = jnp.einsum(
        "hqk,qhc->khc", probs_again.astype(bf16), mixed_grad, preferred_element_type=f32
    ).astype(bf16)
    prob_grad = jnp.einsum("qhc,khc->hqk", mixed_grad, value_low, preferred_element_type=f32)
    delta = jnp.sum(probs_again * prob_grad, axis=-1, keepdims=True)
    score_grad = (probs_again * (prob_grad - delta)).astype(bf16)
    query_rot_grad = (
        jnp.einsum("hqk,khc->qhc", score_grad, key_rot, preferred_element_type=f32) * scale
    )
    key_rot_grad = (
        jnp.einsum("hqk,qhc->khc", score_grad, query_rot, preferred_element_type=f32) * scale
    )
    query_grad = rotate(query_rot_grad, -positions).reshape(rows_dev, heads_dev * HD).astype(bf16)
    key_grad = rotate(key_rot_grad, -positions).reshape(rows_dev, heads_dev * HD).astype(bf16)
    value_flat = value_grad.reshape(rows_dev, heads_dev * HD)
    act_one_grad = (
        contract_last(query_grad, query_whole)
        + contract_last(key_grad, key_whole)
        + contract_last(value_flat, value_whole)
    )
    act_one_total = lax.psum_scatter(act_one_grad, "tensor", scatter_dimension=0, tiled=True)
    dummy_first, first_vjp = jax.vjp(rms_norm, x_half, gain_one)
    in_norm_grad, gain_one_grad = first_vjp(act_one_total)
    tokens_grad = lax.all_gather((mid_grad + in_norm_grad).astype(bf16), "tensor", axis=0, tiled=True)

    query_sum, key_sum, value_sum, output_sum = weight_sums(
        [
            contract_first(act_one, query_grad).astype(bf16),
            contract_first(act_one, key_grad).astype(bf16),
            contract_first(act_one, value_flat).astype(bf16),
            contract_first(attn_grad, mixed).astype(bf16),
        ],
        4,
        "sum_weight_grads",
    )
    gain_grads = lax.psum(jnp.stack([gain_one_grad, gain_two_grad]), ("dp", "tensor"))
    gain_grads = lax.dynamic_slice_in_dim(
        gain_grads, lax.axis_index("dp") * gain_first.shape[0], gain_first.shape[0], axis=1
    )
    return (
        layer_out,
        tokens_grad,
        gain_grads[0],
        query_sum,
        key_sum,
        value_sum,
        output_sum,
        gain_grads[1],
        common_w_grad[0],
        common_w_grad[1],
        common_w_grad[2],
        expert_gate_grad,
        expert_up_grad,
        expert_down_grad,
    )


def solution(mesh):
    body = on_device if (mesh.shape["dp"], mesh.shape["tensor"]) == (16, 2) else on_device_plain
    in_specs = (
        P("dp", None),
        P("dp", None),
        P("dp", None),
        P("dp", None),
        P("dp"),
        P("dp", "tensor"),
        P("dp", "tensor"),
        P("dp", "tensor"),
        P("dp", "tensor"),
        P("dp"),
        P("dp", "tensor"),
        P("dp", "tensor"),
        P("dp", "tensor"),
        P("dp", None, "tensor"),
        P("dp", None, "tensor"),
        P("dp", "tensor", None),
    )
    out_specs = (
        P("dp", None),
        P("dp", None),
        P("dp"),
        P("dp", "tensor"),
        P("dp", "tensor"),
        P("dp", "tensor"),
        P("dp", "tensor"),
        P("dp"),
        P("dp", "tensor"),
        P("dp", "tensor"),
        P("dp", "tensor"),
        P("dp", None, "tensor"),
        P("dp", None, "tensor"),
        P("dp", "tensor", None),
    )
    return jax.shard_map(
        body, mesh=mesh, in_specs=in_specs, out_specs=out_specs, check_vma=False
    )
```

profile of v0, /device:TPU:0, one launch (start us, length us, event | category | flops | bytes accessed | tf_op | source)
XLA Modules:
  0.0 1192.6 jit_solution(13847666611018654236)
XLA Ops:
  12.2 227.7 %gather_weights.1 = (bf16[16,128,1024]{2,1,0:T(8,128)(2,1)}, bf16[16,128,1024]{2,1,0:T(8,128)(2,1)}, bf16[16,128,1024]{2,1,0:T(8,128)(2,1)}, bf16[16,128,1024]{2...) custom-call(bf16[128,1024]{1,0:T(8,128)(2,1)} %refs_0_.1, ...), custom_call_target="tpu_custom_call" | custom-call | tf_op jit(solution)/shard_map/gather_weights/pallas_call | solution.py:617
  240.8 6.6 copy.103
  249.1 6.4 copy.102
  282.2 6.3 all-to-all-start
  290.1 26.0 %copy.124 = bf16[2048,5120]{1,0:T(8,128)(2,1)} copy(bf16[2048,5120]{0,1:T(8,128)(2,1)} %bitcast.235) | data formatting | bytes 41943040 | tf_op jit(solution)/shard_map/dot_general | solution.py:47
  318.4 17.1 %multiply_convert_fusion = (bf16[16,160,2048]{2,1,0:T(8,128)(2,1)}, f32[16,160,2048]{2,1,0:T(8,128)}) fusion(f32[16,160]{1,0:T(8,128)S(1)} %select_reduce_fusion, bf16[16,320,2048]{2,1,0:T(8,128)(2,1)} %bitcast.236, s32[16,320]{1,0:T(8,128)S(1)} %slice_add_fusion, pred[16,320]{1,0:T(8,128)(4,1)S(1)} %bitcast.273), kind=kOutput, calls=%fused_computation.7 | convolution fusion | flops 3367567360 | bytes 52464640 | tf_op jit(solution)/shard_map/jst,jtd->jsd/dot_general | solution.py:823
  335.5 12.5 %fusion.2 = bf16[2560,2048]{1,0:T(8,128)(2,1)} fusion(f32[16,160,2048]{2,1,0:T(8,128)} %get-tuple-element.124, f32[2560]{0:T(1024)S(1)} %mul.519), kind=kLoop, calls=%fused_computation.5 | loop fusion | flops 10485760 | bytes 31467520 | tf_op jit(solution)/shard_map/convert_element_type | solution.py:832
  355.8 114.5 %gather_act.1 = bf16[32,160,2048]{2,1,0:T(8,128)(2,1)} custom-call(bf16[160,2048]{1,0:T(8,128)(2,1)} %multiply_convert_fusion.7.x_ref), custom_call_target="tpu_custom_call" | custom-call | tf_op jit(solution)/shard_map/gather_act/pallas_call | solution.py:404
  470.3 26.4 %copy.123 = bf16[2048,5120]{1,0:T(8,128)(2,1)} copy(bf16[2048,5120]{0,1:T(8,128)(2,1)} %bitcast.231) | data formatting | bytes 41943040 | tf_op jit(solution)/shard_map/dot_general | solution.py:47
  496.7 11.4 fusion.132
  508.1 15.3 %fusion.44 = (bf16[5120,88]{0,1:T(8,128)(2,1)}, bf16[5120,88]{0,1:T(8,128)(2,1)}, bf16[5120,88]{0,1:T(8,128)(2,1)S(1)}) fusion(f32[5120,176]{0,1:T(8,128)S(1)} %fusion.132, bf16[5120,2048]{1,0:T(8,128)(2,1)} %bitcast.237, bf16[11,8,16,128]{3,2,1,0:T(8,128)(2,1)S(1)} %bitcast.265), kind=kOutput, calls=%fused_computation.78 | convolution fusion | flops 1852702720 | bytes 27639808 | tf_op jit(solution)/shard_map/dot_general | solution.py:848
  523.4 11.1 convolution_convert_fusion.7
  534.7 8.5 fusion.52
  549.6 12.3 %convolution_convert_fusion = bf16[16,160,2048]{2,1,0:T(8,128)(2,1)} fusion(bf16[16,320,2048]{2,1,0:T(8,128)(2,1)} %bitcast.233, s32[16,320]{1,0:T(8,128)S(1)} %slice_add_fusion, pred[16,320]{1,0:T(8,128)(4,1)S(1)} %bitcast.274), kind=kOutput, calls=%fused_computation.17 | convolution fusion | flops 3362324480 | bytes 31482880 | tf_op jit(solution)/shard_map/jst,jtd->jsd/dot_general | solution.py:823
  561.9 13.4 %fusion.21 = f32[2560,704]{0,1:T(8,128)} fusion(bf16[2560,2048]{1,0:T(8,128)(2,1)} %bitcast.246, bf16[1,2048,704]{1,2,0:T(8,128)(2,1)S(1)} %copy-done.61), kind=kOutput, calls=%fused_computation.45 | convolution fusion | flops 7381975040 | bytes 20578304 | tf_op jit(solution)/shard_map/dot_general | solution.py:834
  575.3 9.9 fusion.25
  585.2 19.3 %multiply_convert_fusion.2 = (bf16[2560,704]{0,1:T(8,128)(2,1)}, bf16[2560,704]{0,1:T(8,128)(2,1)}, bf16[2560,704]{0,1:T(8,128)(2,1)}) fusion(f32[2560,704]{0,1:T(8,128)} %fusion.25, f32[2560,704]{0,1:T(8,128)} %fusion.21, bf16[2560,2048]{1,0:T(8,128)(2,1)} %bitcast.243, bf16[1,704,2048]{2,1,0:T(8,128)(2,1)S(1)} %copy-done), kind=kOutput, calls=%fused_computation.13 | convolution fusion | flops 7410810880 | bytes 38600704 | tf_op jit(solution)/shard_map/dot_general | solution.py:41
  604.5 13.4 %fusion.23 = f32[2560,2048]{1,0:T(8,128)} fusion(bf16[2560,704]{0,1:T(8,128)(2,1)} %get-tuple-element.87, bf16[1,2048,704]{1,2,0:T(8,128)(2,1)S(1)} %copy-done.60), kind=kOutput, calls=%fused_computation.47 | convolution fusion | flops 7381975040 | bytes 27459584 | tf_op jit(solution)/shard_map/dot_general | solution.py:41
  618.0 16.0 %add_convert_fusion = bf16[2560,2048]{1,0:T(8,128)(2,1)} fusion(f32[2560,2048]{1,0:T(8,128)} %fusion.23, bf16[2560,704]{0,1:T(8,128)(2,1)} %get-tuple-element.86, bf16[1,2048,704]{1,2,0:T(8,128)(2,1)S(1)} %copy-done.61), kind=kOutput, calls=%fused_computation.6 | convolution fusion | flops 7392460800 | bytes 37945344 | tf_op jit(solution)/shard_map/dot_general | solution.py:41
  633.9 18.9 %fusion.8 = f32[16,320,2048]{2,1,0:T(8,128)} fusion(bf16[16,160,2048]{2,1,0:T(8,128)(2,1)} %bitcast.245, s32[16,320]{1,0:T(8,128)S(1)} %slice_add_fusion, pred[16,320]{1,0:T(8,128)(4,1)S(1)} %bitcast.275), kind=kOutput, calls=%fused_computation.27 | convolution fusion | flops 3357081600 | bytes 52454400 | tf_op jit(solution)/shard_map/jst,jsd->jtd/dot_general | solution.py:826
  652.8 22.6 %fusion = bf16[5120,2048]{1,0:T(8,128)(2,1)} fusion(f32[16,320,2048]{2,1,0:T(8,128)} %fusion.8, bf16[2048,176]{0,1:T(8,128)(2,1)} %bitcast_dynamic-update-slice_fusion, bf16[5120,88]{0,1:T(8,128)(2,1)} %get-tuple-element.90, bf16[5120,88]{0,1:T(8,128)(2,1)} %get-tuple-element.89), kind=kOutput, calls=%fused_computation.1 | convolution fusion | flops 3715563520 | bytes 65437696 | tf_op jit(solution)/shard_map/dot_general | solution.py:41
  675.4 100.5 %sum_act_grad.1 = bf16[160,2048]{1,0:T(8,128)(2,1)} custom-call(bf16[32,160,2048]{2,1,0:T(8,128)(2,1)} %bitcast.239), custom_call_target="tpu_custom_call" | custom-call | tf_op jit(solution)/shard_map/sum_act_grad/pallas_call | solution.py:502
  780.6 13.0 %multiply_convert_fusion.1 = bf16[2560,2048]{1,0:T(8,128)(2,1)} fusion(bf16[2560,704]{0,1:T(8,128)(2,1)} %get-tuple-element.88, f32[2560]{0:T(1024)S(1)} %copy-done.46, bf16[1,704,2048]{2,1,0:T(8,128)(2,1)S(1)} %copy-done), kind=kOutput, calls=%fused_computation.8 | convolution fusion | flops 7392460800 | bytes 16984064 | tf_op jit(solution)/shard_map/dot_general | solution.py:853
  793.6 19.1 %fusion.12 = f32[16,320,2048]{2,1,0:T(8,128)} fusion(bf16[16,160,2048]{2,1,0:T(8,128)(2,1)} %bitcast.244, s32[16,320]{1,0:T(8,128)S(1)} %slice_add_fusion, pred[16,320]{1,0:T(8,128)(4,1)S(1)} %bitcast.276), kind=kOutput, calls=%fused_computation.29 | convolution fusion | flops 3357081600 | bytes 52454400 | tf_op jit(solution)/shard_map/jst,jsd->jtd/dot_general | solution.py:826
  833.2 21.8 %fusion.1 = bf16[5120,2048]{1,0:T(8,128)(2,1)} fusion(f32[16,320,2048]{2,1,0:T(8,128)} %fusion.12, bf16[5120,88]{0,1:T(8,128)(2,1)} %copy-done.21, bf16[11,8,16,128]{3,2,1,0:T(8,128)(2,1)S(1)} %bitcast.266), kind=kOutput, calls=%fused_computation.3 | convolution fusion | flops 1866465280 | bytes 64176128 | tf_op jit(solution)/shard_map/dot_general | solution.py:41
  854.9 110.6 %sum_ffn.1 = bf16[160,2048]{1,0:T(8,128)(2,1)} custom-call(bf16[32,160,2048]{2,1,0:T(8,128)(2,1)} %bitcast.238), custom_call_target="tpu_custom_call" | custom-call | tf_op jit(solution)/shard_map/sum_ffn/pallas_call | solution.py:502
  966.1 13.1 %convolution_bitcast_fusion = f32[1,2048,704]{1,2,0:T(8,128)} fusion(bf16[2560,704]{0,1:T(8,128)(2,1)} %get-tuple-element.86, bf16[2560,2048]{1,0:T(8,128)(2,1)} %bitcast.247), kind=kOutput, calls=%fused_computation.34 | convolution fusion | flops 7381975040 | bytes 19857408 | tf_op jit(solution)/shard_map/dot_general | solution.py:47
  979.2 9.5 convolution_bitcast_fusion.1
  996.0 13.3 %convolution_bitcast_fusion.2 = f32[1,704,2048]{2,1,0:T(8,128)} fusion(bf16[2560,704]{0,1:T(8,128)(2,1)} %get-tuple-element.88, bf16[2560,2048]{1,0:T(8,128)(2,1)} %fusion.2), kind=kOutput, calls=%fused_computation.36 | convolution fusion | flops 7381975040 | bytes 19857408 | tf_op jit(solution)/shard_map/dot_general | solution.py:47
  1022.9 5.6 convolution_convert_fusion.1
  1028.5 100.1 %sum_weight_grads.1 = (f32[128,1024]{1,0:T(8,128)}, f32[128,1024]{1,0:T(8,128)}, f32[128,1024]{1,0:T(8,128)}, f32[128,1024]{1,0:T(8,128)}) custom-call(bf16[16,128,1024]{2,1,0:T(8,128)(2,1)} %bitcast.259, bf16[16,128,1024]{2,1,0:T(8,128)(2,1)} %bitcast.260, bf16[16,128,1024]{2,1,0:T(8,128)(2,1)} %bitcast.258, bf16[16,128,1024]{2,1,0:T(8,128)(2,1)} %bitcast.261), custom_call_target="tpu_custom_call" | custom-call | tf_op jit(solution)/shard_map/sum_weight_grads/pallas_call | solution.py:714
  1138.2 40.2 %psum.7 = f32[2,2048]{1,0:T(2,128)S(1)} all-reduce(f32[2,2048]{1,0:T(2,128)S(1)} %pad_maximum_fusion.10), channel_id=1, replica_groups=mesh['dp'=16,'tensor'=2] {'dp','tensor'}, use_global_device_ids=true, to_apply=%region_16.17 | all-reduce | flops 4096 | bytes 32768 | tf_op jit(solution)/shard_map/psum | solution.py:915
  (249 shorter events, 115.1 us)
Async XLA Ops:
  7.2 578.0 %copy-start = (bf16[1,704,2048]{2,1,0:T(8,128)(2,1)S(1)}, bf16[1,704,2048]{2,1,0:T(8,128)(2,1)}, u32[]{:S(2)}) copy-start(bf16[1,704,2048]{2,1,0:T(8,128)(2,1)} %param.31) | copy-start | bytes 8650756
  7.2 344.0 %reduce-scatter.3.cloned.1.call-start = ((), (), s32[]{:S(2)}) async-start(), calls=%async_computation.4 | async-start | bytes 3932160 | tf_op jit(solution)/shard_map/reduce_scatter | solution.py:810
  240.8 20.5 %copy-start.43 = (f32[16,1,128]{2,1,0:T(1,128)}, f32[16,1,128]{2,1,0:T(1,128)S(1)}, u32[]{:S(2)}) copy-start(f32[16,1,128]{2,1,0:T(1,128)S(1)} %get-tuple-element.114) | copy-start | bytes 24580
  240.8 113.3 %copy-start.40 = (f32[16,1,128]{2,1,0:T(1,128)}, f32[16,1,128]{2,1,0:T(1,128)S(1)}, u32[]{:S(2)}) copy-start(f32[16,1,128]{2,1,0:T(1,128)S(1)} %get-tuple-element.113) | copy-start | bytes 24580
  282.2 65.9 %all-to-all-start = ((bf16[16,3,128,88]{2,3,1,0:T(8,128)(2,1)}), bf16[16,3,128,88]{2,3,1,0:T(8,128)(2,1)}, u32[]{:S(2)}, u32[]{:S(2)}) async-start(bf16[16,3,128,88]{2,3,1,0:T(8,128)(2,1)} %copy.112), calls=%async_computation.1 | async-start | bytes 2162688 | tf_op jit(solution)/shard_map/all_to_all | solution.py:778
  318.4 17.1 %copy-start.45 = (f32[2560]{0:T(1024)}, f32[2560]{0:T(1024)S(1)}, u32[]{:S(2)}) copy-start(f32[2560]{0:T(1024)S(1)} %mul.519) | copy-start | bytes 30724
  349.5 158.6 %copy-start.23 = (bf16[1,16,128,88]{2,1,3,0:T(8,128)(2,1)}, bf16[1,16,128,88]{2,1,3,0:T(8,128)(2,1)S(1)}, u32[]{:S(2)}) copy-start(bf16[1,16,128,88]{2,1,3,0:T(8,128)(2,1)S(1)} %copy.115) | copy-start | bytes 1081348
  508.1 26.5 %slice-start = ((s8[20971520]{0:T(1024)(128)(4,1)}), s8[4194304]{0:T(1024)(128)(4,1)S(1)}, s32[]{:S(2)}) async-start(s8[20971520]{0:T(1024)(128)(4,1)} %bitcast.240), calls=%async_computation.9 | async-start | bytes 8388608
  508.1 26.5 %slice-start.1 = ((s8[20971520]{0:T(1024)(128)(4,1)}), s8[4194304]{0:T(1024)(128)(4,1)S(1)}, s32[]{:S(2)}) async-start(s8[20971520]{0:T(1024)(128)(4,1)} %bitcast.240), calls=%async_computation.10 | async-start | bytes 8388608
  508.1 26.5 %slice-start.2 = ((s8[20971520]{0:T(1024)(128)(4,1)}), s8[4194304]{0:T(1024)(128)(4,1)S(1)}, s32[]{:S(2)}) async-start(s8[20971520]{0:T(1024)(128)(4,1)} %bitcast.240), calls=%async_computation.11 | async-start | bytes 8388608
  544.2 584.4 %all-to-all-start.1 = ((bf16[16,128,264]{1,2,0:T(8,128)(2,1)}), bf16[16,128,264]{1,2,0:T(8,128)(2,1)}, u32[]{:S(2)}, u32[]{:S(2)}) async-start(bf16[16,128,264]{1,2,0:T(8,128)(2,1)} %pad_maximum_fusion.3), calls=%async_computation.3 | async-start | bytes 2162688 | tf_op jit(solution)/shard_map/all_to_all | solution.py:865
  549.5 263.2 %all-gather.6.cloned.1.call-start = ((), (), s32[]{:S(2)}) async-start(), calls=%async_computation.6 | async-start | bytes 1966080 | tf_op jit(solution)/shard_map/all_gather | solution.py:872
  561.9 13.4 %copy-start.6 = (bf16[16,160,2048]{2,1,0:T(8,128)(2,1)S(1)}, bf16[16,160,2048]{2,1,0:T(8,128)(2,1)}, u32[]{:S(2)}) copy-start(bf16[16,160,2048]{2,1,0:T(8,128)(2,1)} %convolution_convert_fusion) | copy-start | bytes 31457284
  561.9 13.4 %copy-start.60 = (bf16[1,2048,704]{1,2,0:T(8,128)(2,1)S(1)}, bf16[1,2048,704]{1,2,0:T(8,128)(2,1)}, u32[]{:S(2)}) copy-start(bf16[1,2048,704]{1,2,0:T(8,128)(2,1)} %param.29) | copy-start | bytes 8650756
  675.4 100.5 %copy-start.4 = (f32[160,2048]{1,0:T(8,128)S(1)}, f32[160,2048]{1,0:T(8,128)}, u32[]{:S(2)}) copy-start(f32[160,2048]{1,0:T(8,128)} %copy-done.3) | copy-start | bytes 3932164
  675.4 100.5 %copy-start.41 = (f32[16,1,128]{2,1,0:T(1,128)S(1)}, f32[16,1,128]{2,1,0:T(1,128)}, u32[]{:S(2)}) copy-start(f32[16,1,128]{2,1,0:T(1,128)} %copy-done.40) | copy-start | bytes 24580
  675.4 100.5 %copy-start.50 = (f32[160]{0:T(256)S(1)}, f32[160]{0:T(256)}, u32[]{:S(2)}) copy-start(f32[160]{0:T(256)} %copy-done.49) | copy-start | bytes 1924
  675.4 102.7 %copy-start.54 = (f32[160]{0:T(256)S(1)}, f32[160]{0:T(256)}, u32[]{:S(2)}) copy-start(f32[160]{0:T(256)} %copy-done.53) | copy-start | bytes 1924
  675.4 102.7 %copy-start.22 = (bf16[320,2048]{1,0:T(8,128)(2,1)S(1)}, bf16[320,2048]{1,0:T(8,128)(2,1)}, u32[]{:S(2)}) copy-start(bf16[320,2048]{1,0:T(8,128)(2,1)} %param.17) | copy-start | bytes 3932164
  778.1 15.5 %copy-start.51 = (f32[160]{0:T(256)}, f32[160]{0:T(256)S(1)}, u32[]{:S(2)}) copy-start(f32[160]{0:T(256)S(1)} %multiply_multiply_fusion.1) | copy-start | bytes 1924
  780.5 208.3 %reduce-scatter.5.cloned.1.call-start = ((), (), s32[]{:S(2)}) async-start(), calls=%async_computation.7 | async-start | bytes 3932160 | tf_op jit(solution)/shard_map/reduce_scatter | solution.py:900
  832.2 346.7 %all-gather.4.cloned.1.call-start = ((), (), s32[]{:S(2)}) async-start(), calls=%async_computation.5 | async-start | bytes 1966080 | tf_op jit(solution)/shard_map/all_gather | solution.py:856
  854.9 110.6 %copy-start.52 = (f32[160]{0:T(256)S(1)}, f32[160]{0:T(256)}, u32[]{:S(2)}) copy-start(f32[160]{0:T(256)} %get-tuple-element.105) | copy-start | bytes 1924
  854.9 124.2 %slice-start.5 = ((s8[10485760]{0:T(1024)(128)(4,1)}), s8[2097152]{0:T(1024)(128)(4,1)S(1)}, s32[]{:S(2)}) async-start(s8[10485760]{0:T(1024)(128)(4,1)} %bitcast.249), calls=%async_computation.14 | async-start | bytes 4194304
  966.1 13.1 %slice-start.6 = ((s8[10485760]{0:T(1024)(128)(4,1)}), s8[4194304]{0:T(1024)(128)(4,1)S(1)}, s32[]{:S(2)}) async-start(s8[10485760]{0:T(1024)(128)(4,1)} %bitcast.249), calls=%async_computation.15 | async-start | bytes 8388608
  966.1 13.1 %slice-start.7 = ((s8[10485760]{0:T(1024)(128)(4,1)}), s8[4194304]{0:T(1024)(128)(4,1)S(1)}, s32[]{:S(2)}) async-start(s8[10485760]{0:T(1024)(128)(4,1)} %bitcast.249), calls=%async_computation.16 | async-start | bytes 8388608
  966.1 13.1 %copy-start.64 = (bf16[2560,704]{0,1:T(8,128)(2,1)S(1)}, bf16[2560,704]{0,1:T(8,128)(2,1)}, u32[]{:S(2)}) copy-start(bf16[2560,704]{0,1:T(8,128)(2,1)} %get-tuple-element.87) | copy-start | bytes 10813444
  979.2 12.9 %copy-start.7 = (bf16[160,2048]{1,0:T(8,128)(2,1)S(1)}, bf16[160,2048]{1,0:T(8,128)(2,1)}, u32[]{:S(2)}) copy-start(bf16[160,2048]{1,0:T(8,128)(2,1)} %sum_act_grad.1) | copy-start | bytes 1966084
  995.9 13.4 %copy-start.27 = (bf16[8,40,8,128]{3,2,1,0:T(8,128)(2,1)S(1)}, bf16[8,40,8,128]{3,2,1,0:T(8,128)(2,1)}, u32[]{:S(2)}) copy-start(bf16[8,40,8,128]{3,2,1,0:T(8,128)(2,1)} %copy-done.26) | copy-start | bytes 1966084
  995.9 13.4 %copy-start.56 = (f32[320]{0:T(512)S(1)}, f32[320]{0:T(512)}, u32[]{:S(2)}) copy-start(f32[320]{0:T(512)} %copy-done.55) | copy-start | bytes 3844
  995.9 183.0 %all-gather.8.cloned.1.call-start = ((), (), s32[]{:S(2)}) async-start(), calls=%async_computation.8 | async-start | bytes 1966080 | tf_op jit(solution)/shard_map/all_gather | solution.py:903
  996.0 13.3 %copy-start.9 = (bf16[320,2048]{1,0:T(8,128)(2,1)S(1)}, bf16[320,2048]{1,0:T(8,128)(2,1)}, u32[]{:S(2)}) copy-start(bf16[320,2048]{1,0:T(8,128)(2,1)} %param.16) | copy-start | bytes 3932164
  (48 other events, 187.8 us)
Sparse Core Ops, SparseCore 0:
  275.0 38.0 reduce-scatter.2
  780.6 27.3 all-gather.5
  832.3 50.3 reduce-scatter.4
  996.0 25.6 all-gather.3
  1023.1 25.5 all-gather.7
where the time goes:
time: 1200 us; the launch traced here: 1190 us
  Pallas kernels  653 us (54%)
  matrix products  325 us (27%)
  local copies, waits for them, and re-layouts  101 us (8%)
  other arithmetic  46.7 us (4%)
  blocking collectives  40.2 us (3%)
  between operations  15 us (1%)
    pallas_call x1, Pallas kernels, start_gather(): pl.pallas_call(functools.partial(start_kernel, n), out_shape=[jax.ShapeDt...  228 us
    pallas_call x2, Pallas kernels, scatter_rows(): pl.pallas_call(scatter_kernel, out_shape=jax.ShapeDtypeStruct((rows, widt...  211 us
    pallas_call x1, Pallas kernels, gather_rows(): pl.pallas_call(gather_kernel, out_shape=jax.ShapeDtypeStruct((32, rows, w...  115 us
    dot_general x9, matrix products, contract_last(): lax.dot_general(left, right, (((1,), (1,)), ((), ())), preferred_element_...  102 us
    pallas_call x1, Pallas kernels, weight_sums(): pl.pallas_call(functools.partial(wsum_kernel, n), out_shape=[jax.ShapeDty...  100 us
    dot_general x9, matrix products, contract_first(): lax.dot_general(left, right, (((0,), (0,)), ((), ())), preferred_element_...  74.8 us
    dot_general x2, local copies, waits for them, and re-layouts, contract_first(): lax.dot_general(left, right, (((0,), (0,)), ((), ())), preferred_element_...  52.5 us
    psum x1, blocking collectives, on_device(): lax.psum(jnp.stack([gain_one_grad, gain_two_grad]), ('dp', 'tensor'))  40.2 us
  transfers between devices with their start and end apart: 7, of which 0 were waited for; matrix products, arithmetic and copies ran while one was open for 29% of the time, Pallas kernels for 26%

commit v1 on v0

--- a/solution.py
+++ b/solution.py
@@ -718,13 +718,405 @@
         compiler_params=pltpu.CompilerParams(collective_id=cid, has_side_effects=True, vmem_limit_bytes=56 << 20), name=name)(*[a.reshape(16, depth, width) for a in arrays])
 
 
+def nearest(z, g):
+    one = jnp.where(z == 0, 1, z - 1)
+    two = jnp.where(z == 3, 1, jnp.where(z == 2, 3, 2))
+    three = jnp.where(z >= 2, 0, 3)
+    return jnp.where(g == 0, z, jnp.where(g == 1, one, jnp.where(g == 2, two, three)))
+
+def nt(left, right):
+    return lax.dot_general(left, right, (((1,), (1,)), ((), ())), preferred_element_type=jnp.float32)
+
+def nn(left, right):
+    return jnp.dot(left, right, preferred_element_type=jnp.float32)
+
+def expert_kernel(
+    a_in, deh, dhs, rank_row, rank_col, gate, wg_h, wu_h, wd_h, sgu_h, sdt_h,
+    total, act_all, rows_o, eh_o, deg_o, deu_o, hs_o, dsgu_o, part, ffn_part,
+    wg, wu, wd, sgu, tail, acc, ic, iy0, ix0, ix1, iy1, izu, izd,
+    eg, eu, dehb, ehb, degb, deub, dhsb, hsb, dsgub, eh2, hs2, ot,
+    wsem, usem, ssem, osem, psem, lsem,
+    zs, zr, x0s, x0r, x1s, x1r, y0s, y0r, y1s, y1r, cs, cr,
+    ls, rcs, rcr, ry0s, ry0r, rx0s, rx0r, rx1s, rx1r, ry1s, ry1r, zus, zur, zds, zdr,
+):
+    f32, bf16 = jnp.float32, jnp.bfloat16
+    z, x, y, c = place()
+    rows, width = a_in.shape
+    h = rows // 2
+    cap = deh.shape[1]
+    toks = 2 * rows
+    lo, hi = pl.ds(0, h), pl.ds(h, h)
+    part_of = (lo, hi)
+    xn, yn, cn = dev(z, 1 - x, y, c), dev(z, x, 1 - y, c), dev(z, x, y, 1 - c)
+    greet(z, x, y, c)
+    mine = blk(z, x, y, c)
+    own = pltpu.make_async_copy(a_in, act_all.at[mine], lsem)
+    own.start()
+    weights = [
+        pltpu.make_async_copy(a, b, wsem.at[i])
+        for i, (a, b) in enumerate(((wg_h, wg), (wu_h, wu), (wd_h, wd), (sgu_h, sgu), (sdt_h, tail.at[pl.ds(cap, 256 - cap)])))
+    ]
+    for w in weights:
+        w.start()
+
+    def zcopy(s, up):
+        b = act_all.at[blk(s, x, y, c)]
+        return rcopy(b, b, zs.at[s, up], zr.at[s], dev(z + 2 * up - 1, x, y, c))
+
+    def half_copy(s, xx, yy, p, send, recv, to):
+        b = act_all.at[blk(s, xx, yy, c), part_of[p]]
+        return rcopy(b, b, send, recv, to)
+
+    def x0(s): return half_copy(s, x, y, 0, x0s.at[s], x0r.at[s], xn)
+    def y1(s): return half_copy(s, x, y, 1, y1s.at[s], y1r.at[s], yn)
+    def y0(s, xx): return half_copy(s, xx, y, 0, y0s.at[s, xx], y0r.at[s, xx], yn)
+    def x1(s, yy): return half_copy(s, x, yy, 1, x1s.at[s, yy], x1r.at[s, yy], xn)
+    def side(s, xx, yy, p):
+        i = (s * 2 + xx) * 2 + yy
+        return half_copy(s, xx, yy, p, cs.at[i, p], cr.at[i, p], cn)
+
+    def column(s):
+        x0(s).start(); y1(s).start(); y0(s, x).start(); x1(s, y).start()
+        side(s, x, y, 0).start(); side(s, x, y, 1).start()
+
+    def arrive(g):
+        s = nearest(z, g)
+        up = (s < z).astype(jnp.int32)
+        nxt = z + 2 * up - 1
+        zcopy(s, up).wait_recv()
+        @pl.when((nxt >= 0) & (nxt <= 3))
+        def _(): zcopy(s, up).start()
+        column(s)
+
+    def middle(g):
+        s = nearest(z, g)
+        x0(s).wait_recv()
+        y0(s, 1 - x).start(); side(s, 1 - x, y, 0).start()
+        y1(s).wait_recv()
+        x1(s, 1 - y).start(); side(s, x, 1 - y, 1).start()
+
+    def last_own(g):
+        s = nearest(z, g)
+        y0(s, x).wait_recv(); side(s, x, 1 - y, 0).start()
+
+    def last_other(g):
+        s = nearest(z, g)
+        x1(s, y).wait_recv(); side(s, 1 - x, y, 1).start()
+        y0(s, 1 - x).wait_recv(); side(s, 1 - x, 1 - y, 0).start()
+        x1(s, 1 - y).wait_recv(); side(s, 1 - x, 1 - y, 1).start()
+
+    def spread_cols(j):
+        ranks = rank_col[j]
+        slot = lax.broadcasted_iota(jnp.int32, (toks, 128), 1)
+        one = jnp.where(ranks == slot, 1.0, 0.0)
+        two = jnp.where(ranks == slot + 128, 1.0, 0.0)
+        return one, two
+
+    def seq_of(u):
+        s = nearest(z, u // 2)
+        xx = lax.rem(x + lax.rem(u, 2), 2)
+        return s, xx
+
+    def stores(u):
+        s, xx = seq_of(u)
+        out = []
+        for k in (0, 1):
+            j = (s * 2 + xx) * 2 + k
+            r = pl.ds(k * cap, cap)
+            out += [
+                pltpu.make_async_copy(acc.at[k], rows_o.at[j], ssem.at[k, 0]),
+                pltpu.make_async_copy(ehb.at[r], eh_o.at[j], ssem.at[k, 1]),
+                pltpu.make_async_copy(degb.at[r], deg_o.at[j], ssem.at[k, 2]),
+                pltpu.make_async_copy(deub.at[r], deu_o.at[j], ssem.at[k, 3]),
+                pltpu.make_async_copy(hsb.at[k], hs_o.at[j], ssem.at[k, 4]),
+                pltpu.make_async_copy(dsgub.at[k], dsgu_o.at[j], ssem.at[k, 5]),
+                pltpu.make_async_copy(acc.at[pl.ds(10 + 2 * k, 2)], part.at[pl.ds(2 * j, 2)], ssem.at[k, 6]),
+            ]
+        return out
+
+    def unit(u):
+        s, xx = seq_of(u)
+        base = (s * 2 + xx) * 2
+        for k in (0, 1):
+            pltpu.make_async_copy(deh.at[base + k], dehb.at[pl.ds(k * cap, cap)], usem.at[k, 1]).start()
+            pltpu.make_async_copy(dhs.at[base + k], dhsb.at[k], usem.at[k, 2]).start()
+        for yy in (0, 1):
+            for p in (0, 1):
+                side(s, xx, yy, p).wait_recv()
+        loads = [
+            pltpu.make_async_copy(act_all.at[pl.ds(2 * (base + k), 2)], acc.at[pl.ds(4 + 2 * k, 2)], usem.at[k, 0])
+            for k in (0, 1)
+        ]
+        for k in (0, 1):
+            loads[k].start()
+        @pl.when(u > 0)
+        def _():
+            for copy in stores(u - 1):
+                copy.wait()
+        for k in (0, 1):
+            loads[k].wait()
+            act = acc[4 + 2 * k:6 + 2 * k].reshape(toks, width)
+            ranks = rank_row[base + k]
+            slot = lax.broadcasted_iota(jnp.int32, (cap, toks), 0)
+            pick = jnp.where(ranks == slot, 1.0, 0.0).astype(bf16)
+            acc[k] = nn(pick, act).astype(bf16)
+            pre = nn(act, sgu[...])
+            gp, up = pre[:, :128], pre[:, 128:]
+            pltpu.make_async_copy(dhs.at[base + k], dhsb.at[k], usem.at[k, 2]).wait()
+            dh = dhsb[k]
+            sig = jax.nn.sigmoid(gp)
+            hsb[k] = (gp * sig * up).astype(bf16)
+            dsgub[k, :, 0:128] = (dh * up * sig * (1.0 + gp * (1.0 - sig))).astype(bf16)
+            dsgub[k, :, 128:256] = (dh * gp * sig).astype(bf16)
+        picked = acc[0:2].reshape(2 * cap, width)
+        eg[...] = nn(picked, wg[...])
+        eu[...] = nn(picked, wu[...])
+        for k in (0, 1):
+            pltpu.make_async_copy(deh.at[base + k], dehb.at[pl.ds(k * cap, cap)], usem.at[k, 1]).wait()
+        @pl.loop(0, 2 * cap // 32)
+        def _(r):
+            q = pl.ds(pl.multiple_of(r * 32, 32), 32)
+            gp, up, dh = eg[q], eu[q], dehb[q]
+            sig = jax.nn.sigmoid(gp)
+            silu = gp * sig
+            ehb[q] = (silu * up).astype(bf16)
+            degb[q] = (dh * up * sig * (1.0 + gp * (1.0 - sig))).astype(bf16)
+            deub[q] = (dh * silu).astype(bf16)
+        dg, du = degb[...], deub[...]
+        for n in range(0, width, 512):
+            w = pl.ds(n, 512)
+            back = (nt(dg, wg[w, :]) + nt(du, wu[w, :])).astype(bf16)
+            acc[8, :, w] = back[:cap]
+            acc[9, :, w] = back[cap:]
+        for k in (0, 1):
+            one, two = spread_cols(base + k)
+            left = jnp.concatenate([one, two], axis=1)[:, :cap].astype(bf16)
+            for n in range(0, width, 512):
+                w = pl.ds(n, 512)
+                out = nn(left, acc[8 + k, :, w]) + nt(dsgub[k], sgu[w, :])
+                out = out.astype(bf16)
+                acc[10 + 2 * k, :, w] = out[:rows]
+                acc[11 + 2 * k, :, w] = out[rows:]
+        for copy in stores(u):
+            copy.start()
+
+    own.wait()
+    @pl.when(z < 3)
+    def _(): zcopy(z, 1).start()
+    @pl.when(z > 0)
+    def _(): zcopy(z, 0).start()
+    column(z)
+    for w in weights:
+        w.wait()
+
+    @pl.loop(0, 8)
+    def _(u):
+        @pl.when(u == 0)
+        def _():
+            middle(0); last_own(0); arrive(1)
+        @pl.when(u == 1)
+        def _():
+            last_other(0); arrive(2); middle(1)
+        @pl.when(u == 2)
+        def _():
+            arrive(3); last_own(1); middle(2)
+        @pl.when(u == 3)
+        def _():
+            last_other(1); middle(3)
+        @pl.when(u == 4)
+        def _():
+            last_own(2)
+        @pl.when(u == 5)
+        def _():
+            last_other(2)
+        @pl.when(u == 6)
+        def _():
+            last_own(3)
+        @pl.when(u == 7)
+        def _():
+            last_other(3)
+        unit(u)
+
+    for copy in stores(7):
+        copy.wait()
+
+    def at(s, xx, yy): return (s * 2 + xx) * 2 + yy
+    def load(s, xx, yy):
+        return pltpu.make_async_copy(part.at[blk(s, xx, yy, c)], acc.at[at(s, xx, yy)], ls.at[at(s, xx, yy)])
+    def cross(s, xx, yy):
+        i = at(s, xx, yy)
+        return rcopy(part.at[blk(s, xx, yy, 1 - c)], ic.at[i], rcs.at[i], rcr.at[i], cn)
+    def ry0(s, xx):
+        return rcopy(acc.at[at(s, xx, 1 - y), lo], iy0.at[s * 2 + xx], ry0s.at[s, xx], ry0r.at[s, xx], yn)
+    def rx1(s, yy):
+        return rcopy(acc.at[at(s, 1 - x, yy), hi], ix1.at[s * 2 + yy], rx1s.at[s, yy], rx1r.at[s, yy], xn)
+    def rx0(s):
+        return rcopy(acc.at[at(s, 1 - x, y), lo], ix0.at[s], rx0s.at[s], rx0r.at[s], xn)
+    def ry1(s):
+        return rcopy(acc.at[at(s, x, 1 - y), hi], iy1.at[s], ry1s.at[s], ry1r.at[s], yn)
+    def zu(s):
+        return rcopy(acc.at[at(s, x, y)], izu.at[s], zus.at[s], zur.at[s], dev(z + 1, x, y, c))
+    def zd(s):
+        return rcopy(acc.at[at(s, x, y)], izd.at[s], zds.at[s], zdr.at[s], dev(z - 1, x, y, c))
+    def add(i, start, count, src, j):
+        @pl.loop(0, count // 16)
+        def _(r):
+            a = pl.ds(pl.multiple_of(start + r * 16, 16), 16)
+            b = pl.ds(pl.multiple_of(r * 16, 16), 16)
+            acc[i, a] = acc[i, a] + src[j, b]
+
+    def first(s):
+        for xx in (0, 1):
+            for yy in (0, 1):
+                load(s, xx, yy).wait(); cross(s, xx, yy).wait_recv()
+                add(at(s, xx, yy), 0, rows, ic, at(s, xx, yy))
+                @pl.when(yy != y)
+                def _(): ry0(s, xx).start()
+                @pl.when(xx != x)
+                def _(): rx1(s, yy).start()
+
+    def second(s):
+        ry0(s, 1 - x).wait_recv(); add(at(s, 1 - x, y), 0, h, iy0, s * 2 + 1 - x); rx0(s).start()
+        rx1(s, 1 - y).wait_recv(); add(at(s, x, 1 - y), h, h, ix1, s * 2 + 1 - y); ry1(s).start()
+        ry0(s, x).wait_recv(); add(at(s, x, y), 0, h, iy0, s * 2 + x)
+        rx1(s, y).wait_recv(); add(at(s, x, y), h, h, ix1, s * 2 + y)
+
+    def third(s):
+        me = at(s, x, y)
+        rx0(s).wait_recv(); add(me, 0, h, ix0, s)
+        ry1(s).wait_recv(); add(me, h, h, iy1, s)
+        @pl.when((s >= z) & (z > 0))
+        def _():
+            zu(s).wait_recv(); add(me, 0, rows, izu, s)
+        @pl.when((s <= z) & (z < 3))
+        def _():
+            zd(s).wait_recv(); add(me, 0, rows, izd, s)
+        @pl.when(s > z)
+        def _(): zu(s).start()
+        @pl.when(s < z)
+        def _(): zd(s).start()
+
+    for g in (3, 2, 1, 0):
+        s = nearest(z, g)
+        for xx in (0, 1):
+            for yy in (0, 1):
+                cross(s, xx, yy).start(); load(s, xx, yy).start()
+
+    def out_loads(j, b):
+        return [
+            pltpu.make_async_copy(eh_o.at[j], eh2.at[b], osem.at[b, 0]),
+            pltpu.make_async_copy(hs_o.at[j], hs2.at[b], osem.at[b, 1]),
+        ]
+    def out_store(j, b):
+        return pltpu.make_async_copy(ot.at[b], ffn_part.at[pl.ds(2 * j, 2)], psem.at[b])
+
+    def forward_out(j):
+        b = lax.rem(j, 2)
+        @pl.when(j < 15)
+        def _():
+            for copy in out_loads(j + 1, 1 - b):
+                copy.start()
+        for copy in out_loads(j, b):
+            copy.wait()
+        @pl.when(j >= 2)
+        def _(): out_store(j - 2, b).wait()
+        weight = gate[j]
+        for n in range(0, width, 512):
+            w = pl.ds(n, 512)
+            tail[0:cap, w] = (nn(eh2[b], wd[:, w]) * weight).astype(bf16)
+        one, two = spread_cols(j)
+        left = jnp.concatenate([one, two + hs2[b].astype(f32)], axis=1).astype(bf16)
+        for n in range(0, width, 512):
+            w = pl.ds(n, 512)
+            out = nn(left, tail[:, w]).astype(bf16)
+            ot[b, 0, :, w] = out[:rows]
+            ot[b, 1, :, w] = out[rows:]
+        out_store(j, b).start()
+
+    for copy in out_loads(0, 0):
+        copy.start()
+
+    @pl.loop(0, 6)
+    def _(t):
+        @pl.when(t < 4)
+        def _():
+            first(nearest(z, 3 - t))
+            @pl.loop(0, 4)
+            def _(i): forward_out(4 * t + i)
+        @pl.when((t >= 1) & (t < 5))
+        def _(): second(nearest(z, 4 - t))
+        @pl.when(t >= 2)
+        def _(): third(nearest(z, 5 - t))
+
+    total[...] = acc[at(z, x, y)]
+    out_store(14, 0).wait()
+    out_store(15, 1).wait()
+
+    for s in range(4):
+        x0(s).wait_send(); y1(s).wait_send()
+        rx0(s).wait_send(); ry1(s).wait_send()
+        for q in (0, 1):
+            y0(s, q).wait_send(); x1(s, q).wait_send()
+            ry0(s, q).wait_send(); rx1(s, q).wait_send()
+            for r in (0, 1):
+                cross(s, q, r).wait_send()
+                for p in (0, 1):
+                    side(s, q, r, p).wait_send()
+        @pl.when((z < 3) & (s <= z))
+        def _(): zcopy(s, 1).wait_send()
+        @pl.when((z > 0) & (s >= z))
+        def _(): zcopy(s, 0).wait_send()
+        @pl.when(s > z)
+        def _(): zu(s).wait_send()
+        @pl.when(s < z)
+        def _(): zd(s).wait_send()
+
+def expert_layer(act, deh, dhs, rank_row, rank_col, gate, wg, wu, wd, sgu, sdt, cid):
+    rows, width = act.shape
+    cap, hidden = deh.shape[1:]
+    h = rows // 2
+    f32, bf16 = jnp.float32, jnp.bfloat16
+    D = pltpu.SemaphoreType.DMA
+    S = jax.ShapeDtypeStruct
+    any_ = pl.BlockSpec(memory_space=pl.ANY)
+    vm = pl.BlockSpec(memory_space=pltpu.VMEM)
+    V = lambda *shape, t=bf16: pltpu.VMEM(shape, t)
+    return pl.pallas_call(
+        expert_kernel,
+        out_shape=[
+            S((rows, width), bf16), S((32, rows, width), bf16), S((16, cap, width), bf16),
+            S((16, cap, hidden), bf16), S((16, cap, hidden), bf16), S((16, cap, hidden), bf16),
+            S((16, 2 * rows, 128), bf16), S((16, 2 * rows, 256), bf16),
+            S((32, rows, width), bf16), S((32, rows, width), bf16),
+        ],
+        in_specs=[any_, any_, any_, vm, vm, vm] + [any_] * 5,
+        out_specs=[vm] + [any_] * 9,
+        scratch_shapes=[
+            V(*wg.shape), V(*wu.shape), V(*wd.shape), V(*sgu.shape), V(256, width),
+            V(16, rows, width), V(16, rows, width), V(8, h, width), V(4, h, width), V(8, h, width), V(4, h, width),
+            V(4, rows, width), V(4, rows, width),
+            V(2 * cap, hidden, t=f32), V(2 * cap, hidden, t=f32), V(2 * cap, hidden, t=f32),
+            V(2 * cap, hidden), V(2 * cap, hidden), V(2 * cap, hidden),
+            V(2, 2 * rows, 128, t=f32), V(2, 2 * rows, 128), V(2, 2 * rows, 256),
+            V(2, cap, hidden), V(2, 2 * rows, 128), V(2, 2, rows, width),
+            D((5,)), D((2, 3)), D((2, 7)), D((2, 2)), D((2,)), D,
+            D((4, 2)), D((4,)), D((4,)), D((4,)), D((4, 2)), D((4, 2)), D((4, 2)), D((4, 2)), D((4,)), D((4,)), D((16, 2)), D((16, 2)),
+            D((16,)), D((16,)), D((16,)), D((4, 2)), D((4, 2)), D((4,)), D((4,)), D((4, 2)), D((4, 2)), D((4,)), D((4,)),
+            D((4,)), D((4,)), D((4,)), D((4,)),
+        ],
+        compiler_params=pltpu.CompilerParams(collective_id=cid, has_side_effects=True, vmem_limit_bytes=62 << 20),
+        name="expert_layer",
+    )(act, deh, dhs, rank_row, rank_col, gate, wg, wu, wd, sgu, sdt)
+
+
 def routing_tables(gate_table, capacity):
     member = gate_table > 0.0
     ranks = jnp.cumsum(member.astype(jnp.int32), axis=1) - 1
     slot = jnp.arange(capacity, dtype=jnp.int32)
     pick = (ranks[:, None, :] == slot[None, :, None]) & member[:, None, :]
     slot_gate = jnp.sum(jnp.where(pick, gate_table[:, None, :], 0.0), axis=2)
-    return pick.astype(jnp.bfloat16), slot_gate
+    held = jnp.where(member, ranks, -1)
+    return pick.astype(jnp.bfloat16), slot_gate, held
 
 
 def on_device(
@@ -777,11 +1169,9 @@
     packed = packed.reshape(3, depth, experts, common_dev).transpose(2, 0, 1, 3)
     packed = lax.all_to_all(packed, "dp", split_axis=0, concat_axis=0, tiled=True)
     packed = packed.transpose(1, 0, 2, 3).reshape(3, width, common_dev)
-    common_gu = jnp.concatenate([packed[0], packed[1]], axis=1)
-    common_down = packed[2]
 
     table = lax.dynamic_index_in_dim(tables, lax.axis_index("dp"), axis=1, keepdims=False)
-    pick, slot_gate = routing_tables(table, capacity)
+    pick, slot_gate, held = routing_tables(table, capacity)
 
     x_in = tokens.astype(f32)
     act_one = rms_norm(x_in, gain_one).astype(bf16)
@@ -814,52 +1204,54 @@
     x_mid = x_half + attn
     act_two = rms_norm(x_mid, gain_two).astype(bf16)
 
-    act_all = gather_rows(act_two, 1, "gather_act")
-    act_blocks = act_all.reshape(experts, rows_dev, width)
     grad_blocks = grad_all.reshape(experts, rows_dev, width)
     exp_gate, exp_up, exp_down = expert_gate[0], expert_up[0], expert_down[0]
-
-    def select(blocks):
-        return jnp.einsum("jst,jtd->jsd", pick, blocks, preferred_element_type=f32)
-
-    def spread(rows):
-        return jnp.einsum(
-            "jst,jsd->jtd", pick, rows.reshape(experts, capacity, width), preferred_element_type=f32
-        ).reshape(experts * rows_dev, width)
-
     weight = slot_gate.reshape(slots, 1)
-    rows = select(act_blocks).astype(bf16).reshape(slots, width)
-    rows_out_grad = (weight * select(grad_blocks).reshape(slots, width)).astype(bf16)
-    gate_rows = jnp.dot(rows, exp_gate, preferred_element_type=f32)
-    up_rows = jnp.dot(rows, exp_up, preferred_element_type=f32)
-    hidden_rows, expert_vjp = jax.vjp(gated, gate_rows, up_rows)
-    hidden_rows = hidden_rows.astype(bf16)
-    hidden_rows_grad = contract_last(rows_out_grad, exp_down)
-    gate_rows_grad, up_rows_grad = expert_vjp(hidden_rows_grad)
-    gate_rows_grad = gate_rows_grad.astype(bf16)
-    up_rows_grad = up_rows_grad.astype(bf16)
-    rows_in_grad = contract_last(gate_rows_grad, exp_gate) + contract_last(up_rows_grad, exp_up)
-
-    common_pre = jnp.dot(act_all, common_gu, preferred_element_type=f32)
-    common_hidden, common_vjp = jax.vjp(
-        gated, common_pre[:, :common_dev], common_pre[:, common_dev:]
-    )
-    common_hidden = common_hidden.astype(bf16)
+    rows_out_grad = jnp.einsum("jst,jtd->jsd", pick, grad_blocks, preferred_element_type=f32)
+    rows_out_grad = (weight * rows_out_grad.reshape(slots, width)).astype(bf16)
+    hidden_rows_grad = contract_last(rows_out_grad, exp_down).reshape(experts, capacity, -1)
+    front = capacity - 128
+    back = 128 - front - common_dev
+
+    def widen(w):
+        return jnp.pad(w, ((0, 0), (front, back)))
+
+    common_gu = jnp.concatenate([widen(packed[0]), widen(packed[1])], axis=1)
+    common_down = widen(packed[2])
     common_hidden_grad = jnp.dot(grad_all, common_down, preferred_element_type=f32)
-    common_gu_grad = jnp.concatenate(common_vjp(common_hidden_grad), axis=1).astype(bf16)
-    act_grad = spread(rows_in_grad.astype(bf16)) + contract_last(common_gu_grad, common_gu)
-    act_two_total = scatter_rows(act_grad.astype(bf16), 2, "sum_act_grad").astype(f32)
-
-    rows_out = jnp.dot(hidden_rows, exp_down, preferred_element_type=f32) * weight
-    ffn = spread(rows_out.astype(bf16)) + contract_last(common_hidden, common_down)
-    ffn = scatter_rows(ffn.astype(bf16), 3, "sum_ffn").astype(f32)
+    down_rows = common_down.T[front:]
+    total_grad, act_all, rows, hidden_rows, gate_rows_grad, up_rows_grad, common_hidden, common_gu_grad, unused, ffn = (
+        expert_layer(
+            act_two,
+            hidden_rows_grad,
+            common_hidden_grad.reshape(experts, rows_dev, 128),
+            held[:, None, :],
+            held[:, :, None],
+            slot_gate[:, :, None],
+            exp_gate,
+            exp_up,
+            exp_down,
+            common_gu,
+            down_rows,
+            1,
+        )
+    )
+    act_two_total = total_grad.astype(f32)
+    act_all = act_all.reshape(-1, width)
+    rows = rows.reshape(slots, width)
+    hidden_rows = hidden_rows.reshape(slots, -1)
+    common_hidden = common_hidden.reshape(-1, 128)
+    common_gu_grad = common_gu_grad.reshape(-1, 256)
+    ffn = scatter_rows(ffn.reshape(-1, width), 3, "sum_ffn").astype(f32)
     layer_out = lax.all_gather((x_mid + ffn).astype(bf16), "tensor", axis=0, tiled=True)
 
-    expert_gate_grad = contract_first(rows, gate_rows_grad)[None]
-    expert_up_grad = contract_first(rows, up_rows_grad)[None]
+    expert_gate_grad = contract_first(rows, gate_rows_grad.reshape(slots, -1))[None]
+    expert_up_grad = contract_first(rows, up_rows_grad.reshape(slots, -1))[None]
     expert_down_grad = contract_first(hidden_rows, rows_out_grad)[None]
+    gu_grad = contract_first(act_all, common_gu_grad)
+    down_grad = contract_first(grad_all, common_hidden)
     common_w_grad = jnp.concatenate(
-        [contract_first(act_all, common_gu_grad), contract_first(grad_all, common_hidden)], axis=1
+        [w[:, front : front + common_dev] for w in (gu_grad[:, :128], gu_grad[:, 128:], down_grad)], axis=1
     )
     common_w_grad = common_w_grad.astype(bf16).reshape(experts, depth, 3 * common_dev)
     common_w_grad = lax.all_to_all(common_w_grad, "dp", split_axis=0, concat_axis=0, tiled=True)

time: 1200 us -> 1020 us (0.85)
  matrix products: 325 us -> 143 us
  Pallas kernels: 653 us -> 720 us
  local copies, waits for them, and re-layouts: 101 us -> 50.6 us
  other arithmetic: 46.7 us -> 27.8 us
    pallas_call x1, Pallas kernels: 115 us -> 266 us  [expert_layer(): pl.pallas_call(expert_kernel, out_shape=[S((rows, width), bf16), S((32, r...]
    dot_general x8 -> x1, matrix products: 115 us -> 12.3 us  [on_device(): jnp.einsum('jst,jtd->jsd', pick, grad_blocks, preferred_element_type=f32)]
    pallas_call x2 -> x1, Pallas kernels: 211 us -> 127 us  [scatter_rows(): pl.pallas_call(scatter_kernel, out_shape=jax.ShapeDtypeStruct((rows, widt...]
    dot_general x9 -> x5, matrix products: 102 us -> 23.6 us  [contract_last(): lax.dot_general(left, right, (((1,), (1,)), ((), ())), preferred_element_...]
    dot_general x2 -> x0, local copies, waits for them, and re-layouts: 52.5 us -> none  [contract_first(): lax.dot_general(left, right, (((0,), (0,)), ((), ())), preferred_element_...]
    convert_element_type x1 -> x0, other arithmetic: 12.5 us -> none  [on_device(): (weight * select(grad_blocks).reshape(slots, width)).astype(bf16)]
    unnamed x161 -> x114, local copies, waits for them, and re-layouts: 27.6 us -> 27.3 us
  transfers between devices with their start and end apart: 7 -> 7, of which waited for: 0 -> 1; matrix products, arithmetic and copies ran while one was open for 29% -> 15% of each run, Pallas kernels for 26% -> 22%
where the time goes in v1:
time: 1020 us; the launch traced here: 1010 us
  Pallas kernels  720 us (71%)
  matrix products  143 us (14%)
  local copies, waits for them, and re-layouts  50.6 us (5%)
  blocking collectives  40.4 us (4%)
  other arithmetic  27.8 us (3%)
  between operations  14.9 us (1%)
  starting transfers between devices  13.2 us (1%)
    pallas_call x1, Pallas kernels, expert_layer(): pl.pallas_call(expert_kernel, out_shape=[S((rows, width), bf16), S((32, r...  266 us
    pallas_call x1, Pallas kernels, start_gather(): pl.pallas_call(functools.partial(start_kernel, n), out_shape=[jax.ShapeDt...  228 us
    pallas_call x1, Pallas kernels, scatter_rows(): pl.pallas_call(scatter_kernel, out_shape=jax.ShapeDtypeStruct((rows, widt...  127 us
    pallas_call x1, Pallas kernels, weight_sums(): pl.pallas_call(functools.partial(wsum_kernel, n), out_shape=[jax.ShapeDty...  99.9 us
    dot_general x9, matrix products, contract_first(): lax.dot_general(left, right, (((0,), (0,)), ((), ())), preferred_element_...  78.6 us
    psum x1, blocking collectives, on_device(): lax.psum(jnp.stack([gain_one_grad, gain_two_grad]), ('dp', 'tensor'))  40.4 us
    unnamed x114, local copies, waits for them, and re-layouts  27.3 us
    dot_general x5, matrix products, contract_last(): lax.dot_general(left, right, (((1,), (1,)), ((), ())), preferred_element_...  23.6 us
  transfers between devices with their start and end apart: 7, of which 1 were waited for; matrix products, arithmetic and copies ran while one was open for 15% of the time, Pallas kernels for 22%

profile of v1, /device:TPU:0, one launch (start us, length us, event | category | flops | bytes accessed | tf_op | source)
XLA Modules:
  0.0 1013.6 jit_solution(5793198062087809716)
XLA Ops:
  12.1 227.7 %gather_weights.1 = (bf16[16,128,1024]{2,1,0:T(8,128)(2,1)}, bf16[16,128,1024]{2,1,0:T(8,128)(2,1)}, bf16[16,128,1024]{2,1,0:T(8,128)(2,1)}, bf16[16,128,1024]{2...) custom-call(bf16[128,1024]{1,0:T(8,128)(2,1)} %refs_0_.1, ...), custom_call_target="tpu_custom_call" | custom-call | tf_op jit(solution)/shard_map/gather_weights/pallas_call | solution.py:617
  239.8 6.7 copy.149
  247.8 6.4 copy.150
  254.2 3.5 fusion.36
  261.5 2.0 multiply_cosine_fusion
  270.3 3.2 fusion.55
  276.4 6.1 all-to-all-start
  286.2 12.3 %multiply_convert_fusion = bf16[16,160,2048]{2,1,0:T(8,128)(2,1)} fusion(f32[16,160]{1,0:T(8,128)S(1)} %select_reduce_fusion, bf16[16,320,2048]{2,1,0:T(8,128)(2,1)} %bitcast.190, s32[16,320]{1,0:T(8,128)S(1)} %get-tuple-element.144, pred[16,320]{1,0:T(8,128)(4,1)S(1)} %bitcast.225), kind=kOutput, calls=%fused_computation | convolution fusion | flops 3367567360 | bytes 31493120 | tf_op jit(solution)/shard_map/jst,jtd->jsd/dot_general | solution.py:1210
  299.1 2.3 copy.166.rank_col
  303.0 4.6 copy.162
  307.5 4.6 copy.163
  312.1 13.9 %fusion.4.deh = f32[16,160,704]{2,1,0:T(8,128)} fusion(bf16[16,160,2048]{2,1,0:T(8,128)(2,1)} %multiply_convert_fusion, bf16[1,704,2048]{2,1,0:T(8,128)(2,1)} %param.31), kind=kOutput, calls=%fused_computation.21 | convolution fusion | flops 7381975040 | bytes 20578304 | tf_op jit(solution)/shard_map/dot_general | solution.py:41
  329.0 11.4 %fusion.74.dhs = f32[16,320,128]{2,1,0:T(8,128)} fusion(bf16[16,320,2048]{2,1,0:T(8,128)(2,1)} %bitcast.191, bf16[2048,88]{0,1:T(8,128)(2,1)S(1)} %bitcast.213), kind=kOutput, calls=%fused_computation.125 | convolution fusion | flops 2684354560 | bytes 23953408 | tf_op jit(solution)/shard_map/dot_general | solution.py:1221
  343.1 265.5 %expert_layer.1 = (bf16[160,2048]{1,0:T(8,128)(2,1)}, bf16[32,160,2048]{2,1,0:T(8,128)(2,1)}, bf16[16,160,2048]{2,1,0:T(8,128)(2,1)}, bf16[16,160,704]{2,1,0:T(8...) custom-call(bf16[160,2048]{1,0:T(8,128)(2,1)} %multiply_convert_fusi, ...), custom_call_target="tpu_custom_call" | custom-call | tf_op jit(solution)/shard_map/expert_layer/pallas_call | solution.py:1084
  611.7 12.1 %convolution_convert_fusion.4 = bf16[2048,256]{0,1:T(8,128)(2,1)} fusion(bf16[5120,2048]{1,0:T(8,128)(2,1)} %bitcast.241, bf16[5120,256]{1,0:T(8,128)(2,1)} %bitcast.246), kind=kOutput, calls=%fused_computation.33 | convolution fusion | flops 5369233408 | bytes 24641536 | tf_op jit(solution)/shard_map/dot_general | solution.py:47
  623.8 10.0 fusion.94
  633.8 3.4 all-gather.6.cloned.1.call-done
  637.3 4.2 fusion.39
  653.8 3.1 convolution_add_fusion
  657.0 127.3 %sum_ffn.1 = bf16[160,2048]{1,0:T(8,128)(2,1)} custom-call(bf16[32,160,2048]{2,1,0:T(8,128)(2,1)} %get-tuple-element.41.p_ref), custom_call_target="tpu_custom_call" | custom-call | tf_op jit(solution)/shard_map/sum_ffn/pallas_call | solution.py:502
  785.6 7.0 all-to-all-start.1
  792.6 13.3 %convolution_bitcast_fusion.2 = f32[1,2048,704]{1,2,0:T(8,128)} fusion(bf16[16,160,2048]{2,1,0:T(8,128)(2,1)} %get-tuple-element.50, bf16[16,160,704]{2,1,0:T(8,128)(2,1)} %get-tuple-element.51), kind=kOutput, calls=%fused_computation.16 | convolution fusion | flops 7381975040 | bytes 19857408 | tf_op jit(solution)/shard_map/dot_general | solution.py:47
  805.9 12.0 %convolution_bitcast_fusion = f32[1,704,2048]{2,1,0:T(8,128)} fusion(bf16[16,160,704]{2,1,0:T(8,128)(2,1)S(1)} %copy-done.43, bf16[16,160,2048]{2,1,0:T(8,128)(2,1)} %multiply_convert_fusion), kind=kOutput, calls=%fused_computation.14 | convolution fusion | flops 7381975040 | bytes 19857408 | tf_op jit(solution)/shard_map/dot_general | solution.py:47
  820.0 2.9 fusion.29
  822.9 13.4 %convolution_bitcast_fusion.1 = f32[1,2048,704]{1,2,0:T(8,128)} fusion(bf16[16,160,2048]{2,1,0:T(8,128)(2,1)} %get-tuple-element.50, bf16[16,160,704]{2,1,0:T(8,128)(2,1)} %get-tuple-element.52), kind=kOutput, calls=%fused_computation.15 | convolution fusion | flops 7381975040 | bytes 19857408 | tf_op jit(solution)/shard_map/dot_general | solution.py:47
  836.4 4.4 convolution_convert_fusion.3
  840.8 4.5 convolution_convert_fusion.2
  845.3 4.5 convolution_convert_fusion.1
  849.9 4.3 convolution_convert_fusion
  854.2 99.9 %sum_weight_grads.1 = (f32[128,1024]{1,0:T(8,128)}, f32[128,1024]{1,0:T(8,128)}, f32[128,1024]{1,0:T(8,128)}, f32[128,1024]{1,0:T(8,128)}) custom-call(bf16[16,128,1024]{2,1,0:T(8,128)(2,1)} %bitcast.202, bf16[16,128,1024]{2,1,0:T(8,128)(2,1)} %bitcast.203, bf16[16,128,1024]{2,1,0:T(8,128)(2,1)} %bitcast.204, bf16[16,128,1024]{2,1,0:T(8,128)(2,1)} %bitcast.205), custom_call_target="tpu_custom_call" | custom-call | tf_op jit(solution)/shard_map/sum_weight_grads/pallas_call | solution.py:714
  959.0 40.4 %psum.7 = f32[2,2048]{1,0:T(2,128)S(1)} all-reduce(f32[2,2048]{1,0:T(2,128)S(1)} %pad_maximum_fusion.7), channel_id=1, replica_groups=mesh['dp'=16,'tensor'=2] {'dp','tensor'}, use_global_device_ids=true, to_apply=%region_16.17 | all-reduce | flops 4096 | bytes 32768 | tf_op jit(solution)/shard_map/psum | solution.py:1307
  999.9 2.7 copy.272
  (191 shorter events, 59.0 us)
Async XLA Ops:
  7.2 333.3 %reduce-scatter.3.cloned.1.call-start = ((), (), s32[]{:S(2)}) async-start(), calls=%async_computation.4 | async-start | bytes 3932160 | tf_op jit(solution)/shard_map/reduce_scatter | solution.py:1200
  239.8 7.6 copy-start.2
  247.8 11.6 %copy-start.38 = (f32[320]{0:T(512)}, f32[320]{0:T(512)S(1)}, u32[]{:S(2)}) copy-start(f32[320]{0:T(512)S(1)} %add_rsqrt_fusion) | copy-start | bytes 3844
  254.2 3.6 copy-start.16
  257.8 2.2 copy-start.40
  261.5 5.0 copy-start.22
  267.9 2.4 copy-start.42
  269.0 4.6 copy-start.46
  276.4 49.5 %all-to-all-start = ((bf16[16,3,128,88]{2,3,1,0:T(8,128)(2,1)}), bf16[16,3,128,88]{2,3,1,0:T(8,128)(2,1)S(1)}, u32[]{:S(2)}, u32[]{:S(2)}) async-start(bf16[16,3,128,88]{2,3,1,0:T(8,128)(2,1)} %copy.159), calls=%async_computation.1 | async-start | bytes 2162688 | tf_op jit(solution)/shard_map/all_to_all | solution.py:1170
  282.5 354.8 %all-gather.6.cloned.1.call-start = ((), (), s32[]{:S(2)}) async-start(), calls=%async_computation.6 | async-start | bytes 1966080 | tf_op jit(solution)/shard_map/all_gather | solution.py:1264
  611.7 206.3 %reduce-scatter.5.cloned.1.call-start = ((), (), s32[]{:S(2)}) async-start(), calls=%async_computation.7 | async-start | bytes 3932160 | tf_op jit(solution)/shard_map/reduce_scatter | solution.py:1292
  611.7 12.1 %copy-start.45 = (bf16[16,320,128]{2,1,0:T(8,128)(2,1)S(1)}, bf16[16,320,128]{2,1,0:T(8,128)(2,1)}, u32[]{:S(2)}) copy-start(bf16[16,320,128]{2,1,0:T(8,128)(2,1)} %get-tuple-element.49) | copy-start | bytes 3932164
  633.8 7.7 copy-start.23
  637.3 4.3 copy-start.1
  647.0 6.4 copy-start.20
  647.2 2.2 copy-start.15
  657.0 127.3 %copy-start.34 = (bf16[2048,256]{0,1:T(8,128)(2,1)S(1)}, bf16[2048,256]{0,1:T(8,128)(2,1)}, u32[]{:S(2)}) copy-start(bf16[2048,256]{0,1:T(8,128)(2,1)} %convolution_convert_fusion.4) | copy-start | bytes 3145732
  785.6 168.5 %all-to-all-start.1 = ((bf16[16,128,264]{1,2,0:T(8,128)(2,1)}), bf16[16,128,264]{1,2,0:T(8,128)(2,1)}, u32[]{:S(2)}, u32[]{:S(2)}) async-start(bf16[16,128,264]{1,2,0:T(8,128)(2,1)} %pad_maximum_fusion), calls=%async_computation.3 | async-start | bytes 2162688 | tf_op jit(solution)/shard_map/all_to_all | solution.py:1257
  792.5 207.4 %all-gather.4.cloned.1.call-start = ((), (), s32[]{:S(2)}) async-start(), calls=%async_computation.5 | async-start | bytes 1966080 | tf_op jit(solution)/shard_map/all_gather | solution.py:1246
  792.6 13.3 %copy-start.43 = (bf16[16,160,704]{2,1,0:T(8,128)(2,1)S(1)}, bf16[16,160,704]{2,1,0:T(8,128)(2,1)}, u32[]{:S(2)}) copy-start(bf16[16,160,704]{2,1,0:T(8,128)(2,1)} %get-tuple-element.53) | copy-start | bytes 10813444
  805.9 12.0 %copy-start.3 = (bf16[320,2048]{1,0:T(8,128)(2,1)S(1)}, bf16[320,2048]{1,0:T(8,128)(2,1)}, u32[]{:S(2)}) copy-start(bf16[320,2048]{1,0:T(8,128)(2,1)} %param.16) | copy-start | bytes 3932164
  822.9 177.1 %all-gather.8.cloned.1.call-start = ((), (), s32[]{:S(2)}) async-start(), calls=%async_computation.8 | async-start | bytes 1966080 | tf_op jit(solution)/shard_map/all_gather | solution.py:1295
  822.9 13.4 %copy-start.27 = (bf16[8,40,8,128]{3,2,1,0:T(8,128)(2,1)S(1)}, bf16[8,40,8,128]{3,2,1,0:T(8,128)(2,1)}, u32[]{:S(2)}) copy-start(bf16[8,40,8,128]{3,2,1,0:T(8,128)(2,1)} %copy-done.26) | copy-start | bytes 1966084
  822.9 13.4 %copy-start.39 = (f32[320]{0:T(512)S(1)}, f32[320]{0:T(512)}, u32[]{:S(2)}) copy-start(f32[320]{0:T(512)} %copy-done.38) | copy-start | bytes 3844
  836.4 4.5 copy-start.25
  840.8 4.5 copy-start.21
  845.3 4.5 copy-start.44
  845.3 4.5 copy-start.47
  999.9 2.7 copy-start.19
  999.9 3.7 copy-start.33
  1002.6 2.7 copy-start.31
  1003.7 2.4 copy-start.30
  (23 other events, 35.9 us)
Sparse Core Ops, SparseCore 0:
  273.7 38.0 reduce-scatter.2
  611.8 25.4 all-gather.5
  657.0 65.7 reduce-scatter.4
  823.0 26.4 all-gather.3
  851.4 24.9 all-gather.7

commit v2 on v1

--- a/solution.py
+++ b/solution.py
@@ -616,7 +616,7 @@
     any_ = pl.BlockSpec(memory_space=pl.ANY)
     outs = pl.pallas_call(functools.partial(start_kernel, n),
         out_shape=[jax.ShapeDtypeStruct((16,) + a.shape, a.dtype) for a in arrays] + [jax.ShapeDtypeStruct((32,) + rows.shape, rows.dtype)],
-        in_specs=[any_] * (n + 1), out_specs=[any_] * (n + 1),
+        in_specs=[pl.BlockSpec(memory_space=pltpu.VMEM)] * (n + 1), out_specs=[any_] * (n + 1),
         scratch_shapes=[D((n, 4, 2)), D((n, 4)), D((n, 4)), D((n, 4)), D((n, 8)), D((n, 8)), D((n,)),
             D((4, 2)), D((4,)), D((4,)), D((4,)), D((4, 2)), D((4, 2)), D((8, 2)), D((8, 2)), D],
         compiler_params=pltpu.CompilerParams(collective_id=cid, has_side_effects=True), name=name)(*arrays, rows)
@@ -1089,7 +1089,7 @@
             S((16, 2 * rows, 128), bf16), S((16, 2 * rows, 256), bf16),
             S((32, rows, width), bf16), S((32, rows, width), bf16),
         ],
-        in_specs=[any_, any_, any_, vm, vm, vm] + [any_] * 5,
+        in_specs=[vm, any_, any_, vm, vm, vm] + [any_] * 5,
         out_specs=[vm] + [any_] * 9,
         scratch_shapes=[
             V(*wg.shape), V(*wu.shape), V(*wd.shape), V(*sgu.shape), V(256, width),
@@ -1107,6 +1107,363 @@
         compiler_params=pltpu.CompilerParams(collective_id=cid, has_side_effects=True, vmem_limit_bytes=62 << 20),
         name="expert_layer",
     )(act, deh, dhs, rank_row, rank_col, gate, wg, wu, wd, sgu, sdt)
+
+
+def norm_back(values, gain, grad):
+    width = values.shape[1]
+    inv = lax.rsqrt(jnp.sum(values * values, axis=1, keepdims=True) * (1.0 / width) + EPS)
+    scaled = grad * gain
+    inner = jnp.sum(values * scaled, axis=1, keepdims=True) * (1.0 / width)
+    normed = values * inv
+    return inv * (scaled - normed * (inv * inner)), grad * normed
+
+def attention_back_kernel(
+    part, grad2, x_mid, dy, x_in, gain1, gain2, wq_h, wk_h, wv_h, wo_h, qr, kr, vr, cosine, sine,
+    out_full, tok_full, dattn, dq, dk, dv, g1, g2,
+    ic, tmp, iy0, ix0, ix1, iy1, izu, izd, wa, wb, wc, dmix, dx2, da1, send1, recv1,
+    wsem, ysem, ls, rcs, rcr, ry0s, ry0r, rx0s, rx0r, rx1s, rx1r, ry1s, ry1r, zus, zur, zds, zdr,
+):
+    f32, bf16 = jnp.float32, jnp.bfloat16
+    z, x, y, c = place()
+    rows, width = x_mid.shape
+    h = rows // 2
+    toks = 2 * rows
+    heads = qr.shape[1] // HD
+    lo, hi = pl.ds(0, h), pl.ds(h, h)
+    xn, yn, cn = dev(z, 1 - x, y, c), dev(z, x, 1 - y, c), dev(z, x, y, 1 - c)
+    greet(z, x, y, c)
+
+    def at(s, xx, yy): return (s * 2 + xx) * 2 + yy
+    def load(s, xx, yy):
+        return pltpu.make_async_copy(part.at[blk(s, xx, yy, c)], tmp.at[xx * 2 + yy], ls.at[xx * 2 + yy])
+    def cross(s, xx, yy):
+        i = at(s, xx, yy)
+        return rcopy(part.at[blk(s, xx, yy, 1 - c)], ic.at[i], rcs.at[i], rcr.at[i], cn)
+    def ry0(s, xx):
+        return rcopy(ic.at[at(s, xx, 1 - y), lo], iy0.at[s * 2 + xx], ry0s.at[s, xx], ry0r.at[s, xx], yn)
+    def rx1(s, yy):
+        return rcopy(ic.at[at(s, 1 - x, yy), hi], ix1.at[s * 2 + yy], rx1s.at[s, yy], rx1r.at[s, yy], xn)
+    def rx0(s):
+        return rcopy(ic.at[at(s, 1 - x, y), lo], ix0.at[s], rx0s.at[s], rx0r.at[s], xn)
+    def ry1(s):
+        return rcopy(ic.at[at(s, x, 1 - y), hi], iy1.at[s], ry1s.at[s], ry1r.at[s], yn)
+    def zu(s):
+        return rcopy(ic.at[at(s, x, y)], izu.at[s], zus.at[s], zur.at[s], dev(z + 1, x, y, c))
+    def zd(s):
+        return rcopy(ic.at[at(s, x, y)], izd.at[s], zds.at[s], zdr.at[s], dev(z - 1, x, y, c))
+    def add(i, start, count, src, j):
+        @pl.loop(0, count // 16)
+        def _(r):
+            a = pl.ds(pl.multiple_of(start + r * 16, 16), 16)
+            b = pl.ds(pl.multiple_of(r * 16, 16), 16)
+            ic[i, a] = ic[i, a] + src[j, b]
+
+    four = [(xx, yy) for xx in (0, 1) for yy in (0, 1)]
+
+    def first(g):
+        s = nearest(z, g)
+        for xx, yy in four:
+            load(s, xx, yy).wait(); cross(s, xx, yy).wait_recv()
+            add(at(s, xx, yy), 0, rows, tmp, xx * 2 + yy)
+            @pl.when(yy != y)
+            def _(): ry0(s, xx).start()
+            @pl.when(xx != x)
+            def _(): rx1(s, yy).start()
+        if g > 0:
+            for xx, yy in four:
+                load(nearest(z, g - 1), xx, yy).start()
+
+    def second(g):
+        s = nearest(z, g)
+        ry0(s, 1 - x).wait_recv(); add(at(s, 1 - x, y), 0, h, iy0, s * 2 + 1 - x); rx0(s).start()
+        rx1(s, 1 - y).wait_recv(); add(at(s, x, 1 - y), h, h, ix1, s * 2 + 1 - y); ry1(s).start()
+        ry0(s, x).wait_recv(); add(at(s, x, y), 0, h, iy0, s * 2 + x)
+        rx1(s, y).wait_recv(); add(at(s, x, y), h, h, ix1, s * 2 + y)
+
+    def third(g):
+        s = nearest(z, g)
+        me = at(s, x, y)
+        rx0(s).wait_recv(); add(me, 0, h, ix0, s)
+        ry1(s).wait_recv(); add(me, h, h, iy1, s)
+        @pl.when((s >= z) & (z > 0))
+        def _():
+            zu(s).wait_recv(); add(me, 0, rows, izu, s)
+        @pl.when((s <= z) & (z < 3))
+        def _():
+            zd(s).wait_recv(); add(me, 0, rows, izd, s)
+        @pl.when(s > z)
+        def _(): zu(s).start()
+        @pl.when(s < z)
+        def _(): zd(s).start()
+
+    for g in (3, 2, 1, 0):
+        s = nearest(z, g)
+        for xx, yy in four:
+            cross(s, xx, yy).start()
+            if g == 3:
+                load(s, xx, yy).start()
+    w_out = pltpu.make_async_copy(wo_h, wa, wsem.at[0])
+    w_query = pltpu.make_async_copy(wq_h, wb, wsem.at[1])
+    w_key = pltpu.make_async_copy(wk_h, wc, wsem.at[2])
+    w_value = pltpu.make_async_copy(wv_h, wa, wsem.at[3])
+    w_out.start(); w_query.start(); w_key.start()
+
+    g1[...] = jnp.zeros_like(g1)
+    g2[...] = jnp.zeros_like(g2)
+    @pl.loop(0, rows // 16)
+    def _(r):
+        q = pl.ds(pl.multiple_of(r * 16, 16), 16)
+        back, terms = norm_back(x_mid[q], gain2[...], grad2[q].astype(f32))
+        back = back + dy[q].astype(f32)
+        dx2[q] = back
+        dattn[y, q] = back.astype(bf16)
+        g2[...] += jnp.sum(terms, axis=0, keepdims=True)
+    attn_swap = rcopy(dattn.at[y], dattn.at[y], ysem.at[0], ysem.at[1], yn)
+    attn_swap.start()
+    first(3)
+    first(2)
+    w_out.wait()
+    attn_swap.wait_recv()
+    full = dattn[...].reshape(toks, width)
+    dmix[...] = nn(full, wa[...]).astype(bf16)
+    w_value.start()
+
+    scale = HD ** (-0.5)
+    def turn_back(values):
+        return values * cosine[...] - pltpu.roll(values, HD // 2, 1) * sine[...]
+    @pl.loop(0, heads)
+    def _(n):
+        @pl.when(n == 2)
+        def _():
+            second(3); first(1)
+        @pl.when(n == 5)
+        def _():
+            second(2); third(3); first(0)
+        w = pl.ds(pl.multiple_of(n * HD, HD), HD)
+        qh, kh, vh, doh = qr[:, w], kr[:, w], vr[:, w], dmix[:, w]
+        scores = nt(qh, kh) * scale
+        ahead = lax.broadcasted_iota(jnp.int32, (toks, toks), 0) >= lax.broadcasted_iota(jnp.int32, (toks, toks), 1)
+        scores = jnp.where(ahead, scores, -1e30)
+        expo = jnp.exp(scores - jnp.max(scores, axis=1, keepdims=True))
+        probs = expo * (1.0 / jnp.sum(expo, axis=1, keepdims=True))
+        dv[:, w] = lax.dot_general(
+            probs.astype(bf16), doh, (((0,), (0,)), ((), ())), preferred_element_type=f32
+        ).astype(bf16)
+        dprob = nt(doh, vh)
+        delta = jnp.sum(probs * dprob, axis=1, keepdims=True)
+        ds = (probs * (dprob - delta)).astype(bf16)
+        dq[:, w] = turn_back(nn(ds, kh) * scale).astype(bf16)
+        dkr = lax.dot_general(ds, qh, (((0,), (0,)), ((), ())), preferred_element_type=f32)
+        dk[:, w] = turn_back(dkr * scale).astype(bf16)
+
+    w_query.wait(); w_key.wait(); w_value.wait()
+    for n in range(0, width, 512):
+        w = pl.ds(n, 512)
+        out = nt(dq[...], wb[w, :]) + nt(dk[...], wc[w, :]) + nt(dv[...], wa[w, :])
+        da1[0, :, w] = out[:rows]
+        da1[1, :, w] = out[rows:]
+    @pl.loop(0, rows // 16)
+    def _(r):
+        q = pl.ds(pl.multiple_of(r * 16, 16), 16)
+        send1[q] = da1[1 - y, q].astype(bf16)
+    da1_swap = rcopy(send1, recv1, ysem.at[2], ysem.at[3], yn)
+    da1_swap.start()
+    second(1); third(2)
+    da1_swap.wait_recv()
+    @pl.loop(0, rows // 16)
+    def _(r):
+        q = pl.ds(pl.multiple_of(r * 16, 16), 16)
+        back, terms = norm_back(x_in[q].astype(f32), gain1[...], da1[y, q] + recv1[q].astype(f32))
+        tok_full[y, q] = (back + dx2[q]).astype(bf16)
+        g1[...] += jnp.sum(terms, axis=0, keepdims=True)
+    tok_swap = rcopy(tok_full.at[y], tok_full.at[y], ysem.at[4], ysem.at[5], yn)
+    tok_swap.start()
+    second(0); third(1); third(0)
+    @pl.loop(0, rows // 16)
+    def _(r):
+        q = pl.ds(pl.multiple_of(r * 16, 16), 16)
+        out_full[y, q] = (x_mid[q] + ic[at(z, x, y), q].astype(f32)).astype(bf16)
+    out_swap = rcopy(out_full.at[y], out_full.at[y], ysem.at[6], ysem.at[7], yn)
+    out_swap.start()
+    tok_swap.wait_recv()
+    out_swap.wait_recv()
+    for swap in (attn_swap, da1_swap, tok_swap, out_swap):
+        swap.wait_send()
+    for s in range(4):
+        rx0(s).wait_send(); ry1(s).wait_send()
+        for q in (0, 1):
+            ry0(s, q).wait_send(); rx1(s, q).wait_send()
+            for r in (0, 1):
+                cross(s, q, r).wait_send()
+        @pl.when(s > z)
+        def _(): zu(s).wait_send()
+        @pl.when(s < z)
+        def _(): zd(s).wait_send()
+
+def attention_back(part, grad2, x_mid, dy, x_in, gain1, gain2, weights, qr, kr, vr, cosine, sine, cid):
+    rows, width = x_mid.shape
+    toks, hw = qr.shape
+    h = rows // 2
+    f32, bf16 = jnp.float32, jnp.bfloat16
+    D = pltpu.SemaphoreType.DMA
+    S = jax.ShapeDtypeStruct
+    any_ = pl.BlockSpec(memory_space=pl.ANY)
+    vm = pl.BlockSpec(memory_space=pltpu.VMEM)
+    V = lambda *shape, t=bf16: pltpu.VMEM(shape, t)
+    return pl.pallas_call(
+        attention_back_kernel,
+        out_shape=[
+            S((2, rows, width), bf16), S((2, rows, width), bf16), S((2, rows, width), bf16),
+            S((toks, hw), bf16), S((toks, hw), bf16), S((toks, hw), bf16), S((1, width), f32), S((1, width), f32),
+        ],
+        in_specs=[any_] + [vm] * 6 + [any_] * 4 + [vm] * 5,
+        out_specs=[vm] * 8,
+        scratch_shapes=[
+            V(16, rows, width), V(4, rows, width), V(8, h, width), V(4, h, width), V(8, h, width), V(4, h, width),
+            V(4, rows, width), V(4, rows, width),
+            V(width, hw), V(width, hw), V(width, hw), V(toks, hw), V(rows, width, t=f32), V(2, rows, width, t=f32),
+            V(rows, width), V(rows, width),
+            D((4,)), D((8,)), D((4,)), D((16,)), D((16,)), D((4, 2)), D((4, 2)), D((4,)), D((4,)), D((4, 2)), D((4, 2)), D((4,)), D((4,)),
+            D((4,)), D((4,)), D((4,)), D((4,)),
+        ],
+        compiler_params=pltpu.CompilerParams(collective_id=cid, has_side_effects=True, vmem_limit_bytes=63 << 20),
+        name="attention_back",
+    )(part, grad2, x_mid, dy, x_in, gain1, gain2, *weights, qr, kr, vr, cosine, sine)
+
+def weight_grad_kernel(
+    a1, dattn, dq, dk, dv, mixed, gains,
+    oq, ok, ov, oo, og,
+    acc, ic, ix, izu, izd, gc, gx, gu, gd, gy, gbuf,
+    cs, cr, xs, xr, zus, zur, zds, zdr, gss, gsr,
+):
+    f32, bf16 = jnp.float32, jnp.bfloat16
+    z, x, y, c = place()
+    xn, yn, cn = dev(z, 1 - x, y, c), dev(z, x, 1 - y, c), dev(z, x, y, 1 - c)
+    n, depth = 4, acc.shape[2]
+    outs = (oq, ok, ov, oo)
+    greet(z, x, y, c)
+    def pos(s, xx, cc): return (s * 2 + xx) * 2 + cc
+    def wc(a, s, xx):
+        i = s * 2 + xx
+        return rcopy(acc.at[a, pos(s, xx, 1 - c)], ic.at[a, i], cs.at[a, i], cr.at[a, i], cn)
+    def wx(a, s):
+        return rcopy(acc.at[a, pos(s, 1 - x, c)], ix.at[a, s], xs.at[a, s], xr.at[a, s], xn)
+    def zu(a, s):
+        return rcopy(acc.at[a, pos(s, x, c)], izu.at[a, s], zus.at[a, s], zur.at[a, s], dev(z + 1, x, y, c))
+    def zd(a, s):
+        return rcopy(acc.at[a, pos(s, x, c)], izd.at[a, s], zds.at[a, s], zdr.at[a, s], dev(z - 1, x, y, c))
+    def add(a, i, src, j):
+        @pl.loop(0, depth // 16)
+        def _(r):
+            b = pl.ds(pl.multiple_of(r * 16, 16), 16)
+            acc[a, i, b] = acc[a, i, b] + src[a, j, b]
+    def make(g):
+        s = nearest(z, g)
+        w = pl.ds(pl.multiple_of(s * 4 * depth, 4 * depth), 4 * depth)
+        for a, (left, right) in ((3, (dattn, mixed)), (0, (a1, dq)), (1, (a1, dk)), (2, (a1, dv))):
+            out = lax.dot_general(left[:, w], right[...], (((0,), (0,)), ((), ())), preferred_element_type=f32).astype(bf16)
+            for i in range(4):
+                acc[a, s * 4 + i] = out[i * depth:(i + 1) * depth]
+            for q in (0, 1):
+                wc(a, s, q).start()
+    def first(g):
+        s = nearest(z, g)
+        for a in (3, 0, 1, 2):
+            for q in (0, 1):
+                wc(a, s, q).wait_recv()
+                add(a, pos(s, q, c), ic, s * 2 + q)
+            wx(a, s).start()
+    def second(g):
+        s = nearest(z, g)
+        for a in (3, 0, 1, 2):
+            wx(a, s).wait_recv(); add(a, pos(s, x, c), ix, s)
+            @pl.when((s >= z) & (z > 0))
+            def _():
+                zu(a, s).wait_recv(); add(a, pos(s, x, c), izu, s)
+            @pl.when((s <= z) & (z < 3))
+            def _():
+                zd(a, s).wait_recv(); add(a, pos(s, x, c), izd, s)
+            @pl.when(s > z)
+            def _(): zu(a, s).start()
+            @pl.when(s < z)
+            def _(): zd(a, s).start()
+    g_c = rcopy(gains.at[1 - c], gc, gss.at[0], gsr.at[0], cn)
+    g_x = rcopy(gbuf.at[1 - x], gx, gss.at[1], gsr.at[1], xn)
+    g_u = rcopy(gu.at[1], gu.at[0], gss.at[2], gsr.at[2], dev(z + 1, x, y, c))
+    g_d = rcopy(gd.at[1], gd.at[0], gss.at[3], gsr.at[3], dev(z - 1, x, y, c))
+    g_y = rcopy(gy.at[0], gy.at[1], gss.at[4], gsr.at[4], yn)
+    g_c.start()
+    make(3); make(2)
+    g_c.wait_recv()
+    gbuf[...] = gains[c] + gc[...]
+    g_x.start()
+    first(3); make(1); first(2); make(0)
+    g_x.wait_recv()
+    gbuf[x] = gbuf[x] + gx[...]
+    second(3)
+    gu[1] = gbuf[x]
+    gd[1] = gbuf[x]
+    @pl.when(z > 0)
+    def _():
+        g_u.wait_recv()
+        gu[1] = gu[1] + gu[0]
+    @pl.when(z < 3)
+    def _():
+        g_u.start()
+    first(1)
+    second(2)
+    @pl.when(z < 3)
+    def _():
+        g_d.wait_recv()
+        gd[1] = gd[1] + gd[0]
+    @pl.when(z > 0)
+    def _():
+        g_d.start()
+    first(0)
+    second(1)
+    gy[0] = gu[1, z] + gd[1, z] - gbuf[x, z]
+    g_y.start()
+    second(0)
+    for a in range(n):
+        outs[a][...] = acc[a, pos(z, x, c)].astype(f32)
+    g_y.wait_recv()
+    og[...] = gy[0] + gy[1]
+    g_c.wait_send(); g_x.wait_send(); g_y.wait_send()
+    @pl.when(z < 3)
+    def _(): g_u.wait_send()
+    @pl.when(z > 0)
+    def _(): g_d.wait_send()
+    for s in range(4):
+        for a in range(n):
+            for q in (0, 1): wc(a, s, q).wait_send()
+            wx(a, s).wait_send()
+            @pl.when(s > z)
+            def _(): zu(a, s).wait_send()
+            @pl.when(s < z)
+            def _(): zd(a, s).wait_send()
+
+def weight_grads(a1, dattn, dq, dk, dv, mixed, gains, cid):
+    toks, width = a1.shape
+    hw = dq.shape[1]
+    depth = width // 16
+    f32, bf16 = jnp.float32, jnp.bfloat16
+    D = pltpu.SemaphoreType.DMA
+    S = jax.ShapeDtypeStruct
+    vm = pl.BlockSpec(memory_space=pltpu.VMEM)
+    V = lambda *shape, t=bf16: pltpu.VMEM(shape, t)
+    return pl.pallas_call(
+        weight_grad_kernel,
+        out_shape=[S((depth, hw), f32)] * 4 + [S((8, 128), f32)],
+        in_specs=[vm] * 7,
+        out_specs=[vm] * 5,
+        scratch_shapes=[
+            V(4, 16, depth, hw), V(4, 8, depth, hw), V(4, 4, depth, hw), V(4, 4, depth, hw), V(4, 4, depth, hw),
+            V(2, 4, 8, 128, t=f32), V(4, 8, 128, t=f32), V(2, 4, 8, 128, t=f32), V(2, 4, 8, 128, t=f32), V(2, 8, 128, t=f32), V(2, 4, 8, 128, t=f32),
+            D((4, 8)), D((4, 8)), D((4, 4)), D((4, 4)), D((4, 4)), D((4, 4)), D((4, 4)), D((4, 4)), D((5,)), D((5,)),
+        ],
+        compiler_params=pltpu.CompilerParams(collective_id=cid, has_side_effects=True, vmem_limit_bytes=60 << 20),
+        name="weight_grads",
+    )(a1, dattn, dq, dk, dv, mixed, gains)
 
 
 def routing_tables(gate_table, capacity):
@@ -1194,7 +1551,6 @@
     expo = jnp.exp(scores - top)
     total = jnp.sum(expo, axis=-1, keepdims=True)
     probs = expo / total
-    log_total = top + jnp.log(total)
     mixed = jnp.einsum("hqk,khc->qhc", probs.astype(bf16), value_low, preferred_element_type=f32)
     mixed = mixed.reshape(rows_dev, heads_dev * HD).astype(bf16)
     attn = lax.psum_scatter(
@@ -1236,15 +1592,11 @@
             1,
         )
     )
-    act_two_total = total_grad.astype(f32)
     act_all = act_all.reshape(-1, width)
     rows = rows.reshape(slots, width)
     hidden_rows = hidden_rows.reshape(slots, -1)
     common_hidden = common_hidden.reshape(-1, 128)
     common_gu_grad = common_gu_grad.reshape(-1, 256)
-    ffn = scatter_rows(ffn.reshape(-1, width), 3, "sum_ffn").astype(f32)
-    layer_out = lax.all_gather((x_mid + ffn).astype(bf16), "tensor", axis=0, tiled=True)
-
     expert_gate_grad = contract_first(rows, gate_rows_grad.reshape(slots, -1))[None]
     expert_up_grad = contract_first(rows, up_rows_grad.reshape(slots, -1))[None]
     expert_down_grad = contract_first(hidden_rows, rows_out_grad)[None]
@@ -1258,59 +1610,34 @@
     common_w_grad = common_w_grad.astype(f32).reshape(experts, depth, 3, common_dev)
     common_w_grad = common_w_grad.transpose(2, 1, 0, 3).reshape(3, depth, common_width)
 
-    dummy_second, second_vjp = jax.vjp(rms_norm, x_mid, gain_two)
-    mid_norm_grad, gain_two_grad = second_vjp(act_two_total)
-    mid_grad = grad_half.astype(f32) + mid_norm_grad
-    attn_grad = lax.all_gather(mid_grad.astype(bf16), "tensor", axis=0, tiled=True)
-
-    mixed_grad = (
-        jnp.dot(attn_grad, output_whole, preferred_element_type=f32)
-        .astype(bf16)
-        .reshape(rows_dev, heads_dev, HD)
-    )
-    probs_again = jnp.exp(masked_scores(query_rot, key_rot, causal, scale) - log_total)
-    value_grad = jnp.einsum(
-        "hqk,qhc->khc", probs_again.astype(bf16), mixed_grad, preferred_element_type=f32
-    ).astype(bf16)
-    prob_grad = jnp.einsum("qhc,khc->hqk", mixed_grad, value_low, preferred_element_type=f32)
-    delta = jnp.sum(probs_again * prob_grad, axis=-1, keepdims=True)
-    score_grad = (probs_again * (prob_grad - delta)).astype(bf16)
-    query_rot_grad = (
-        jnp.einsum("hqk,khc->qhc", score_grad, key_rot, preferred_element_type=f32) * scale
-    )
-    key_rot_grad = (
-        jnp.einsum("hqk,qhc->khc", score_grad, query_rot, preferred_element_type=f32) * scale
-    )
-    query_grad = rotate(query_rot_grad, -positions).reshape(rows_dev, heads_dev * HD).astype(bf16)
-    key_grad = rotate(key_rot_grad, -positions).reshape(rows_dev, heads_dev * HD).astype(bf16)
-    value_flat = value_grad.reshape(rows_dev, heads_dev * HD)
-    act_one_grad = (
-        contract_last(query_grad, query_whole)
-        + contract_last(key_grad, key_whole)
-        + contract_last(value_flat, value_whole)
-    )
-    act_one_total = lax.psum_scatter(act_one_grad, "tensor", scatter_dimension=0, tiled=True)
-    dummy_first, first_vjp = jax.vjp(rms_norm, x_half, gain_one)
-    in_norm_grad, gain_one_grad = first_vjp(act_one_total)
-    tokens_grad = lax.all_gather((mid_grad + in_norm_grad).astype(bf16), "tensor", axis=0, tiled=True)
-
-    query_sum, key_sum, value_sum, output_sum = weight_sums(
-        [
-            contract_first(act_one, query_grad).astype(bf16),
-            contract_first(act_one, key_grad).astype(bf16),
-            contract_first(act_one, value_flat).astype(bf16),
-            contract_first(attn_grad, mixed).astype(bf16),
-        ],
-        4,
-        "sum_weight_grads",
-    )
-    gain_grads = lax.psum(jnp.stack([gain_one_grad, gain_two_grad]), ("dp", "tensor"))
-    gain_grads = lax.dynamic_slice_in_dim(
-        gain_grads, lax.axis_index("dp") * gain_first.shape[0], gain_first.shape[0], axis=1
+    freqs = 10000.0 ** (-2.0 * jnp.arange(HD // 2, dtype=f32) / HD)
+    angles = positions[:, None] * freqs[None, :]
+    cosine = jnp.concatenate([jnp.cos(angles)] * 2, axis=1)
+    sine = jnp.concatenate([-jnp.sin(angles), jnp.sin(angles)], axis=1)
+    layer_out, tokens_grad, attn_grad, query_grad, key_grad, value_grad, gain_one_grad, gain_two_grad = attention_back(
+        ffn,
+        total_grad,
+        x_mid,
+        grad_half,
+        lax.dynamic_slice_in_dim(tokens, mine, half, axis=0),
+        gain_one[None],
+        gain_two[None],
+        (query_whole, key_whole, value_whole, output_whole),
+        query_rot.reshape(rows_dev, -1),
+        key_rot.reshape(rows_dev, -1),
+        value_low.reshape(rows_dev, -1),
+        cosine,
+        sine,
+        2,
+    )
+    gains = jnp.concatenate([gain_one_grad, gain_two_grad, jnp.zeros((6, width), f32)])
+    gains = gains.reshape(8, 4, 2, 2, width // 16).transpose(3, 2, 1, 0, 4)
+    query_sum, key_sum, value_sum, output_sum, gain_grads = weight_grads(
+        act_one, attn_grad.reshape(rows_dev, width), query_grad, key_grad, value_grad, mixed, gains, 4
     )
     return (
-        layer_out,
-        tokens_grad,
+        layer_out.reshape(rows_dev, width),
+        tokens_grad.reshape(rows_dev, width),
         gain_grads[0],
         query_sum,
         key_sum,

time: 1020 us -> 910 us (0.89)
  blocking collectives: 40.4 us -> 0 us
  Pallas kernels: 720 us -> 688 us
  matrix products: 143 us -> 117 us
    pallas_call x1, Pallas kernels: 228 us -> 182 us  [start_gather(): pl.pallas_call(functools.partial(start_kernel, n), out_shape=[jax.ShapeDt...]
    psum x1 -> x0, blocking collectives: 40.4 us -> none  [on_device(): lax.psum(jnp.stack([gain_one_grad, gain_two_grad]), ('dp', 'tensor'))]
    pallas_call x2, Pallas kernels: 227 us -> 259 us  [the longest x1 154 us: attention_back(): pl.pallas_call(attention_back_kernel, out_shape=[S((2, rows, width), bf16...]
    dot_general x9 -> x5, matrix products: 78.6 us -> 58.7 us  [contract_first(): lax.dot_general(left, right, (((0,), (0,)), ((), ())), preferred_element_...]
    pallas_call x1, Pallas kernels: 266 us -> 247 us  [expert_layer(): pl.pallas_call(expert_kernel, out_shape=[S((rows, width), bf16), S((32, r...]
    dot_general x5 -> x2, matrix products: 23.6 us -> 17 us  [contract_last(): lax.dot_general(left, right, (((1,), (1,)), ((), ())), preferred_element_...]
    unnamed x114 -> x58, local copies, waits for them, and re-layouts: 27.3 us -> 25.2 us
  transfers between devices with their start and end apart: 7 -> 3, of which waited for: 1 -> 0; matrix products, arithmetic and copies ran while one was open for 15% -> 15% of each run, Pallas kernels for 22% -> 49%
where the time goes in v2:
time: 910 us; the launch traced here: 905 us
  Pallas kernels  688 us (76%)
  matrix products  117 us (13%)
  local copies, waits for them, and re-layouts  52.7 us (6%)
  other arithmetic  17.7 us (2%)
  between operations  14.7 us (2%)
  starting transfers between devices  13.7 us (2%)
    pallas_call x1, Pallas kernels, expert_layer(): pl.pallas_call(expert_kernel, out_shape=[S((rows, width), bf16), S((32, r...  247 us
    pallas_call x1, Pallas kernels, start_gather(): pl.pallas_call(functools.partial(start_kernel, n), out_shape=[jax.ShapeDt...  182 us
    pallas_call x1, Pallas kernels, attention_back(): pl.pallas_call(attention_back_kernel, out_shape=[S((2, rows, width), bf16...  154 us
    pallas_call x1, Pallas kernels, weight_grads(): pl.pallas_call(weight_grad_kernel, out_shape=[S((depth, hw), f32)] * 4 +...  105 us
    dot_general x5, matrix products, contract_first(): lax.dot_general(left, right, (((0,), (0,)), ((), ())), preferred_element_...  58.7 us
    unnamed x58, local copies, waits for them, and re-layouts  25.2 us
  transfers between devices with their start and end apart: 3, of which 0 were waited for; matrix products, arithmetic and copies ran while one was open for 15% of the time, Pallas kernels for 49%

profile of v2, /device:TPU:0, one launch (start us, length us, event | category | flops | bytes accessed | tf_op | source)
XLA Modules:
  0.0 904.6 jit_solution(13896647744715796262)
XLA Ops:
  12.1 7.5 all-to-all-start
  23.0 182.2 %gather_weights.1 = (bf16[16,128,1024]{2,1,0:T(8,128)(2,1)}, bf16[16,128,1024]{2,1,0:T(8,128)(2,1)}, bf16[16,128,1024]{2,1,0:T(8,128)(2,1)}, bf16[16,128,1024]{2...) custom-call(bf16[128,1024]{1,0:T(8,128)(2,1)} %refs_0_.1, ...), custom_call_target="tpu_custom_call" | custom-call | tf_op jit(solution)/shard_map/gather_weights/pallas_call | solution.py:617
  205.2 1.5 fusion.37
  206.6 6.4 copy.167
  213.5 5.1 fusion.42.vr
  218.6 1.6 fusion.18
  220.1 6.4 copy.166
  226.6 3.7 fusion.20
  232.0 3.4 fusion.41
  235.4 3.3 fusion.22
  239.5 3.0 fusion.38
  245.7 13.4 %multiply_convert_fusion = bf16[16,160,2048]{2,1,0:T(8,128)(2,1)} fusion(f32[16,160]{1,0:T(8,128)S(1)} %select_reduce_fusion, bf16[16,320,2048]{2,1,0:T(8,128)(2,1)} %bitcast.168, s32[16,320]{1,0:T(8,128)S(1)} %get-tuple-element.152, pred[16,320]{1,0:T(8,128)(4,1)S(1)} %bitcast.206), kind=kOutput, calls=%fused_computation.1 | convolution fusion | flops 3367567360 | bytes 31493120 | tf_op jit(solution)/shard_map/jst,jtd->jsd/dot_general | solution.py:1566
  262.1 4.6 copy.149
  266.7 4.6 copy.150
  271.9 1.5 copy.154.gate
  273.5 2.3 copy.153.rank_col
  276.8 13.9 %fusion.4.deh = f32[16,160,704]{2,1,0:T(8,128)} fusion(bf16[16,160,2048]{2,1,0:T(8,128)(2,1)} %multiply_convert_fusion, bf16[1,704,2048]{2,1,0:T(8,128)(2,1)} %param.31), kind=kOutput, calls=%fused_computation.14 | convolution fusion | flops 7381975040 | bytes 20578304 | tf_op jit(solution)/shard_map/dot_general | solution.py:41
  290.7 1.3 fusion.40
  293.5 1.4 fusion.23.sgu_h
  295.0 11.3 %fusion.26.dhs = f32[16,320,128]{2,1,0:T(8,128)} fusion(bf16[16,320,2048]{2,1,0:T(8,128)(2,1)} %bitcast.169, bf16[2048,88]{0,1:T(8,128)(2,1)S(1)} %bitcast.191), kind=kOutput, calls=%fused_computation.58 | convolution fusion | flops 2684354560 | bytes 23953408 | tf_op jit(solution)/shard_map/dot_general | solution.py:1577
  306.3 2.3 multiply_reduce_fusion
  310.7 247.2 %expert_layer.1 = (bf16[160,2048]{1,0:T(8,128)(2,1)}, bf16[32,160,2048]{2,1,0:T(8,128)(2,1)}, bf16[16,160,2048]{2,1,0:T(8,128)(2,1)}, bf16[16,160,704]{2,1,0:T(8...) custom-call(bf16[160,2048]{1,0:T(8,128)(2,1)} %multiply_convert_fusi, ...), custom_call_target="tpu_custom_call" | custom-call | tf_op jit(solution)/shard_map/expert_layer/pallas_call | solution.py:1084
  557.9 13.4 %convolution_bitcast_fusion = f32[1,704,2048]{2,1,0:T(8,128)} fusion(bf16[16,160,704]{2,1,0:T(8,128)(2,1)} %get-tuple-element.71, bf16[16,160,2048]{2,1,0:T(8,128)(2,1)} %multiply_convert_fusion), kind=kOutput, calls=%fused_computation.8 | convolution fusion | flops 7381975040 | bytes 19857408 | tf_op jit(solution)/shard_map/dot_general | solution.py:47
  571.4 10.1 %fusion.43 = bf16[2048,128]{0,1:T(8,128)(2,1)S(1)} fusion(bf16[5120,2048]{1,0:T(8,128)(2,1)} %bitcast.170, bf16[5120,128]{1,0:T(8,128)(2,1)S(1)} %bitcast.216), kind=kOutput, calls=%fused_computation.110 | convolution fusion | flops 2684354560 | bytes 22806528 | tf_op jit(solution)/shard_map/dot_general | solution.py:47
  581.6 10.1 %convolution_convert_fusion = bf16[2048,256]{0,1:T(8,128)(2,1)S(1)} fusion(bf16[5120,2048]{1,0:T(8,128)(2,1)} %bitcast.214, bf16[5120,256]{1,0:T(8,128)(2,1)S(1)} %bitcast.215), kind=kOutput, calls=%fused_computation.19 | convolution fusion | flops 5369233408 | bytes 24641536 | tf_op jit(solution)/shard_map/dot_general | solution.py:47
  592.9 6.2 all-to-all-start.1
  599.1 13.2 %convolution_bitcast_fusion.2 = f32[1,2048,704]{1,2,0:T(8,128)} fusion(bf16[16,160,2048]{2,1,0:T(8,128)(2,1)} %get-tuple-element.68, bf16[16,160,704]{2,1,0:T(8,128)(2,1)} %get-tuple-element.69), kind=kOutput, calls=%fused_computation.10 | convolution fusion | flops 7381975040 | bytes 19857408 | tf_op jit(solution)/shard_map/dot_general | solution.py:47
  612.2 153.8 %attention_back.1 = (bf16[2,160,2048]{2,1,0:T(8,128)(2,1)}, bf16[2,160,2048]{2,1,0:T(8,128)(2,1)}, bf16[2,160,2048]{2,1,0:T(8,128)(2,1)}, bf16[320,1024]{1,0:T(8...) custom-call(bf16[32,160,2048]{2,1,0:T(8,128)(2,1)} %get-tuple-element, ...), custom_call_target="tpu_custom_call" | custom-call | tf_op jit(solution)/shard_map/attention_back/pallas_call | solution.py:1313
  767.5 105.1 %weight_grads.1 = (f32[128,1024]{1,0:T(8,128)}, f32[128,1024]{1,0:T(8,128)}, f32[128,1024]{1,0:T(8,128)}, f32[128,1024]{1,0:T(8,128)}, f32[8,128]{1,0:T(8,128)}) custom-call(bf16[320,2048]{1,0:T(8,128)(2,1)} %copy-done.2, bf16[320,2048]{1,0:T(8,128)(2,1)} %bitcast.200, bf16[320,1024]{1,0:T(8,128)(2,1)} %get-tuple-element.55.dq, ...), custom_call_target="tpu_custom_call" | custom-call | tf_op jit(solution)/shard_map/weight_grads/pallas_call | solution.py:1454
  873.9 12.0 %convolution_bitcast_fusion.1 = f32[1,2048,704]{1,2,0:T(8,128)} fusion(bf16[16,160,2048]{2,1,0:T(8,128)(2,1)} %get-tuple-element.68, bf16[16,160,704]{2,1,0:T(8,128)(2,1)S(1)} %copy-done.17), kind=kOutput, calls=%fused_computation.9 | convolution fusion | flops 7381975040 | bytes 19857408 | tf_op jit(solution)/shard_map/dot_general | solution.py:47
  885.8 1.4 convert_bitcast_fusion
  890.8 2.6 copy.215
  (106 shorter events, 34.1 us)
Async XLA Ops:
  10.9 8.8 copy-start.1
  10.9 9.9 %copy-start.13 = (f32[320,6]{0,1:T(8,128)S(1)}, f32[320,6]{0,1:T(8,128)}, u32[]{:S(2)}) copy-start(f32[320,6]{0,1:T(8,128)} %param.19) | copy-start | bytes 23044
  11.0 9.9 %copy-start.14 = (s32[320,6]{0,1:T(8,128)S(1)}, s32[320,6]{0,1:T(8,128)}, u32[]{:S(2)}) copy-start(s32[320,6]{0,1:T(8,128)} %param.18) | copy-start | bytes 23044
  12.1 9.4 %copy-start.12 = (bf16[320,2048]{1,0:T(8,128)(2,1)S(1)}, bf16[320,2048]{1,0:T(8,128)(2,1)}, u32[]{:S(2)}) copy-start(bf16[320,2048]{1,0:T(8,128)(2,1)} %param.17) | copy-start | bytes 3932164
  12.1 10.3 %copy-start.15 = (bf16[128]{0:T(256)(128)(2,1)S(1)}, bf16[128]{0:T(256)(128)(2,1)}, u32[]{:S(2)}) copy-start(bf16[128]{0:T(256)(128)(2,1)} %param.25) | copy-start | bytes 772
  12.1 10.3 %copy-start.16 = (bf16[128]{0:T(256)(128)(2,1)S(1)}, bf16[128]{0:T(256)(128)(2,1)}, u32[]{:S(2)}) copy-start(bf16[128]{0:T(256)(128)(2,1)} %param.20) | copy-start | bytes 772
  12.1 278.6 %all-to-all-start = ((bf16[16,3,128,88]{2,3,1,0:T(8,128)(2,1)}), bf16[16,3,128,88]{2,3,1,0:T(8,128)(2,1)}, u32[]{:S(2)}, u32[]{:S(2)}) async-start(bf16[16,3,128,88]{2,3,1,0:T(8,128)(2,1)} %copy.146), calls=%async_computation.1 | async-start | bytes 2162688 | tf_op jit(solution)/shard_map/all_to_all | solution.py:1527
  19.6 286.7 %reduce-scatter.2.cloned.1.call-start = ((), (), s32[]{:S(2)}) async-start(), calls=%async_computation.3 | async-start | bytes 3932160 | tf_op jit(solution)/shard_map/reduce_scatter | solution.py:1556
  213.4 5.1 copy-start.2
  213.5 5.1 copy-start.4
  235.4 4.1 copy-start.3
  238.6 0.8 copy-start.6
  259.2 1.9 copy-start.7
  308.6 1.1 copy-start
  557.9 13.4 %copy-start.19 = (bf16[16,320,128]{2,1,0:T(8,128)(2,1)S(1)}, bf16[16,320,128]{2,1,0:T(8,128)(2,1)}, u32[]{:S(2)}) copy-start(bf16[16,320,128]{2,1,0:T(8,128)(2,1)} %get-tuple-element.67) | copy-start | bytes 3932164
  571.4 10.2 %copy-start.18 = (bf16[16,320,256]{2,1,0:T(8,128)(2,1)S(1)}, bf16[16,320,256]{2,1,0:T(8,128)(2,1)}, u32[]{:S(2)}) copy-start(bf16[16,320,256]{2,1,0:T(8,128)(2,1)} %get-tuple-element.66) | copy-start | bytes 7864324
  592.9 292.9 %all-to-all-start.1 = ((bf16[16,128,264]{1,2,0:T(8,128)(2,1)}), bf16[16,128,264]{1,2,0:T(8,128)(2,1)}, u32[]{:S(2)}, u32[]{:S(2)}) async-start(bf16[16,128,264]{1,2,0:T(8,128)(2,1)} %pad_maximum_fusion), calls=%async_computation.2 | async-start | bytes 2162688 | tf_op jit(solution)/shard_map/all_to_all | solution.py:1609
  767.5 106.4 %copy-start.17 = (bf16[16,160,704]{2,1,0:T(8,128)(2,1)S(1)}, bf16[16,160,704]{2,1,0:T(8,128)(2,1)}, u32[]{:S(2)}) copy-start(bf16[16,160,704]{2,1,0:T(8,128)(2,1)} %get-tuple-element.70) | copy-start | bytes 10813444
  888.5 4.9 copy-start.5
  890.7 3.7 copy-start.11
  890.7 4.5 copy-start.10
  893.4 2.7 copy-start.9
  893.4 3.5 copy-start.8
Sparse Core Ops, SparseCore 0:
  242.7 38.4 reduce-scatter.1

commit v3 on v2

--- a/solution.py
+++ b/solution.py
@@ -312,412 +312,6 @@
 def rcopy(src, dst, ssem, rsem, device):
     return pltpu.make_async_remote_copy(src_ref=src, dst_ref=dst, send_sem=ssem, recv_sem=rsem, device_id=device, device_id_type=MESH)
 
-def gather_kernel(x_ref, o_ref, zs, zr, x0s, x0r, x1s, x1r, y0s, y0r, y1s, y1r, cs, cr, lsem):
-    z, x, y, c = place()
-    rows = x_ref.shape[0]; h = rows // 2
-    lo, hi = pl.ds(0, h), pl.ds(h, h)
-    part = (lo, hi)
-    xn, yn, cn = dev(z, 1 - x, y, c), dev(z, x, 1 - y, c), dev(z, x, y, 1 - c)
-    greet(z, x, y, c)
-    mine = blk(z, x, y, c)
-    own = pltpu.make_async_copy(x_ref, o_ref.at[mine], lsem)
-    own.start()
-
-    def zcopy(s, up):
-        src = o_ref.at[blk(s, x, y, c)]
-        return rcopy(src, o_ref.at[blk(s, x, y, c)], zs.at[s, up], zr.at[s], dev(z + (1 if up else -1), x, y, c))
-    def x0(s):
-        b = blk(s, x, y, c)
-        return rcopy(o_ref.at[b, lo], o_ref.at[b, lo], x0s.at[s], x0r.at[s], xn)
-    def y1(s):
-        b = blk(s, x, y, c)
-        return rcopy(o_ref.at[b, hi], o_ref.at[b, hi], y1s.at[s], y1r.at[s], yn)
-    def y0(s, xx):
-        b = blk(s, xx, y, c)
-        return rcopy(o_ref.at[b, lo], o_ref.at[b, lo], y0s.at[s, xx], y0r.at[s, xx], yn)
-    def x1(s, yy):
-        b = blk(s, x, yy, c)
-        return rcopy(o_ref.at[b, hi], o_ref.at[b, hi], x1s.at[s, yy], x1r.at[s, yy], xn)
-    def cc(s, xx, yy, p):
-        b = blk(s, xx, yy, c)
-        i = (s * 2 + xx) * 2 + yy
-        return rcopy(o_ref.at[b, part[p]], o_ref.at[b, part[p]], cs.at[i, p], cr.at[i, p], cn)
-    def column(s):
-        x0(s).start(); y1(s).start(); y0(s, x).start(); x1(s, y).start()
-        cc(s, x, y, 0).start(); cc(s, x, y, 1).start()
-    def middle(s):
-        x0(s).wait_recv()
-        y0(s, 1 - x).start(); cc(s, 1 - x, y, 0).start()
-        y1(s).wait_recv()
-        x1(s, 1 - y).start(); cc(s, x, 1 - y, 1).start()
-    def last(s):
-        for q in (0, 1):
-            y0(s, q).wait_recv(); cc(s, q, 1 - y, 0).start()
-            x1(s, q).wait_recv(); cc(s, 1 - x, q, 1).start()
-
-    own.wait()
-    @pl.when(z < 3)
-    def _(): zcopy(z, 1).start()
-    @pl.when(z > 0)
-    def _(): zcopy(z, 0).start()
-    column(z)
-    def each(k, fn):
-        if k == 0:
-            fn(z)
-            return
-        for sign in (-1, 1):
-            s = z + sign * k
-            @pl.when((s >= 0) & (s <= 3))
-            def _(s=s): fn(s)
-    for k in range(1, 4):
-        for sign in (-1, 1):
-            s = z + sign * k
-            @pl.when((s >= 0) & (s <= 3))
-            def _(s=s, sign=sign):
-                up = 1 if sign < 0 else 0
-                zcopy(s, up).wait_recv()
-                @pl.when((z + (1 if up else -1) >= 0) & (z + (1 if up else -1) <= 3))
-                def _(): zcopy(s, up).start()
-                column(s)
-        each(k - 1, middle)
-        if k >= 2: each(k - 2, last)
-    each(3, middle); each(2, last); each(3, last)
-    for s in range(4):
-        for xx in (0, 1):
-            for yy in (0, 1):
-                for p in (0, 1):
-                    cc(s, xx, yy, p).wait_recv()
-    for s in range(4):
-        x0(s).wait_send(); y1(s).wait_send()
-        for q in (0, 1):
-            y0(s, q).wait_send(); x1(s, q).wait_send()
-            for r in (0, 1):
-                for p in (0, 1): cc(s, q, r, p).wait_send()
-        @pl.when((z < 3) & (s <= z))
-        def _(): zcopy(s, 1).wait_send()
-        @pl.when((z > 0) & (s >= z))
-        def _(): zcopy(s, 0).wait_send()
-
-def gather_rows(x, cid, name):
-    rows, width = x.shape
-    D = pltpu.SemaphoreType.DMA
-    out = pl.pallas_call(gather_kernel, out_shape=jax.ShapeDtypeStruct((32, rows, width), x.dtype),
-        in_specs=[pl.BlockSpec(memory_space=pl.ANY)], out_specs=pl.BlockSpec(memory_space=pl.ANY),
-        scratch_shapes=[D((4, 2)), D((4,)), D((4,)), D((4,)), D((4, 2)), D((4, 2)), D((4, 2)), D((4, 2)), D((4,)), D((4,)), D((16, 2)), D((16, 2)), D],
-        compiler_params=pltpu.CompilerParams(collective_id=cid, has_side_effects=True), name=name)(x)
-    return out.reshape(32 * rows, width)
-
-def scatter_kernel(p_ref, o_ref, acc, ic, iy0, ix0, ix1, iy1, izu, izd, ls, cs, cr, y0s, y0r, x0s, x0r, x1s, x1r, y1s, y1r, zus, zur, zds, zdr):
-    z, x, y, c = place()
-    rows = p_ref.shape[1]; h = rows // 2
-    lo, hi = pl.ds(0, h), pl.ds(h, h)
-    xn, yn, cn = dev(z, 1 - x, y, c), dev(z, x, 1 - y, c), dev(z, x, y, 1 - c)
-    greet(z, x, y, c)
-    def at(s, xx, yy): return (s * 2 + xx) * 2 + yy
-    def load(s, xx, yy):
-        return pltpu.make_async_copy(p_ref.at[blk(s, xx, yy, c)], acc.at[at(s, xx, yy)], ls.at[at(s, xx, yy)])
-    def cc(s, xx, yy):
-        i = at(s, xx, yy)
-        return rcopy(p_ref.at[blk(s, xx, yy, 1 - c)], ic.at[i], cs.at[i], cr.at[i], cn)
-    def y0(s, xx):
-        return rcopy(acc.at[at(s, xx, 1 - y), lo], iy0.at[s * 2 + xx], y0s.at[s, xx], y0r.at[s, xx], yn)
-    def x1(s, yy):
-        return rcopy(acc.at[at(s, 1 - x, yy), hi], ix1.at[s * 2 + yy], x1s.at[s, yy], x1r.at[s, yy], xn)
-    def x0(s):
-        return rcopy(acc.at[at(s, 1 - x, y), lo], ix0.at[s], x0s.at[s], x0r.at[s], xn)
-    def y1(s):
-        return rcopy(acc.at[at(s, x, 1 - y), hi], iy1.at[s], y1s.at[s], y1r.at[s], yn)
-    def zu(s):
-        return rcopy(acc.at[at(s, x, y)], izu.at[s], zus.at[s], zur.at[s], dev(z + 1, x, y, c))
-    def zd(s):
-        return rcopy(acc.at[at(s, x, y)], izd.at[s], zds.at[s], zdr.at[s], dev(z - 1, x, y, c))
-    def add(i, start, count, src, j):
-        step = 16
-        @pl.loop(0, count // step)
-        def _(r):
-            a = pl.ds(pl.multiple_of(start + r * step, step), step)
-            b = pl.ds(pl.multiple_of(r * step, step), step)
-            acc[i, a] = acc[i, a] + src[j, b]
-    def order(fn, k):
-        if k == 0:
-            fn(z); return
-        for sign in (-1, 1):
-            s = z + sign * k
-            @pl.when((s >= 0) & (s <= 3))
-            def _(s=s): fn(s)
-    def start(s):
-        for xx in (0, 1):
-            for yy in (0, 1):
-                cc(s, xx, yy).start(); load(s, xx, yy).start()
-    def first(s):
-        for xx in (0, 1):
-            for yy in (0, 1):
-                load(s, xx, yy).wait(); cc(s, xx, yy).wait_recv()
-                add(at(s, xx, yy), 0, rows, ic, at(s, xx, yy))
-                @pl.when(yy != y)
-                def _(): y0(s, xx).start()
-                @pl.when(xx != x)
-                def _(): x1(s, yy).start()
-    def second(s):
-        y0(s, 1 - x).wait_recv(); add(at(s, 1 - x, y), 0, h, iy0, s * 2 + 1 - x); x0(s).start()
-        x1(s, 1 - y).wait_recv(); add(at(s, x, 1 - y), h, h, ix1, s * 2 + 1 - y); y1(s).start()
-        y0(s, x).wait_recv(); add(at(s, x, y), 0, h, iy0, s * 2 + x)
-        x1(s, y).wait_recv(); add(at(s, x, y), h, h, ix1, s * 2 + y)
-    def third(s):
-        me = at(s, x, y)
-        x0(s).wait_recv(); add(me, 0, h, ix0, s)
-        y1(s).wait_recv(); add(me, h, h, iy1, s)
-        @pl.when((s >= z) & (z > 0))
-        def _():
-            zu(s).wait_recv(); add(me, 0, rows, izu, s)
-        @pl.when((s <= z) & (z < 3))
-        def _():
-            zd(s).wait_recv(); add(me, 0, rows, izd, s)
-        @pl.when(s > z)
-        def _(): zu(s).start()
-        @pl.when(s < z)
-        def _(): zd(s).start()
-    for k in (3, 2, 1, 0): order(start, k)
-    for k in (3, 2, 1, 0):
-        order(first, k)
-        if k + 1 <= 3: order(second, k + 1)
-        if k + 2 <= 3: order(third, k + 2)
-    order(second, 0); order(third, 1); order(third, 0)
-    o_ref[...] = acc[at(z, x, y)]
-    for s in range(4):
-        for q in (0, 1):
-            for r in (0, 1): cc(s, q, r).wait_send()
-            y0(s, q).wait_send(); x1(s, q).wait_send()
-        x0(s).wait_send(); y1(s).wait_send()
-        @pl.when(s > z)
-        def _(): zu(s).wait_send()
-        @pl.when(s < z)
-        def _(): zd(s).wait_send()
-
-def scatter_rows(p, cid, name):
-    total, width = p.shape
-    rows = total // 32; h = rows // 2
-    D = pltpu.SemaphoreType.DMA
-    V = lambda n, r: pltpu.VMEM((n, r, width), p.dtype)
-    return pl.pallas_call(scatter_kernel, out_shape=jax.ShapeDtypeStruct((rows, width), p.dtype),
-        in_specs=[pl.BlockSpec(memory_space=pl.ANY)], out_specs=pl.BlockSpec(memory_space=pltpu.VMEM),
-        scratch_shapes=[V(16, rows), V(16, rows), V(8, h), V(4, h), V(8, h), V(4, h), V(4, rows), V(4, rows),
-            D((16,)), D((16,)), D((16,)), D((4, 2)), D((4, 2)), D((4,)), D((4,)), D((4, 2)), D((4, 2)), D((4,)), D((4,)), D((4,)), D((4,)), D((4,)), D((4,))],
-        compiler_params=pltpu.CompilerParams(collective_id=cid, has_side_effects=True, vmem_limit_bytes=56 << 20), name=name)(p.reshape(32, rows, width))
-
-
-def start_kernel(n, *refs):
-    ins, g_in = refs[:n], refs[n]
-    outs, g_out = refs[n + 1:2 * n + 1], refs[2 * n + 1]
-    zs, zr, xs, xr, cs, cr, ls = refs[2 * n + 2:2 * n + 9]
-    gzs, gzr, gxs, gxr, gys, gyr, gcs, gcr, gl = refs[2 * n + 9:]
-    z, x, y, c = place()
-    xn, yn, cn = dev(z, 1 - x, y, c), dev(z, x, 1 - y, c), dev(z, x, y, 1 - c)
-    greet(z, x, y, c)
-    def pos(s, xx, cc_): return (s * 2 + xx) * 2 + cc_
-    me = pos(z, x, c)
-    owns = [pltpu.make_async_copy(ins[a], outs[a].at[me], ls.at[a]) for a in range(n)]
-    owns.append(pltpu.make_async_copy(g_in, g_out.at[blk(z, x, y, c)], gl))
-    for o in owns: o.start()
-    def wz(a, s, up):
-        r = outs[a].at[pos(s, x, c)]
-        return rcopy(r, r, zs.at[a, s, up], zr.at[a, s], dev(z + (1 if up else -1), x, y, c))
-    def wx(a, s):
-        r = outs[a].at[pos(s, x, c)]
-        return rcopy(r, r, xs.at[a, s], xr.at[a, s], xn)
-    def wc(a, s, xx):
-        r = outs[a].at[pos(s, xx, c)]
-        return rcopy(r, r, cs.at[a, s * 2 + xx], cr.at[a, s * 2 + xx], cn)
-    def gz(s, up):
-        r = g_out.at[blk(s, x, y, c)]
-        return rcopy(r, r, gzs.at[s, up], gzr.at[s], dev(z + (1 if up else -1), x, y, c))
-    def gx(s):
-        r = g_out.at[blk(s, x, y, c)]
-        return rcopy(r, r, gxs.at[s], gxr.at[s], xn)
-    def gy(s, xx):
-        r = g_out.at[blk(s, xx, y, c)]
-        return rcopy(r, r, gys.at[s, xx], gyr.at[s, xx], yn)
-    def gc(s, xx, yy):
-        r = g_out.at[blk(s, xx, yy, c)]
-        return rcopy(r, r, gcs.at[s * 2 + xx, yy], gcr.at[s * 2 + xx, yy], cn)
-    for o in owns: o.wait()
-    def inside(v): return (v >= 0) & (v <= 3)
-    def each(k, fn):
-        if k == 0:
-            fn(z); return
-        for sign in (-1, 1):
-            s = z + sign * k
-            @pl.when(inside(s))
-            def _(s=s): fn(s)
-    def column(s):
-        for a in range(n):
-            wx(a, s).start(); wc(a, s, x).start()
-    def gcolumn(s):
-        gx(s).start(); gy(s, x).start(); gc(s, x, y).start()
-    def middle(s):
-        for a in range(n):
-            wx(a, s).wait_recv(); wc(a, s, 1 - x).start()
-    def gmiddle(s):
-        gx(s).wait_recv(); gy(s, 1 - x).start(); gc(s, 1 - x, y).start()
-    def glast(s):
-        for q in (0, 1):
-            gy(s, q).wait_recv(); gc(s, q, 1 - y).start()
-    def launch(fn):
-        @pl.when(z < 3)
-        def _(): fn(1)
-        @pl.when(z > 0)
-        def _(): fn(0)
-    launch(lambda up: [wz(a, z, up).start() for a in range(n)])
-    column(z)
-    launch(lambda up: gz(z, up).start())
-    gcolumn(z)
-    def arrive(k, recv, go, then):
-        for sign in (-1, 1):
-            s = z + sign * k
-            @pl.when(inside(s))
-            def _(s=s, sign=sign):
-                up = 1 if sign < 0 else 0
-                nxt = inside(z - sign)
-                recv(s, up)
-                @pl.when(nxt)
-                def _(): go(s, up)
-                then(s)
-    for k in range(1, 4):
-        arrive(k, lambda s, up: [wz(a, s, up).wait_recv() for a in range(n)], lambda s, up: [wz(a, s, up).start() for a in range(n)], column)
-        each(k - 1, middle)
-        arrive(k, lambda s, up: gz(s, up).wait_recv(), lambda s, up: gz(s, up).start(), gcolumn)
-        each(k - 1, gmiddle)
-    each(3, middle); each(3, gmiddle)
-    for k in range(4): each(k, glast)
-    for s in range(4):
-        for q in (0, 1):
-            for a in range(n): wc(a, s, q).wait_recv()
-            for r in (0, 1): gc(s, q, r).wait_recv()
-    for s in range(4):
-        for a in range(n):
-            wx(a, s).wait_send()
-            for q in (0, 1): wc(a, s, q).wait_send()
-        gx(s).wait_send()
-        for q in (0, 1):
-            gy(s, q).wait_send()
-            for r in (0, 1): gc(s, q, r).wait_send()
-        @pl.when((z < 3) & (s <= z))
-        def _():
-            gz(s, 1).wait_send()
-            for a in range(n): wz(a, s, 1).wait_send()
-        @pl.when((z > 0) & (s >= z))
-        def _():
-            gz(s, 0).wait_send()
-            for a in range(n): wz(a, s, 0).wait_send()
-
-def start_gather(arrays, rows, cid, name):
-    n = len(arrays)
-    D = pltpu.SemaphoreType.DMA
-    any_ = pl.BlockSpec(memory_space=pl.ANY)
-    outs = pl.pallas_call(functools.partial(start_kernel, n),
-        out_shape=[jax.ShapeDtypeStruct((16,) + a.shape, a.dtype) for a in arrays] + [jax.ShapeDtypeStruct((32,) + rows.shape, rows.dtype)],
-        in_specs=[pl.BlockSpec(memory_space=pltpu.VMEM)] * (n + 1), out_specs=[any_] * (n + 1),
-        scratch_shapes=[D((n, 4, 2)), D((n, 4)), D((n, 4)), D((n, 4)), D((n, 8)), D((n, 8)), D((n,)),
-            D((4, 2)), D((4,)), D((4,)), D((4,)), D((4, 2)), D((4, 2)), D((8, 2)), D((8, 2)), D],
-        compiler_params=pltpu.CompilerParams(collective_id=cid, has_side_effects=True), name=name)(*arrays, rows)
-    return outs
-
-def wsum_kernel(n, *refs):
-    ins, outs = refs[:n], refs[n:2 * n]
-    acc, ic, ix, izu, izd, ls, cs, cr, xs, xr, zus, zur, zds, zdr = refs[2 * n:]
-    z, x, y, c = place()
-    depth = ins[0].shape[1]
-    xn, cn = dev(z, 1 - x, y, c), dev(z, x, y, 1 - c)
-    greet_plane(z, x, y, c)
-    def at(s, xx): return s * 2 + xx
-    def pos(s, xx, cc_): return (s * 2 + xx) * 2 + cc_
-    def load(a, s, xx):
-        i = at(s, xx)
-        return pltpu.make_async_copy(ins[a].at[pos(s, xx, c)], acc.at[a, i], ls.at[a, i])
-    def wc(a, s, xx):
-        i = at(s, xx)
-        return rcopy(ins[a].at[pos(s, xx, 1 - c)], ic.at[a, i], cs.at[a, i], cr.at[a, i], cn)
-    def wx(a, s):
-        return rcopy(acc.at[a, at(s, 1 - x)], ix.at[a, s], xs.at[a, s], xr.at[a, s], xn)
-    def zu(a, s):
-        return rcopy(acc.at[a, at(s, x)], izu.at[a, s], zus.at[a, s], zur.at[a, s], dev(z + 1, x, y, c))
-    def zd(a, s):
-        return rcopy(acc.at[a, at(s, x)], izd.at[a, s], zds.at[a, s], zdr.at[a, s], dev(z - 1, x, y, c))
-    def add(a, i, src, j):
-        step = 16
-        @pl.loop(0, depth // step)
-        def _(r):
-            b = pl.ds(pl.multiple_of(r * step, step), step)
-            acc[a, i, b] = acc[a, i, b] + src[a, j, b]
-    def order(fn, k):
-        if k == 0:
-            fn(z); return
-        for sign in (-1, 1):
-            s = z + sign * k
-            @pl.when((s >= 0) & (s <= 3))
-            def _(s=s): fn(s)
-    def start(s):
-        for a in range(n):
-            for q in (0, 1):
-                wc(a, s, q).start(); load(a, s, q).start()
-    def first(s):
-        for a in range(n):
-            for q in (0, 1):
-                load(a, s, q).wait(); wc(a, s, q).wait_recv()
-                add(a, at(s, q), ic, at(s, q))
-            wx(a, s).start()
-    def second(s):
-        for a in range(n):
-            wx(a, s).wait_recv(); add(a, at(s, x), ix, s)
-            @pl.when((s >= z) & (z > 0))
-            def _():
-                zu(a, s).wait_recv(); add(a, at(s, x), izu, s)
-            @pl.when((s <= z) & (z < 3))
-            def _():
-                zd(a, s).wait_recv(); add(a, at(s, x), izd, s)
-            @pl.when(s > z)
-            def _(): zu(a, s).start()
-            @pl.when(s < z)
-            def _(): zd(a, s).start()
-    for k in (3, 2, 1, 0): order(start, k)
-    for k in (3, 2, 1, 0):
-        order(first, k)
-        if k + 1 <= 3: order(second, k + 1)
-    order(second, 0)
-    for a in range(n):
-        outs[a][...] = acc[a, at(z, x)].astype(jnp.float32)
-    for s in range(4):
-        for a in range(n):
-            for q in (0, 1): wc(a, s, q).wait_send()
-            wx(a, s).wait_send()
-            @pl.when(s > z)
-            def _(): zu(a, s).wait_send()
-            @pl.when(s < z)
-            def _(): zd(a, s).wait_send()
-
-def greet_plane(z, x, y, c):
-    bar = pltpu.get_barrier_semaphore()
-    for other in (dev(z, 1 - x, y, c), dev(z, x, y, 1 - c)):
-        pl.semaphore_signal(bar, inc=1, device_id=other, device_id_type=MESH)
-    @pl.when(z > 0)
-    def _():
-        pl.semaphore_signal(bar, inc=1, device_id=dev(z - 1, x, y, c), device_id_type=MESH)
-    @pl.when(z < 3)
-    def _():
-        pl.semaphore_signal(bar, inc=1, device_id=dev(z + 1, x, y, c), device_id_type=MESH)
-    pl.semaphore_wait(bar, 2 + (z > 0).astype(jnp.int32) + (z < 3).astype(jnp.int32))
-
-def weight_sums(arrays, cid, name):
-    n = len(arrays); total, width = arrays[0].shape; depth = total // 16
-    D = pltpu.SemaphoreType.DMA
-    V = lambda k: pltpu.VMEM((n, k, depth, width), arrays[0].dtype)
-    return pl.pallas_call(functools.partial(wsum_kernel, n),
-        out_shape=[jax.ShapeDtypeStruct((depth, width), jnp.float32)] * n,
-        in_specs=[pl.BlockSpec(memory_space=pl.ANY)] * n, out_specs=[pl.BlockSpec(memory_space=pltpu.VMEM)] * n,
-        scratch_shapes=[V(8), V(8), V(4), V(4), V(4), D((n, 8)), D((n, 8)), D((n, 8)), D((n, 4)), D((n, 4)), D((n, 4)), D((n, 4)), D((n, 4)), D((n, 4))],
-        compiler_params=pltpu.CompilerParams(collective_id=cid, has_side_effects=True, vmem_limit_bytes=56 << 20), name=name)(*[a.reshape(16, depth, width) for a in arrays])
-
-
 def nearest(z, g):
     one = jnp.where(z == 0, 1, z - 1)
     two = jnp.where(z == 3, 1, jnp.where(z == 2, 3, 2))
@@ -730,14 +324,24 @@
 def nn(left, right):
     return jnp.dot(left, right, preferred_element_type=jnp.float32)
 
+def greet_all(z, x, y, c):
+    bar = pltpu.get_barrier_semaphore()
+    for other in (dev(z, 1 - x, y, c), dev(z, x, 1 - y, c), dev(z, x, y, 1 - c)):
+        pl.semaphore_signal(bar, inc=1, device_id=other, device_id_type=MESH)
+    for s in range(4):
+        @pl.when(s != z)
+        def _(): pl.semaphore_signal(bar, inc=1, device_id=dev(s, x, y, c), device_id_type=MESH)
+    pl.semaphore_wait(bar, 6)
+
+
 def expert_kernel(
-    a_in, deh, dhs, rank_row, rank_col, gate, wg_h, wu_h, wd_h, sgu_h, sdt_h,
+    a_in, deh, dy_all, rank_row, rank_col, gate, wg_h, wu_h, wd_h, sgu_h, sdt_h, sd_h,
     total, act_all, rows_o, eh_o, deg_o, deu_o, hs_o, dsgu_o, part, ffn_part,
-    wg, wu, wd, sgu, tail, acc, ic, iy0, ix0, ix1, iy1, izu, izd,
-    eg, eu, dehb, ehb, degb, deub, dhsb, hsb, dsgub, eh2, hs2, ot,
+    wg, wu, wd, sgu, tail, acc, ic, iy0, ix0, ix1, iy1, iz,
+    eg, eu, dehb, ehb, degb, deub, sd, dhs, hsb, dsgub, eh2, hs2, ot,
     wsem, usem, ssem, osem, psem, lsem,
     zs, zr, x0s, x0r, x1s, x1r, y0s, y0r, y1s, y1r, cs, cr,
-    ls, rcs, rcr, ry0s, ry0r, rx0s, rx0r, rx1s, rx1r, ry1s, ry1r, zus, zur, zds, zdr,
+    ls, rcs, rcr, ry0s, ry0r, rx0s, rx0r, rx1s, rx1r, ry1s, ry1r, rzs, rzr,
 ):
     f32, bf16 = jnp.float32, jnp.bfloat16
     z, x, y, c = place()
@@ -748,13 +352,13 @@
     lo, hi = pl.ds(0, h), pl.ds(h, h)
     part_of = (lo, hi)
     xn, yn, cn = dev(z, 1 - x, y, c), dev(z, x, 1 - y, c), dev(z, x, y, 1 - c)
-    greet(z, x, y, c)
+    greet_all(z, x, y, c)
     mine = blk(z, x, y, c)
     own = pltpu.make_async_copy(a_in, act_all.at[mine], lsem)
     own.start()
     weights = [
         pltpu.make_async_copy(a, b, wsem.at[i])
-        for i, (a, b) in enumerate(((wg_h, wg), (wu_h, wu), (wd_h, wd), (sgu_h, sgu), (sdt_h, tail.at[pl.ds(cap, 256 - cap)])))
+        for i, (a, b) in enumerate(((wg_h, wg), (wu_h, wu), (wd_h, wd), (sgu_h, sgu), (sdt_h, tail.at[pl.ds(cap, 256 - cap)]), (sd_h, sd)))
     ]
     for w in weights:
         w.start()
@@ -830,16 +434,40 @@
                 pltpu.make_async_copy(deub.at[r], deu_o.at[j], ssem.at[k, 3]),
                 pltpu.make_async_copy(hsb.at[k], hs_o.at[j], ssem.at[k, 4]),
                 pltpu.make_async_copy(dsgub.at[k], dsgu_o.at[j], ssem.at[k, 5]),
-                pltpu.make_async_copy(acc.at[pl.ds(10 + 2 * k, 2)], part.at[pl.ds(2 * j, 2)], ssem.at[k, 6]),
             ]
         return out
+
+    def at(s, xx, yy): return (s * 2 + xx) * 2 + yy
+    def keep(u, k):
+        s, xx = seq_of(u)
+        return pltpu.make_async_copy(acc.at[pl.ds(10 + 2 * k, 2)], part.at[pl.ds(at(s, xx, 0), 2)], ssem.at[k, 6])
+    def cross(s, xx, yy, k):
+        i = at(s, xx, yy)
+        return rcopy(acc.at[10 + 2 * k + yy], ic.at[i], rcs.at[i], rcr.at[i], cn)
+    def hand_over(u):
+        s, xx = seq_of(u)
+        for k in (0, 1):
+            @pl.when(c == k)
+            def _(): keep(u, k).start()
+            @pl.when(c != k)
+            def _():
+                for yy in (0, 1):
+                    cross(s, xx, yy, k).start()
+    def handed_over(u):
+        s, xx = seq_of(u)
+        for k in (0, 1):
+            @pl.when(c == k)
+            def _(): keep(u, k).wait()
+            @pl.when(c != k)
+            def _():
+                for yy in (0, 1):
+                    cross(s, xx, yy, k).wait_send()
 
     def unit(u):
         s, xx = seq_of(u)
         base = (s * 2 + xx) * 2
         for k in (0, 1):
             pltpu.make_async_copy(deh.at[base + k], dehb.at[pl.ds(k * cap, cap)], usem.at[k, 1]).start()
-            pltpu.make_async_copy(dhs.at[base + k], dhsb.at[k], usem.at[k, 2]).start()
         for yy in (0, 1):
             for p in (0, 1):
                 side(s, xx, yy, p).wait_recv()
@@ -853,6 +481,7 @@
         def _():
             for copy in stores(u - 1):
                 copy.wait()
+            handed_over(u - 1)
         for k in (0, 1):
             loads[k].wait()
             act = acc[4 + 2 * k:6 + 2 * k].reshape(toks, width)
@@ -862,15 +491,14 @@
             acc[k] = nn(pick, act).astype(bf16)
             pre = nn(act, sgu[...])
             gp, up = pre[:, :128], pre[:, 128:]
-            pltpu.make_async_copy(dhs.at[base + k], dhsb.at[k], usem.at[k, 2]).wait()
-            dh = dhsb[k]
+            dh = dhs[base + k]
             sig = jax.nn.sigmoid(gp)
             hsb[k] = (gp * sig * up).astype(bf16)
             dsgub[k, :, 0:128] = (dh * up * sig * (1.0 + gp * (1.0 - sig))).astype(bf16)
             dsgub[k, :, 128:256] = (dh * gp * sig).astype(bf16)
         picked = acc[0:2].reshape(2 * cap, width)
-        eg[...] = nn(picked, wg[...])
-        eu[...] = nn(picked, wu[...])
+        eg[...] = nt(picked, wg[...])
+        eu[...] = nt(picked, wu[...])
         for k in (0, 1):
             pltpu.make_async_copy(deh.at[base + k], dehb.at[pl.ds(k * cap, cap)], usem.at[k, 1]).wait()
         @pl.loop(0, 2 * cap // 32)
@@ -885,7 +513,7 @@
         dg, du = degb[...], deub[...]
         for n in range(0, width, 512):
             w = pl.ds(n, 512)
-            back = (nt(dg, wg[w, :]) + nt(du, wu[w, :])).astype(bf16)
+            back = (nn(dg, wg[:, w]) + nn(du, wu[:, w])).astype(bf16)
             acc[8, :, w] = back[:cap]
             acc[9, :, w] = back[cap:]
         for k in (0, 1):
@@ -899,6 +527,57 @@
                 acc[11 + 2 * k, :, w] = out[rows:]
         for copy in stores(u):
             copy.start()
+        hand_over(u)
+
+    def ry0(s, xx):
+        return rcopy(ic.at[at(s, xx, 1 - y), lo], iy0.at[s * 2 + xx], ry0s.at[s, xx], ry0r.at[s, xx], yn)
+    def rx1(s, yy):
+        return rcopy(ic.at[at(s, 1 - x, yy), hi], ix1.at[s * 2 + yy], rx1s.at[s, yy], rx1r.at[s, yy], xn)
+    def rx0(s):
+        return rcopy(ic.at[at(s, 1 - x, y), lo], ix0.at[s], rx0s.at[s], rx0r.at[s], xn)
+    def ry1(s):
+        return rcopy(ic.at[at(s, x, 1 - y), hi], iy1.at[s], ry1s.at[s], ry1r.at[s], yn)
+    def rz(s):
+        return rcopy(ic.at[at(s, x, y)], iz.at[z], rzs.at[s], rzr.at[z], dev(s, x, y, c))
+    def rz_wait(s):
+        rcopy(iz.at[s], iz.at[s], rzs.at[s], rzr.at[s], dev(s, x, y, c)).wait_recv()
+    def add(i, start, count, src, j):
+        @pl.loop(0, count // 16)
+        def _(r):
+            a = pl.ds(pl.multiple_of(start + r * 16, 16), 16)
+            b = pl.ds(pl.multiple_of(r * 16, 16), 16)
+            ic[i, a] = ic[i, a] + src[j, b]
+
+    def first(g):
+        s = nearest(z, g)
+        def load(xx, yy):
+            return pltpu.make_async_copy(part.at[at(s, xx, yy)], acc.at[4 + 2 * xx + yy], ls.at[2 * xx + yy])
+        for xx in (0, 1):
+            for yy in (0, 1):
+                load(xx, yy).start()
+        for xx in (0, 1):
+            for yy in (0, 1):
+                load(xx, yy).wait(); cross(s, xx, yy, 0).wait_recv()
+                add(at(s, xx, yy), 0, rows, acc, 4 + 2 * xx + yy)
+                @pl.when(yy != y)
+                def _(): ry0(s, xx).start()
+                @pl.when(xx != x)
+                def _(): rx1(s, yy).start()
+
+    def second(g):
+        s = nearest(z, g)
+        ry0(s, 1 - x).wait_recv(); add(at(s, 1 - x, y), 0, h, iy0, s * 2 + 1 - x); rx0(s).start()
+        rx1(s, 1 - y).wait_recv(); add(at(s, x, 1 - y), h, h, ix1, s * 2 + 1 - y); ry1(s).start()
+        ry0(s, x).wait_recv(); add(at(s, x, y), 0, h, iy0, s * 2 + x)
+        rx1(s, y).wait_recv(); add(at(s, x, y), h, h, ix1, s * 2 + y)
+
+    def third(g):
+        s = nearest(z, g)
+        me = at(s, x, y)
+        rx0(s).wait_recv(); add(me, 0, h, ix0, s)
+        ry1(s).wait_recv(); add(me, h, h, iy1, s)
+        if g > 0:
+            rz(s).start()
 
     own.wait()
     @pl.when(z < 3)
@@ -906,8 +585,19 @@
     @pl.when(z > 0)
     def _(): zcopy(z, 0).start()
     column(z)
+    def dy_load(j, b):
+        return pltpu.make_async_copy(dy_all.at[pl.ds(2 * j, 2)], acc.at[pl.ds(2 + 12 * b, 2)], usem.at[b, 2])
+    dy_load(0, 0).start()
     for w in weights:
         w.wait()
+    @pl.loop(0, 8)
+    def _(i):
+        for b in (0, 1):
+            j = 2 * i + b
+            @pl.when(j < 15)
+            def _(): dy_load(j + 1, 1 - b).start()
+            dy_load(j, b).wait()
+            dhs[j] = nn(acc[2 + 12 * b:4 + 12 * b].reshape(toks, width), sd[...])
 
     @pl.loop(0, 8)
     def _(u):
@@ -922,85 +612,24 @@
             arrive(3); last_own(1); middle(2)
         @pl.when(u == 3)
         def _():
-            last_other(1); middle(3)
+            last_other(1); middle(3); first(0)
         @pl.when(u == 4)
         def _():
             last_own(2)
         @pl.when(u == 5)
         def _():
-            last_other(2)
+            last_other(2); first(1); second(0)
         @pl.when(u == 6)
         def _():
             last_own(3)
         @pl.when(u == 7)
         def _():
-            last_other(3)
+            last_other(3); first(2); second(1); third(0)
         unit(u)
 
     for copy in stores(7):
         copy.wait()
-
-    def at(s, xx, yy): return (s * 2 + xx) * 2 + yy
-    def load(s, xx, yy):
-        return pltpu.make_async_copy(part.at[blk(s, xx, yy, c)], acc.at[at(s, xx, yy)], ls.at[at(s, xx, yy)])
-    def cross(s, xx, yy):
-        i = at(s, xx, yy)
-        return rcopy(part.at[blk(s, xx, yy, 1 - c)], ic.at[i], rcs.at[i], rcr.at[i], cn)
-    def ry0(s, xx):
-        return rcopy(acc.at[at(s, xx, 1 - y), lo], iy0.at[s * 2 + xx], ry0s.at[s, xx], ry0r.at[s, xx], yn)
-    def rx1(s, yy):
-        return rcopy(acc.at[at(s, 1 - x, yy), hi], ix1.at[s * 2 + yy], rx1s.at[s, yy], rx1r.at[s, yy], xn)
-    def rx0(s):
-        return rcopy(acc.at[at(s, 1 - x, y), lo], ix0.at[s], rx0s.at[s], rx0r.at[s], xn)
-    def ry1(s):
-        return rcopy(acc.at[at(s, x, 1 - y), hi], iy1.at[s], ry1s.at[s], ry1r.at[s], yn)
-    def zu(s):
-        return rcopy(acc.at[at(s, x, y)], izu.at[s], zus.at[s], zur.at[s], dev(z + 1, x, y, c))
-    def zd(s):
-        return rcopy(acc.at[at(s, x, y)], izd.at[s], zds.at[s], zdr.at[s], dev(z - 1, x, y, c))
-    def add(i, start, count, src, j):
-        @pl.loop(0, count // 16)
-        def _(r):
-            a = pl.ds(pl.multiple_of(start + r * 16, 16), 16)
-            b = pl.ds(pl.multiple_of(r * 16, 16), 16)
-            acc[i, a] = acc[i, a] + src[j, b]
-
-    def first(s):
-        for xx in (0, 1):
-            for yy in (0, 1):
-                load(s, xx, yy).wait(); cross(s, xx, yy).wait_recv()
-                add(at(s, xx, yy), 0, rows, ic, at(s, xx, yy))
-                @pl.when(yy != y)
-                def _(): ry0(s, xx).start()
-                @pl.when(xx != x)
-                def _(): rx1(s, yy).start()
-
-    def second(s):
-        ry0(s, 1 - x).wait_recv(); add(at(s, 1 - x, y), 0, h, iy0, s * 2 + 1 - x); rx0(s).start()
-        rx1(s, 1 - y).wait_recv(); add(at(s, x, 1 - y), h, h, ix1, s * 2 + 1 - y); ry1(s).start()
-        ry0(s, x).wait_recv(); add(at(s, x, y), 0, h, iy0, s * 2 + x)
-        rx1(s, y).wait_recv(); add(at(s, x, y), h, h, ix1, s * 2 + y)
-
-    def third(s):
-        me = at(s, x, y)
-        rx0(s).wait_recv(); add(me, 0, h, ix0, s)
-        ry1(s).wait_recv(); add(me, h, h, iy1, s)
-        @pl.when((s >= z) & (z > 0))
-        def _():
-            zu(s).wait_recv(); add(me, 0, rows, izu, s)
-        @pl.when((s <= z) & (z < 3))
-        def _():
-            zd(s).wait_recv(); add(me, 0, rows, izd, s)
-        @pl.when(s > z)
-        def _(): zu(s).start()
-        @pl.when(s < z)
-        def _(): zd(s).start()
-
-    for g in (3, 2, 1, 0):
-        s = nearest(z, g)
-        for xx in (0, 1):
-            for yy in (0, 1):
-                cross(s, xx, yy).start(); load(s, xx, yy).start()
+    handed_over(7)
 
     def out_loads(j, b):
         return [
@@ -1036,42 +665,47 @@
     for copy in out_loads(0, 0):
         copy.start()
 
-    @pl.loop(0, 6)
-    def _(t):
-        @pl.when(t < 4)
-        def _():
-            first(nearest(z, 3 - t))
-            @pl.loop(0, 4)
-            def _(i): forward_out(4 * t + i)
-        @pl.when((t >= 1) & (t < 5))
-        def _(): second(nearest(z, 4 - t))
-        @pl.when(t >= 2)
-        def _(): third(nearest(z, 5 - t))
-
-    total[...] = acc[at(z, x, y)]
+    first(3)
+    second(2); third(1)
+    @pl.loop(0, 16)
+    def _(j):
+        @pl.when(j == 4)
+        def _():
+            second(3); third(2)
+        @pl.when(j == 8)
+        def _(): third(3)
+        forward_out(j)
+    me = at(z, x, y)
+    for g in (1, 2, 3):
+        rz_wait(nearest(z, g))
+    @pl.loop(0, rows // 16)
+    def _(r):
+        q = pl.ds(pl.multiple_of(r * 16, 16), 16)
+        out = ic[me, q].astype(f32)
+        for g in (1, 2, 3):
+            out = out + iz[nearest(z, g), q].astype(f32)
+        total[q] = out
     out_store(14, 0).wait()
     out_store(15, 1).wait()
 
     for s in range(4):
+        @pl.when((z < 3) & (s <= z))
+        def _(): zcopy(s, 1).wait_send()
+        @pl.when((z > 0) & (s >= z))
+        def _(): zcopy(s, 0).wait_send()
         x0(s).wait_send(); y1(s).wait_send()
         rx0(s).wait_send(); ry1(s).wait_send()
         for q in (0, 1):
             y0(s, q).wait_send(); x1(s, q).wait_send()
             ry0(s, q).wait_send(); rx1(s, q).wait_send()
             for r in (0, 1):
-                cross(s, q, r).wait_send()
                 for p in (0, 1):
                     side(s, q, r, p).wait_send()
-        @pl.when((z < 3) & (s <= z))
-        def _(): zcopy(s, 1).wait_send()
-        @pl.when((z > 0) & (s >= z))
-        def _(): zcopy(s, 0).wait_send()
-        @pl.when(s > z)
-        def _(): zu(s).wait_send()
-        @pl.when(s < z)
-        def _(): zd(s).wait_send()
-
-def expert_layer(act, deh, dhs, rank_row, rank_col, gate, wg, wu, wd, sgu, sdt, cid):
+        @pl.when(s != z)
+        def _():
+            rz(s).wait_send()
+
+def expert_layer(act, deh, dy_all, rank_row, rank_col, gate, wg, wu, wd, sgu, sdt, sd, cid):
     rows, width = act.shape
     cap, hidden = deh.shape[1:]
     h = rows // 2
@@ -1084,29 +718,29 @@
     return pl.pallas_call(
         expert_kernel,
         out_shape=[
-            S((rows, width), bf16), S((32, rows, width), bf16), S((16, cap, width), bf16),
+            S((rows, width), f32), S((32, rows, width), bf16), S((16, cap, width), bf16),
             S((16, cap, hidden), bf16), S((16, cap, hidden), bf16), S((16, cap, hidden), bf16),
             S((16, 2 * rows, 128), bf16), S((16, 2 * rows, 256), bf16),
-            S((32, rows, width), bf16), S((32, rows, width), bf16),
+            S((16, rows, width), bf16), S((32, rows, width), bf16),
         ],
-        in_specs=[vm, any_, any_, vm, vm, vm] + [any_] * 5,
+        in_specs=[vm, any_, any_, vm, vm, vm] + [any_] * 6,
         out_specs=[vm] + [any_] * 9,
         scratch_shapes=[
             V(*wg.shape), V(*wu.shape), V(*wd.shape), V(*sgu.shape), V(256, width),
             V(16, rows, width), V(16, rows, width), V(8, h, width), V(4, h, width), V(8, h, width), V(4, h, width),
-            V(4, rows, width), V(4, rows, width),
+            V(4, rows, width),
             V(2 * cap, hidden, t=f32), V(2 * cap, hidden, t=f32), V(2 * cap, hidden, t=f32),
             V(2 * cap, hidden), V(2 * cap, hidden), V(2 * cap, hidden),
-            V(2, 2 * rows, 128, t=f32), V(2, 2 * rows, 128), V(2, 2 * rows, 256),
+            V(*sd.shape), V(16, 2 * rows, 128, t=f32), V(2, 2 * rows, 128), V(2, 2 * rows, 256),
             V(2, cap, hidden), V(2, 2 * rows, 128), V(2, 2, rows, width),
-            D((5,)), D((2, 3)), D((2, 7)), D((2, 2)), D((2,)), D,
+            D((6,)), D((2, 3)), D((2, 7)), D((2, 2)), D((2,)), D,
             D((4, 2)), D((4,)), D((4,)), D((4,)), D((4, 2)), D((4, 2)), D((4, 2)), D((4, 2)), D((4,)), D((4,)), D((16, 2)), D((16, 2)),
-            D((16,)), D((16,)), D((16,)), D((4, 2)), D((4, 2)), D((4,)), D((4,)), D((4, 2)), D((4, 2)), D((4,)), D((4,)),
-            D((4,)), D((4,)), D((4,)), D((4,)),
+            D((4,)), D((16,)), D((16,)), D((4, 2)), D((4, 2)), D((4,)), D((4,)), D((4, 2)), D((4, 2)), D((4,)), D((4,)),
+            D((4,)), D((4,)),
         ],
-        compiler_params=pltpu.CompilerParams(collective_id=cid, has_side_effects=True, vmem_limit_bytes=62 << 20),
+        compiler_params=pltpu.CompilerParams(collective_id=cid, has_side_effects=True, vmem_limit_bytes=63 << 20),
         name="expert_layer",
-    )(act, deh, dhs, rank_row, rank_col, gate, wg, wu, wd, sgu, sdt)
+    )(act, deh, dy_all, rank_row, rank_col, gate, wg, wu, wd, sgu, sdt, sd)
 
 
 def norm_back(values, gain, grad):
@@ -1213,7 +847,7 @@
     @pl.loop(0, rows // 16)
     def _(r):
         q = pl.ds(pl.multiple_of(r * 16, 16), 16)
-        back, terms = norm_back(x_mid[q], gain2[...], grad2[q].astype(f32))
+        back, terms = norm_back(x_mid[q], gain2[...], grad2[q])
         back = back + dy[q].astype(f32)
         dx2[q] = back
         dattn[y, q] = back.astype(bf16)
@@ -1466,14 +1100,328 @@
     )(a1, dattn, dq, dk, dv, mixed, gains)
 
 
-def routing_tables(gate_table, capacity):
-    member = gate_table > 0.0
-    ranks = jnp.cumsum(member.astype(jnp.int32), axis=1) - 1
-    slot = jnp.arange(capacity, dtype=jnp.int32)
-    pick = (ranks[:, None, :] == slot[None, :, None]) & member[:, None, :]
-    slot_gate = jnp.sum(jnp.where(pick, gate_table[:, None, :], 0.0), axis=2)
-    held = jnp.where(member, ranks, -1)
-    return pick.astype(jnp.bfloat16), slot_gate, held
+def expert_grads_kernel(deg, deu, eh, dsgu, hs, rows, deo, act, dy, e_gate, e_up, e_down, gu, down):
+    def tn(left, right):
+        return lax.dot_general(left, right, (((0,), (0,)), ((), ())), preferred_element_type=jnp.float32)
+    gu[...] = tn(act[...], dsgu[...]).astype(gu.dtype)
+    down[...] = tn(dy[...], hs[...]).astype(down.dtype)
+    e_gate[...] = tn(deg[...], rows[...])
+    e_up[...] = tn(deu[...], rows[...])
+    e_down[...] = tn(eh[...], deo[...])
+
+
+def expert_grads(deg, deu, eh, dsgu, hs, rows, deo, act, dy):
+    width = rows.shape[1]
+    S = jax.ShapeDtypeStruct
+    whole = lambda a: pl.BlockSpec(a.shape, lambda i: (0, 0), pipeline_mode=pl.Buffered(1))
+    tile = lambda n: pl.BlockSpec((n, 256), lambda i: (0, i))
+    hidden = deg.shape[1]
+    return pl.pallas_call(
+        expert_grads_kernel,
+        grid=(width // 256,),
+        out_shape=[S((hidden, width), jnp.float32)] * 3 + [S((width, 256), jnp.bfloat16), S((width, 128), jnp.bfloat16)],
+        in_specs=[whole(a) for a in (deg, deu, eh, dsgu, hs)] + [tile(a.shape[0]) for a in (rows, deo, act, dy)],
+        out_specs=[tile(hidden)] * 3 + [pl.BlockSpec((256, n), lambda i: (i, 0)) for n in (256, 128)],
+        compiler_params=pltpu.CompilerParams(vmem_limit_bytes=60 << 20),
+        name="expert_grads",
+    )(deg, deu, eh, dsgu, hs, rows, deo, act, dy)
+
+
+def attention_kernel(
+    x_in, wq_in, wk_in, wv_in, wo_in, gain_in, table_in, dy_in, wd_h, cosine, sine,
+    wq_o, wk_o, wv_o, wo_o, dy_all, act1, qr, kr, vr, mixed, x_mid, act2, grow, rank_row, rank_col, gate, deo_o, deh_o,
+    gland, tland, inv, wbuf, wob, wd, qa, ka, va, own_attn, send, recv, gm, dyt, deo, deh,
+    wsem, lsem, dsem, ssem, ysem, zs, zr, xs, xr, cs, cr, gzs, gzr, gxs, gxr, gys, gyr, gcs, gcr,
+):
+    f32, bf16 = jnp.float32, jnp.bfloat16
+    z, x, y, c = place()
+    toks, width = x_in.shape
+    rows = toks // 2
+    depth, hw = wq_in.shape
+    cap, hidden = deh_o.shape[1:]
+    xn, yn, cn = dev(z, 1 - x, y, c), dev(z, x, 1 - y, c), dev(z, x, y, 1 - c)
+    expert = (z * 2 + x) * 2 + c
+    greet(z, x, y, c)
+    ins = (gain_in, table_in, wq_in, wk_in, wv_in, wo_in)
+    outs = (gland, tland, wq_o, wk_o, wv_o, wo_o)
+    n = len(outs)
+    def pos(s, xx, cc): return (s * 2 + xx) * 2 + cc
+    owns = [pltpu.make_async_copy(ins[a], outs[a].at[expert], lsem.at[a]) for a in range(n)]
+    owns.append(pltpu.make_async_copy(dy_in, dy_all.at[blk(z, x, y, c)], lsem.at[n]))
+    for o in owns:
+        o.start()
+    w_down = pltpu.make_async_copy(wd_h, wd, wsem.at[3])
+    w_down.start()
+
+    def wz(a, s, up):
+        r = outs[a].at[pos(s, x, c)]
+        return rcopy(r, r, zs.at[a, s, up], zr.at[a, s], dev(z + 2 * up - 1, x, y, c))
+    def wx(a, s):
+        r = outs[a].at[pos(s, x, c)]
+        return rcopy(r, r, xs.at[a, s], xr.at[a, s], xn)
+    def wc(a, s, xx):
+        r = outs[a].at[pos(s, xx, c)]
+        return rcopy(r, r, cs.at[a, s * 2 + xx], cr.at[a, s * 2 + xx], cn)
+    def gz(s, up):
+        r = dy_all.at[blk(s, x, y, c)]
+        return rcopy(r, r, gzs.at[s, up], gzr.at[s], dev(z + 2 * up - 1, x, y, c))
+    def gx(s):
+        r = dy_all.at[blk(s, x, y, c)]
+        return rcopy(r, r, gxs.at[s], gxr.at[s], xn)
+    def gy(s, xx):
+        r = dy_all.at[blk(s, xx, y, c)]
+        return rcopy(r, r, gys.at[s, xx], gyr.at[s, xx], yn)
+    def gc(s, xx, yy):
+        r = dy_all.at[blk(s, xx, yy, c)]
+        return rcopy(r, r, gcs.at[s * 2 + xx, yy], gcr.at[s * 2 + xx, yy], cn)
+
+    def column(s):
+        for a in range(n):
+            wx(a, s).start(); wc(a, s, x).start()
+    def middle(g):
+        s = nearest(z, g)
+        for a in range(n):
+            wx(a, s).wait_recv(); wc(a, s, 1 - x).start()
+    def gcolumn(s):
+        gx(s).start(); gy(s, x).start(); gc(s, x, y).start()
+    def gmiddle(g):
+        s = nearest(z, g)
+        gx(s).wait_recv(); gy(s, 1 - x).start(); gc(s, 1 - x, y).start()
+    def glast(g):
+        s = nearest(z, g)
+        for q in (0, 1):
+            gy(s, q).wait_recv(); gc(s, q, 1 - y).start()
+    def launch(fn):
+        @pl.when(z < 3)
+        def _(): fn(1)
+        @pl.when(z > 0)
+        def _(): fn(0)
+    def towards(g):
+        s = nearest(z, g)
+        up = (s < z).astype(jnp.int32)
+        nxt = z + 2 * up - 1
+        return s, up, (nxt >= 0) & (nxt <= 3)
+    def arrive(g):
+        s, up, more = towards(g)
+        for a in range(n):
+            wz(a, s, up).wait_recv()
+            @pl.when(more)
+            def _(): wz(a, s, up).start()
+        column(s)
+    def garrive(g):
+        s, up, more = towards(g)
+        gz(s, up).wait_recv()
+        @pl.when(more)
+        def _(): gz(s, up).start()
+        gcolumn(s)
+
+    def project(g):
+        s = nearest(z, g)
+        for a in range(n):
+            for q in (0, 1):
+                wc(a, s, q).wait_recv()
+        loads = [
+            pltpu.make_async_copy(w.at[pl.ds(4 * s, 4)], wbuf.at[i], wsem.at[i])
+            for i, w in enumerate((wq_o, wk_o, wv_o))
+        ]
+        for l in loads:
+            l.start()
+        for i in range(4):
+            at = pl.ds(pl.multiple_of((4 * s + i) * depth, depth), depth)
+            two = gland[4 * s + i][0:8].astype(f32)
+            grow[:, at] = two
+        w = pl.ds(pl.multiple_of(4 * s * depth, 4 * depth), 4 * depth)
+        a1 = (x_in[:, w].astype(f32) * inv[...] * grow[0:1, w]).astype(bf16)
+        act1[:, w] = a1
+        for i, acc in enumerate((qa, ka, va)):
+            loads[i].wait()
+            out = nn(a1, wbuf[i].reshape(4 * depth, hw))
+            if g == 0:
+                acc[...] = out
+            else:
+                acc[...] += out
+
+    def ranks_of(g):
+        s = nearest(z, g)
+        for i in range(4):
+            gm[i:i + 1, :] = tland[4 * s + i, pl.ds(expert, 1), :]
+        member = (gm[...] > 0.0).astype(f32).astype(bf16)
+        one = lax.broadcasted_iota(jnp.int32, (toks, toks), 0)
+        two = lax.broadcasted_iota(jnp.int32, (toks, toks), 1)
+        upper = jnp.where(one <= two, 1.0, 0.0).astype(bf16)
+        lower = jnp.where(one >= two, 1.0, 0.0).astype(bf16)
+        same = jnp.where(one == two, 1.0, 0.0).astype(bf16)
+        by_row = jnp.where(gm[...] > 0.0, nn(member, upper) - 1.0, -1.0).astype(jnp.int32)
+        by_col = jnp.where(nt(same, member) > 0.5, nt(lower, member) - 1.0, -1.0).astype(jnp.int32)
+        for i in range(4):
+            rank_row[4 * s + i] = by_row[i:i + 1]
+            rank_col[4 * s + i] = by_col[:, i:i + 1]
+    def stores(g, xx):
+        s = nearest(z, g)
+        base = (s * 2 + xx) * 2
+        out = []
+        for k in (0, 1):
+            out.append(pltpu.make_async_copy(deo.at[k], deo_o.at[base + k], ssem.at[k, 0]))
+            out.append(pltpu.make_async_copy(deh.at[pl.ds(k * cap, cap)], deh_o.at[base + k], ssem.at[k, 1]))
+        return out
+    def hidden_grads(g):
+        s = nearest(z, g)
+        ranks_of(g)
+        for xx in (0, 1):
+            for yy in (0, 1):
+                gc(s, xx, yy).wait_recv()
+        @pl.loop(0, 2)
+        def _(xx):
+            base = (s * 2 + xx) * 2
+            loads = [pltpu.make_async_copy(dy_all.at[pl.ds(2 * (base + k), 2)], dyt.at[k], dsem.at[k]) for k in (0, 1)]
+            for l in loads:
+                l.start()
+            if g > 0:
+                @pl.when(xx == 0)
+                def _():
+                    for copy in stores(g - 1, 1):
+                        copy.wait()
+            @pl.when(xx == 1)
+            def _():
+                for copy in stores(g, 0):
+                    copy.wait()
+            for k in (0, 1):
+                loads[k].wait()
+                hit = rank_row[base + k] == lax.broadcasted_iota(jnp.int32, (cap, toks), 0)
+                weight = jnp.sum(jnp.where(hit, tland[base + k, pl.ds(expert, 1), :], 0.0), axis=1, keepdims=True)
+                gate[base + k] = weight
+                pick = jnp.where(hit, 1.0, 0.0).astype(bf16)
+                grads = dyt[k].reshape(toks, width)
+                for m in range(0, width, 512):
+                    deo[k, :, m:m + 512] = (nn(pick, grads[:, m:m + 512]) * weight).astype(bf16)
+            deh[...] = nt(deo[...].reshape(2 * cap, width), wd[...])
+            for copy in stores(g, xx):
+                copy.start()
+
+    for o in owns:
+        o.wait()
+    launch(lambda up: [wz(a, z, up).start() for a in range(n)])
+    column(z)
+    launch(lambda up: gz(z, up).start())
+    gcolumn(z)
+    @pl.loop(0, toks // 16)
+    def _(r):
+        q = pl.ds(pl.multiple_of(r * 16, 16), 16)
+        v = x_in[q].astype(f32)
+        inv[q] = lax.rsqrt(jnp.sum(v * v, axis=1, keepdims=True) * (1.0 / width) + EPS)
+    gm[...] = jnp.zeros_like(gm)
+    w_down.wait()
+    arrive(1); middle(0); project(0)
+    garrive(1); gmiddle(0)
+    arrive(2); middle(1); project(1)
+    garrive(2); gmiddle(1); glast(0)
+    hidden_grads(0)
+    arrive(3); middle(2); project(2)
+    garrive(3); gmiddle(2); glast(1)
+    hidden_grads(1)
+    middle(3); project(3)
+    w_out = pltpu.make_async_copy(wo_o, wob, wsem.at[3])
+    w_out.start()
+
+    scale = HD ** (-0.5)
+    def turn(values):
+        return values * cosine[...] + pltpu.roll(values, HD // 2, 1) * sine[...]
+    @pl.loop(0, hw // HD)
+    def _(i):
+        @pl.when(i == 4)
+        def _(): gmiddle(3)
+        w = pl.ds(pl.multiple_of(i * HD, HD), HD)
+        qh, kh, vh = turn(qa[:, w]).astype(bf16), turn(ka[:, w]).astype(bf16), va[:, w].astype(bf16)
+        qr[:, w] = qh
+        kr[:, w] = kh
+        vr[:, w] = vh
+        scores = nt(qh, kh) * scale
+        ahead = lax.broadcasted_iota(jnp.int32, (toks, toks), 0) >= lax.broadcasted_iota(jnp.int32, (toks, toks), 1)
+        scores = jnp.where(ahead, scores, -1e30)
+        expo = jnp.exp(scores - jnp.max(scores, axis=1, keepdims=True))
+        probs = expo * (1.0 / jnp.sum(expo, axis=1, keepdims=True))
+        mixed[:, w] = nn(probs.astype(bf16), vh).astype(bf16)
+    w_out.wait()
+    whole = wob[...].reshape(width, hw)
+    other = pl.ds(pl.multiple_of((1 - y) * rows, rows), rows)
+    here = pl.ds(pl.multiple_of(y * rows, rows), rows)
+    for m in range(0, width, 512):
+        send[:, m:m + 512] = nt(mixed[other, :], whole[m:m + 512]).astype(bf16)
+    swap = rcopy(send, recv, ysem.at[0], ysem.at[1], yn)
+    swap.start()
+    for m in range(0, width, 512):
+        own_attn[:, m:m + 512] = nt(mixed[here, :], whole[m:m + 512])
+    glast(2)
+    hidden_grads(2)
+    swap.wait_recv()
+    @pl.loop(0, rows // 16)
+    def _(r):
+        q = pl.ds(pl.multiple_of(r * 16, 16), 16)
+        at = pl.ds(pl.multiple_of(y * rows + r * 16, 16), 16)
+        v = x_in[at].astype(f32) + own_attn[q] + recv[q].astype(f32)
+        x_mid[q] = v
+        scaled = v * lax.rsqrt(jnp.sum(v * v, axis=1, keepdims=True) * (1.0 / width) + EPS)
+        act2[q] = (scaled * grow[1:2]).astype(bf16)
+    glast(3)
+    hidden_grads(3)
+    for copy in stores(3, 1):
+        copy.wait()
+    swap.wait_send()
+    for s in range(4):
+        for a in range(n):
+            wx(a, s).wait_send()
+            for q in (0, 1):
+                wc(a, s, q).wait_send()
+        gx(s).wait_send()
+        for q in (0, 1):
+            gy(s, q).wait_send()
+            for r in (0, 1):
+                gc(s, q, r).wait_send()
+        @pl.when((z < 3) & (s <= z))
+        def _():
+            gz(s, 1).wait_send()
+            for a in range(n):
+                wz(a, s, 1).wait_send()
+        @pl.when((z > 0) & (s >= z))
+        def _():
+            gz(s, 0).wait_send()
+            for a in range(n):
+                wz(a, s, 0).wait_send()
+
+def attention_layer(x_in, weights, gains, table, dy, wd, cosine, sine, cap, cid):
+    toks, width = x_in.shape
+    depth, hw = weights[0].shape
+    rows = toks // 2
+    hidden = wd.shape[0]
+    n = 6
+    f32, bf16, i32 = jnp.float32, jnp.bfloat16, jnp.int32
+    D = pltpu.SemaphoreType.DMA
+    S = jax.ShapeDtypeStruct
+    any_ = pl.BlockSpec(memory_space=pl.ANY)
+    vm = pl.BlockSpec(memory_space=pltpu.VMEM)
+    V = lambda *shape, t=bf16: pltpu.VMEM(shape, t)
+    return pl.pallas_call(
+        attention_kernel,
+        out_shape=[S((16, depth, hw), bf16)] * 4
+        + [S((32, rows, width), bf16), S((toks, width), bf16)]
+        + [S((toks, hw), bf16)] * 4
+        + [
+            S((rows, width), f32), S((rows, width), bf16), S((8, width), f32), S((16, 1, toks), i32), S((16, toks, 1), i32),
+            S((16, cap, 1), f32), S((16, cap, width), bf16), S((16, cap, hidden), f32),
+        ],
+        in_specs=[vm] * 8 + [any_] + [vm] * 2,
+        out_specs=[any_] * 5 + [vm] * 11 + [any_] * 2,
+        scratch_shapes=[
+            V(16, *gains.shape), V(16, *table.shape, t=f32), V(toks, 1, t=f32), V(3, 4, depth, hw), V(16, depth, hw), V(hidden, width),
+            V(toks, hw, t=f32), V(toks, hw, t=f32), V(toks, hw, t=f32), V(rows, width, t=f32), V(rows, width), V(rows, width),
+            V(8, toks, t=f32), V(2, 2, rows, width), V(2, cap, width), V(2 * cap, hidden, t=f32),
+            D((4,)), D((n + 1,)), D((2,)), D((2, 2)), D((2,)),
+            D((n, 4, 2)), D((n, 4)), D((n, 4)), D((n, 4)), D((n, 8)), D((n, 8)),
+            D((4, 2)), D((4,)), D((4,)), D((4,)), D((4, 2)), D((4, 2)), D((8, 2)), D((8, 2)),
+        ],
+        compiler_params=pltpu.CompilerParams(collective_id=cid, has_side_effects=True, vmem_limit_bytes=60 << 20),
+        name="attention_layer",
+    )(x_in, *weights, gains, table, dy, wd, cosine, sine)
 
 
 def on_device(
@@ -1498,27 +1446,20 @@
     rows_dev, width = tokens.shape
     topk = route_ids.shape[1]
     experts = lax.axis_size("dp")
-    splits = lax.axis_size("tensor")
-    half = rows_dev // splits
+    half = rows_dev // lax.axis_size("tensor")
     mine = lax.axis_index("tensor") * half
     capacity = rows_dev * topk * 4 // (3 * experts)
     slots = experts * capacity
-    scale = HD ** (-0.5)
     positions = jnp.arange(rows_dev, dtype=f32)
-    causal = jnp.arange(rows_dev)[:, None] >= jnp.arange(rows_dev)[None, :]
+    freqs = 10000.0 ** (-2.0 * jnp.arange(HD // 2, dtype=f32) / HD)
+    angles = positions[:, None] * freqs[None, :]
+    cosine = jnp.concatenate([jnp.cos(angles)] * 2, axis=1)
+    sine = jnp.concatenate([-jnp.sin(angles), jnp.sin(angles)], axis=1)
     grad_half = lax.dynamic_slice_in_dim(cotangent, mine, half, axis=0)
     chosen = route_ids[:, :, None] == jnp.arange(experts, dtype=jnp.int32)[None, None, :]
     table = jnp.sum(jnp.where(chosen, route_gates[:, :, None], 0.0), axis=1)
     gains = jnp.concatenate([gain_first[None], gain_second[None], jnp.zeros((14, gain_first.shape[0]), bf16)])
-    query_whole, key_whole, value_whole, output_whole, gains, tables, grad_all = start_gather(
-        [w_query, w_key, w_value, w_output, gains, table.T], grad_half, 0, "gather_weights"
-    )
-    query_whole, key_whole, value_whole, output_whole = [
-        w.reshape(width, -1) for w in (query_whole, key_whole, value_whole, output_whole)
-    ]
-    grad_all = grad_all.reshape(-1, width)
-    gain_one = gains[:, 0].reshape(-1).astype(f32)
-    gain_two = gains[:, 1].reshape(-1).astype(f32)
+    exp_gate, exp_up, exp_down = expert_gate[0].T, expert_up[0].T, expert_down[0]
 
     depth, common_width = shared_gate.shape
     common_dev = common_width // experts
@@ -1526,46 +1467,6 @@
     packed = packed.reshape(3, depth, experts, common_dev).transpose(2, 0, 1, 3)
     packed = lax.all_to_all(packed, "dp", split_axis=0, concat_axis=0, tiled=True)
     packed = packed.transpose(1, 0, 2, 3).reshape(3, width, common_dev)
-
-    table = lax.dynamic_index_in_dim(tables, lax.axis_index("dp"), axis=1, keepdims=False)
-    pick, slot_gate, held = routing_tables(table, capacity)
-
-    x_in = tokens.astype(f32)
-    act_one = rms_norm(x_in, gain_one).astype(bf16)
-    heads_dev = query_whole.shape[1] // HD
-    query_pre = jnp.dot(act_one, query_whole, preferred_element_type=f32).reshape(
-        rows_dev, heads_dev, HD
-    )
-    key_pre = jnp.dot(act_one, key_whole, preferred_element_type=f32).reshape(
-        rows_dev, heads_dev, HD
-    )
-    query_rot = rotate(query_pre, positions).astype(bf16)
-    key_rot = rotate(key_pre, positions).astype(bf16)
-    value_low = (
-        jnp.dot(act_one, value_whole, preferred_element_type=f32)
-        .astype(bf16)
-        .reshape(rows_dev, heads_dev, HD)
-    )
-    scores = masked_scores(query_rot, key_rot, causal, scale)
-    top = jnp.max(scores, axis=-1, keepdims=True)
-    expo = jnp.exp(scores - top)
-    total = jnp.sum(expo, axis=-1, keepdims=True)
-    probs = expo / total
-    mixed = jnp.einsum("hqk,khc->qhc", probs.astype(bf16), value_low, preferred_element_type=f32)
-    mixed = mixed.reshape(rows_dev, heads_dev * HD).astype(bf16)
-    attn = lax.psum_scatter(
-        contract_last(mixed, output_whole), "tensor", scatter_dimension=0, tiled=True
-    )
-    x_half = lax.dynamic_slice_in_dim(tokens, mine, half, axis=0).astype(f32)
-    x_mid = x_half + attn
-    act_two = rms_norm(x_mid, gain_two).astype(bf16)
-
-    grad_blocks = grad_all.reshape(experts, rows_dev, width)
-    exp_gate, exp_up, exp_down = expert_gate[0], expert_up[0], expert_down[0]
-    weight = slot_gate.reshape(slots, 1)
-    rows_out_grad = jnp.einsum("jst,jtd->jsd", pick, grad_blocks, preferred_element_type=f32)
-    rows_out_grad = (weight * rows_out_grad.reshape(slots, width)).astype(bf16)
-    hidden_rows_grad = contract_last(rows_out_grad, exp_down).reshape(experts, capacity, -1)
     front = capacity - 128
     back = 128 - front - common_dev
 
@@ -1574,58 +1475,52 @@
 
     common_gu = jnp.concatenate([widen(packed[0]), widen(packed[1])], axis=1)
     common_down = widen(packed[2])
-    common_hidden_grad = jnp.dot(grad_all, common_down, preferred_element_type=f32)
-    down_rows = common_down.T[front:]
+
+    (
+        query_whole, key_whole, value_whole, output_whole, grad_all, act_one, query_rot, key_rot, value_low, mixed,
+        x_mid, act_two, gain_rows, rank_row, rank_col, slot_gate, rows_out_grad, hidden_rows_grad,
+    ) = attention_layer(
+        tokens, (w_query, w_key, w_value, w_output), gains, table.T, grad_half, exp_down, cosine, sine, capacity, 0
+    )
+    weights = [w.reshape(width, -1) for w in (query_whole, key_whole, value_whole, output_whole)]
+
     total_grad, act_all, rows, hidden_rows, gate_rows_grad, up_rows_grad, common_hidden, common_gu_grad, unused, ffn = (
         expert_layer(
-            act_two,
-            hidden_rows_grad,
-            common_hidden_grad.reshape(experts, rows_dev, 128),
-            held[:, None, :],
-            held[:, :, None],
-            slot_gate[:, :, None],
-            exp_gate,
-            exp_up,
-            exp_down,
-            common_gu,
-            down_rows,
-            1,
+            act_two, hidden_rows_grad, grad_all, rank_row, rank_col, slot_gate,
+            exp_gate, exp_up, exp_down, common_gu, common_down.T[front:], common_down, 1,
         )
     )
     act_all = act_all.reshape(-1, width)
+    grad_all = grad_all.reshape(-1, width)
     rows = rows.reshape(slots, width)
+    rows_out_grad = rows_out_grad.reshape(slots, width)
     hidden_rows = hidden_rows.reshape(slots, -1)
     common_hidden = common_hidden.reshape(-1, 128)
     common_gu_grad = common_gu_grad.reshape(-1, 256)
-    expert_gate_grad = contract_first(rows, gate_rows_grad.reshape(slots, -1))[None]
-    expert_up_grad = contract_first(rows, up_rows_grad.reshape(slots, -1))[None]
-    expert_down_grad = contract_first(hidden_rows, rows_out_grad)[None]
-    gu_grad = contract_first(act_all, common_gu_grad)
-    down_grad = contract_first(grad_all, common_hidden)
+    expert_gate_grad, expert_up_grad, expert_down_grad, gu_grad, down_grad = expert_grads(
+        gate_rows_grad.reshape(slots, -1), up_rows_grad.reshape(slots, -1), hidden_rows,
+        common_gu_grad, common_hidden, rows, rows_out_grad, act_all, grad_all,
+    )
     common_w_grad = jnp.concatenate(
         [w[:, front : front + common_dev] for w in (gu_grad[:, :128], gu_grad[:, 128:], down_grad)], axis=1
     )
-    common_w_grad = common_w_grad.astype(bf16).reshape(experts, depth, 3 * common_dev)
+    common_w_grad = common_w_grad.reshape(experts, depth, 3 * common_dev)
     common_w_grad = lax.all_to_all(common_w_grad, "dp", split_axis=0, concat_axis=0, tiled=True)
-    common_w_grad = common_w_grad.astype(f32).reshape(experts, depth, 3, common_dev)
-    common_w_grad = common_w_grad.transpose(2, 1, 0, 3).reshape(3, depth, common_width)
-
-    freqs = 10000.0 ** (-2.0 * jnp.arange(HD // 2, dtype=f32) / HD)
-    angles = positions[:, None] * freqs[None, :]
-    cosine = jnp.concatenate([jnp.cos(angles)] * 2, axis=1)
-    sine = jnp.concatenate([-jnp.sin(angles), jnp.sin(angles)], axis=1)
+    common_w_grad = common_w_grad.reshape(experts, depth, 3, common_dev).transpose(2, 1, 0, 3)
+    common_w_grad = common_w_grad.reshape(3, depth, common_width).astype(f32)
+
     layer_out, tokens_grad, attn_grad, query_grad, key_grad, value_grad, gain_one_grad, gain_two_grad = attention_back(
         ffn,
         total_grad,
         x_mid,
         grad_half,
         lax.dynamic_slice_in_dim(tokens, mine, half, axis=0),
-        gain_one[None],
-        gain_two[None],
-        (query_whole, key_whole, value_whole, output_whole),
-        query_rot.reshape(rows_dev, -1),
-        key_rot.reshape(rows_dev, -1),
-        value_low.reshape(rows_dev, -1),
+        gain_rows[0:1],
+        gain_rows[1:2],
+        weights,
+        query_rot,
+        key_rot,
+        value_low,
         cosine,
         sine,
         2,
@@ -1647,9 +1542,9 @@
         common_w_grad[0],
         common_w_grad[1],
         common_w_grad[2],
-        expert_gate_grad,
-        expert_up_grad,
-        expert_down_grad,
+        expert_gate_grad.T[None],
+        expert_up_grad.T[None],
+        expert_down_grad[None],
     )
 
 

time: 910 us -> 824 us (0.905)
  matrix products: 117 us -> 0 us
  Pallas kernels: 688 us -> 753 us
  local copies, waits for them, and re-layouts: 52.7 us -> 25.8 us
  between operations: 14.7 us -> 1.31 us
  starting transfers between devices: 13.7 us -> 25.1 us
  other arithmetic: 17.7 us -> 7.26 us
    dot_general x13 -> x0, matrix products: 114 us -> none  [the longest x5 58.7 us: contract_first(): lax.dot_general(left, right, (((0,), (0,)), ((), ())), preferred_element_...]
    pallas_call x2 -> x3, Pallas kernels: 429 us -> 494 us  [the longest x1 231 us: expert_layer(): pl.pallas_call(expert_kernel, out_shape=[S((rows, width), f32), S((32, ro...]
    dot_general x2 -> x0, local copies, waits for them, and re-layouts: 12.9 us -> none  [the longest x1 6.43 us: on_device(): jnp.dot(act_one, query_whole, preferred_element_type=f32)]
    unnamed x58 -> x36, local copies, waits for them, and re-layouts: 25.2 us -> 12.3 us
    all_to_all x1, starting transfers between devices: 6.16 us -> 17.6 us  [on_device(): lax.all_to_all(common_w_grad, 'dp', split_axis=0, concat_axis=0, tiled=True)]
  transfers between devices with their start and end apart: 3 -> 2, of which waited for: 0 -> 0; matrix products, arithmetic and copies ran while one was open for 15% -> 1% of each run, Pallas kernels for 49% -> 58%
where the time goes in v3:
time: 824 us; the launch traced here: 813 us
  Pallas kernels  753 us (91%)
  local copies, waits for them, and re-layouts  25.8 us (3%)
  starting transfers between devices  25.1 us (3%)
    pallas_call x1, Pallas kernels, expert_layer(): pl.pallas_call(expert_kernel, out_shape=[S((rows, width), f32), S((32, ro...  231 us
    pallas_call x1, Pallas kernels, attention_layer(): pl.pallas_call(attention_kernel, out_shape=[S((16, depth, hw), bf16)] * 4...  216 us
    pallas_call x1, Pallas kernels, attention_back(): pl.pallas_call(attention_back_kernel, out_shape=[S((2, rows, width), bf16...  154 us
    pallas_call x1, Pallas kernels, weight_grads(): pl.pallas_call(weight_grad_kernel, out_shape=[S((depth, hw), f32)] * 4 +...  105 us
    pallas_call x1, Pallas kernels, expert_grads(): pl.pallas_call(expert_grads_kernel, grid=(width // 256,), out_shape=[S((h...  47 us
    all_to_all x1, starting transfers between devices, on_device(): lax.all_to_all(common_w_grad, 'dp', split_axis=0, concat_axis=0, tiled=True)  17.6 us
  transfers between devices with their start and end apart: 2, of which 0 were waited for; matrix products, arithmetic and copies ran while one was open for 1% of the time, Pallas kernels for 58%

profile of v3, /device:TPU:0, one launch (start us, length us, event | category | flops | bytes accessed | tf_op | source)
XLA Modules:
  0.0 812.6 jit_solution(7677778309466797844)
XLA Ops:
  0.6 1.2 copy.66
  1.8 1.2 copy.67
  3.1 1.2 copy.68
  4.4 1.1 copy.69
  5.5 7.5 all-to-all-start
  14.4 0.9 pad_maximum_fusion.1
  15.9 2.2 constant_dynamic-slice_fusion
  18.2 216.2 %attention_layer.1 = (bf16[16,128,1024]{2,1,0:T(8,128)(2,1)}, bf16[16,128,1024]{2,1,0:T(8,128)(2,1)}, bf16[16,128,1024]{2,1,0:T(8,128)(2,1)}, bf16[16,128,1024]{...) custom-call(bf16[320,2048]{1,0:T(8,128)(2,1)} %x_in.1, ...), custom_call_target="tpu_custom_call" | custom-call | tf_op jit(solution)/shard_map/attention_layer/pallas_call | solution.py:1403
  235.4 1.0 fusion.9
  236.6 1.0 copy.73.sdt_h
  237.5 1.4 fusion.2.sgu_h
  238.9 231.1 %expert_layer.1 = (f32[160,2048]{1,0:T(8,128)}, bf16[32,160,2048]{2,1,0:T(8,128)(2,1)}, bf16[16,160,2048]{2,1,0:T(8,128)(2,1)}, bf16[16,160,704]{2,1,0:T(8,128)(...) custom-call(bf16[160,2048]{1,0:T(8,128)(2,1)} %get-tuple-element.59., ...), custom_call_target="tpu_custom_call" | custom-call | tf_op jit(solution)/shard_map/expert_layer/pallas_call | solution.py:718
  470.0 47.0 %expert_grads.1 = (f32[704,2048]{1,0:T(8,128)}, f32[704,2048]{1,0:T(8,128)}, f32[704,2048]{1,0:T(8,128)}, bf16[2048,256]{1,0:T(8,128)(2,1)}, bf16[2048,128]{1,0:T(8,128)(2,1)}) custom-call(bf16[2560,704]{1,0:T(8,128)(2,1)} %bitcast.73, bf16[2560,704]{1,0:T(8,128)(2,1)} %bitcast.74, bf16[2560,704]{1,0:T(8,128)(2,1)} %bitcast.72, bf16[5120,256]{1,0:T(8,128)(2,1)} %bitcast.80, ...), custom_call_target="tpu_custom_call" | custom-call | tf_op jit(solution)/shard_map/expert_grads/pallas_call | solution.py:1119
  517.1 1.6 fusion.8
  518.9 0.8 pad_maximum_fusion
  519.7 1.5 copy.75
  521.2 17.6 %all-to-all-start.1 = ((bf16[16,128,264]{1,2,0:T(8,128)(2,1)}), bf16[16,128,264]{1,2,0:T(8,128)(2,1)}, u32[]{:S(2)}, u32[]{:S(2)}) async-start(bf16[16,128,264]{1,2,0:T(8,128)(2,1)} %copy.75), calls=%async_computation.1 | async-start | bytes 2162688 | tf_op jit(solution)/shard_map/all_to_all | solution.py:1508
  538.9 1.5 fusion.10
  540.5 153.7 %attention_back.1 = (bf16[2,160,2048]{2,1,0:T(8,128)(2,1)}, bf16[2,160,2048]{2,1,0:T(8,128)(2,1)}, bf16[2,160,2048]{2,1,0:T(8,128)(2,1)}, bf16[320,1024]{1,0:T(8...) custom-call(bf16[32,160,2048]{2,1,0:T(8,128)(2,1)} %get-tuple-element, ...), custom_call_target="tpu_custom_call" | custom-call | tf_op jit(solution)/shard_map/attention_back/pallas_call | solution.py:947
  694.2 0.8 maximum_maximum_fusion
  695.6 105.0 %weight_grads.1 = (f32[128,1024]{1,0:T(8,128)}, f32[128,1024]{1,0:T(8,128)}, f32[128,1024]{1,0:T(8,128)}, f32[128,1024]{1,0:T(8,128)}, f32[8,128]{1,0:T(8,128)}) custom-call(bf16[320,2048]{1,0:T(8,128)(2,1)} %get-tuple-element.78.a1, bf16[320,2048]{1,0:T(8,128)(2,1)} %bitcast.89, bf16[320,1024]{1,0:T(8,128)(2,1)} %get-tuple-element.80.dq, ...), custom_call_target="tpu_custom_call" | custom-call | tf_op jit(solution)/shard_map/weight_grads/pallas_call | solution.py:1088
  800.6 1.3 slice_bitcast_fusion
  801.9 1.4 convert_bitcast_fusion
  803.5 1.1 copy.78
  804.6 1.1 copy.77
  805.7 1.1 copy.76
  806.8 1.1 copy.87
  807.9 1.1 copy.88
  809.0 0.8 copy.89
  809.8 0.8 copy.90
  810.6 0.8 copy.91
  811.4 0.8 copy.92
  (43 shorter events, 4.4 us)
Async XLA Ops:
  4.4 8.7 %copy-start.8 = (f32[320,6]{0,1:T(8,128)S(1)}, f32[320,6]{0,1:T(8,128)}, u32[]{:S(2)}) copy-start(f32[320,6]{0,1:T(8,128)} %param.19) | copy-start | bytes 23044
  4.4 8.7 %copy-start.9 = (s32[320,6]{0,1:T(8,128)S(1)}, s32[320,6]{0,1:T(8,128)}, u32[]{:S(2)}) copy-start(s32[320,6]{0,1:T(8,128)} %param.18) | copy-start | bytes 23044
  5.5 9.8 %copy-start.10 = (bf16[128]{0:T(256)(128)(2,1)S(1)}, bf16[128]{0:T(256)(128)(2,1)}, u32[]{:S(2)}) copy-start(bf16[128]{0:T(256)(128)(2,1)} %param.25) | copy-start | bytes 772
  5.5 9.8 %copy-start.11 = (bf16[128]{0:T(256)(128)(2,1)S(1)}, bf16[128]{0:T(256)(128)(2,1)}, u32[]{:S(2)}) copy-start(bf16[128]{0:T(256)(128)(2,1)} %param.20) | copy-start | bytes 772
  5.5 10.4 %copy-start = (bf16[320,2048]{1,0:T(8,128)(2,1)S(1)}, bf16[320,2048]{1,0:T(8,128)(2,1)}, u32[]{:S(2)}) copy-start(bf16[320,2048]{1,0:T(8,128)(2,1)} %x_in.1) | copy-start | bytes 3932164
  5.5 228.9 %all-to-all-start = ((bf16[16,3,128,88]{2,3,1,0:T(8,128)(2,1)}), bf16[16,3,128,88]{2,3,1,0:T(8,128)(2,1)S(1)}, u32[]{:S(2)}, u32[]{:S(2)}) async-start(bf16[16,3,128,88]{2,3,1,0:T(8,128)(2,1)} %copy.69), calls=%async_computation | async-start | bytes 2162688 | tf_op jit(solution)/shard_map/all_to_all | solution.py:1468
  517.0 1.6 copy-start.7
  521.2 280.7 %all-to-all-start.1 = ((bf16[16,128,264]{1,2,0:T(8,128)(2,1)}), bf16[16,128,264]{1,2,0:T(8,128)(2,1)}, u32[]{:S(2)}, u32[]{:S(2)}) async-start(bf16[16,128,264]{1,2,0:T(8,128)(2,1)} %copy.75), calls=%async_computation.1 | async-start | bytes 2162688 | tf_op jit(solution)/shard_map/all_to_all | solution.py:1508
  803.4 3.4 copy-start.2
  805.7 2.2 copy-start.1
  806.8 2.1 copy-start.6
  807.9 1.9 copy-start.5
  807.9 2.7 copy-start.4
  809.0 2.4 copy-start.3

commit v4 on v3

--- a/solution.py
+++ b/solution.py
@@ -618,13 +618,13 @@
             last_own(2)
         @pl.when(u == 5)
         def _():
-            last_other(2); first(1); second(0)
+            last_other(2); first(1)
         @pl.when(u == 6)
         def _():
-            last_own(3)
+            last_own(3); second(0)
         @pl.when(u == 7)
         def _():
-            last_other(3); first(2); second(1); third(0)
+            last_other(3); first(2); third(0)
         unit(u)
 
     for copy in stores(7):
@@ -665,7 +665,7 @@
     for copy in out_loads(0, 0):
         copy.start()
 
-    first(3)
+    first(3); second(1)
     second(2); third(1)
     @pl.loop(0, 16)
     def _(j):
@@ -753,17 +753,17 @@
 
 def attention_back_kernel(
     part, grad2, x_mid, dy, x_in, gain1, gain2, wq_h, wk_h, wv_h, wo_h, qr, kr, vr, cosine, sine,
-    out_full, tok_full, dattn, dq, dk, dv, g1, g2,
+    out_half, tok_half, dattn, dq, dk, dv, g1, g2,
     ic, tmp, iy0, ix0, ix1, iy1, izu, izd, wa, wb, wc, dmix, dx2, da1, send1, recv1,
     wsem, ysem, ls, rcs, rcr, ry0s, ry0r, rx0s, rx0r, rx1s, rx1r, ry1s, ry1r, zus, zur, zds, zdr,
 ):
     f32, bf16 = jnp.float32, jnp.bfloat16
     z, x, y, c = place()
     rows, width = x_mid.shape
-    h = rows // 2
+    h = 48
     toks = 2 * rows
     heads = qr.shape[1] // HD
-    lo, hi = pl.ds(0, h), pl.ds(h, h)
+    lo, hi = pl.ds(0, h), pl.ds(h, rows - h)
     xn, yn, cn = dev(z, 1 - x, y, c), dev(z, x, 1 - y, c), dev(z, x, y, 1 - c)
     greet(z, x, y, c)
 
@@ -810,15 +810,15 @@
     def second(g):
         s = nearest(z, g)
         ry0(s, 1 - x).wait_recv(); add(at(s, 1 - x, y), 0, h, iy0, s * 2 + 1 - x); rx0(s).start()
-        rx1(s, 1 - y).wait_recv(); add(at(s, x, 1 - y), h, h, ix1, s * 2 + 1 - y); ry1(s).start()
+        rx1(s, 1 - y).wait_recv(); add(at(s, x, 1 - y), h, rows - h, ix1, s * 2 + 1 - y); ry1(s).start()
         ry0(s, x).wait_recv(); add(at(s, x, y), 0, h, iy0, s * 2 + x)
-        rx1(s, y).wait_recv(); add(at(s, x, y), h, h, ix1, s * 2 + y)
+        rx1(s, y).wait_recv(); add(at(s, x, y), h, rows - h, ix1, s * 2 + y)
 
     def third(g):
         s = nearest(z, g)
         me = at(s, x, y)
         rx0(s).wait_recv(); add(me, 0, h, ix0, s)
-        ry1(s).wait_recv(); add(me, h, h, iy1, s)
+        ry1(s).wait_recv(); add(me, h, rows - h, iy1, s)
         @pl.when((s >= z) & (z > 0))
         def _():
             zu(s).wait_recv(); add(me, 0, rows, izu, s)
@@ -848,7 +848,7 @@
     def _(r):
         q = pl.ds(pl.multiple_of(r * 16, 16), 16)
         back, terms = norm_back(x_mid[q], gain2[...], grad2[q])
-        back = back + dy[q].astype(f32)
+        back = back + dy[pl.ds(pl.multiple_of(y * rows + r * 16, 16), 16)].astype(f32)
         dx2[q] = back
         dattn[y, q] = back.astype(bf16)
         g2[...] += jnp.sum(terms, axis=0, keepdims=True)
@@ -907,21 +907,17 @@
     @pl.loop(0, rows // 16)
     def _(r):
         q = pl.ds(pl.multiple_of(r * 16, 16), 16)
-        back, terms = norm_back(x_in[q].astype(f32), gain1[...], da1[y, q] + recv1[q].astype(f32))
-        tok_full[y, q] = (back + dx2[q]).astype(bf16)
+        back, terms = norm_back(
+            x_in[pl.ds(pl.multiple_of(y * rows + r * 16, 16), 16)].astype(f32), gain1[...], da1[y, q] + recv1[q].astype(f32)
+        )
+        tok_half[q] = (back + dx2[q]).astype(bf16)
         g1[...] += jnp.sum(terms, axis=0, keepdims=True)
-    tok_swap = rcopy(tok_full.at[y], tok_full.at[y], ysem.at[4], ysem.at[5], yn)
-    tok_swap.start()
     second(0); third(1); third(0)
     @pl.loop(0, rows // 16)
     def _(r):
         q = pl.ds(pl.multiple_of(r * 16, 16), 16)
-        out_full[y, q] = (x_mid[q] + ic[at(z, x, y), q].astype(f32)).astype(bf16)
-    out_swap = rcopy(out_full.at[y], out_full.at[y], ysem.at[6], ysem.at[7], yn)
-    out_swap.start()
-    tok_swap.wait_recv()
-    out_swap.wait_recv()
-    for swap in (attn_swap, da1_swap, tok_swap, out_swap):
+        out_half[q] = (x_mid[q] + ic[at(z, x, y), q].astype(f32)).astype(bf16)
+    for swap in (attn_swap, da1_swap):
         swap.wait_send()
     for s in range(4):
         rx0(s).wait_send(); ry1(s).wait_send()
@@ -937,7 +933,7 @@
 def attention_back(part, grad2, x_mid, dy, x_in, gain1, gain2, weights, qr, kr, vr, cosine, sine, cid):
     rows, width = x_mid.shape
     toks, hw = qr.shape
-    h = rows // 2
+    h = 48
     f32, bf16 = jnp.float32, jnp.bfloat16
     D = pltpu.SemaphoreType.DMA
     S = jax.ShapeDtypeStruct
@@ -947,17 +943,17 @@
     return pl.pallas_call(
         attention_back_kernel,
         out_shape=[
-            S((2, rows, width), bf16), S((2, rows, width), bf16), S((2, rows, width), bf16),
+            S((rows, width), bf16), S((rows, width), bf16), S((2, rows, width), bf16),
             S((toks, hw), bf16), S((toks, hw), bf16), S((toks, hw), bf16), S((1, width), f32), S((1, width), f32),
         ],
         in_specs=[any_] + [vm] * 6 + [any_] * 4 + [vm] * 5,
         out_specs=[vm] * 8,
         scratch_shapes=[
-            V(16, rows, width), V(4, rows, width), V(8, h, width), V(4, h, width), V(8, h, width), V(4, h, width),
+            V(16, rows, width), V(4, rows, width), V(8, h, width), V(4, h, width), V(8, rows - h, width), V(4, rows - h, width),
             V(4, rows, width), V(4, rows, width),
             V(width, hw), V(width, hw), V(width, hw), V(toks, hw), V(rows, width, t=f32), V(2, rows, width, t=f32),
             V(rows, width), V(rows, width),
-            D((4,)), D((8,)), D((4,)), D((16,)), D((16,)), D((4, 2)), D((4, 2)), D((4,)), D((4,)), D((4, 2)), D((4, 2)), D((4,)), D((4,)),
+            D((4,)), D((4,)), D((4,)), D((16,)), D((16,)), D((4, 2)), D((4, 2)), D((4,)), D((4,)), D((4, 2)), D((4, 2)), D((4,)), D((4,)),
             D((4,)), D((4,)), D((4,)), D((4,)),
         ],
         compiler_params=pltpu.CompilerParams(collective_id=cid, has_side_effects=True, vmem_limit_bytes=63 << 20),
@@ -965,10 +961,10 @@
     )(part, grad2, x_mid, dy, x_in, gain1, gain2, *weights, qr, kr, vr, cosine, sine)
 
 def weight_grad_kernel(
-    a1, dattn, dq, dk, dv, mixed, gains,
-    oq, ok, ov, oo, og,
+    a1, dattn, dq, dk, dv, mixed, gains, out_half, tok_half,
+    oq, ok, ov, oo, og, out_full, tok_full,
     acc, ic, ix, izu, izd, gc, gx, gu, gd, gy, gbuf,
-    cs, cr, xs, xr, zus, zur, zds, zdr, gss, gsr,
+    cs, cr, xs, xr, zus, zur, zds, zdr, gss, gsr, fsem,
 ):
     f32, bf16 = jnp.float32, jnp.bfloat16
     z, x, y, c = place()
@@ -1026,8 +1022,15 @@
     g_u = rcopy(gu.at[1], gu.at[0], gss.at[2], gsr.at[2], dev(z + 1, x, y, c))
     g_d = rcopy(gd.at[1], gd.at[0], gss.at[3], gsr.at[3], dev(z - 1, x, y, c))
     g_y = rcopy(gy.at[0], gy.at[1], gss.at[4], gsr.at[4], yn)
+    swaps = [
+        rcopy(a, b.at[y], fsem.at[i], fsem.at[i + 2], yn) for i, (a, b) in enumerate(((out_half, out_full), (tok_half, tok_full)))
+    ]
     g_c.start()
     make(3); make(2)
+    for swap in swaps:
+        swap.start()
+    out_full[y] = out_half[...]
+    tok_full[y] = tok_half[...]
     g_c.wait_recv()
     gbuf[...] = gains[c] + gc[...]
     g_x.start()
@@ -1062,6 +1065,8 @@
         outs[a][...] = acc[a, pos(z, x, c)].astype(f32)
     g_y.wait_recv()
     og[...] = gy[0] + gy[1]
+    for swap in swaps:
+        swap.wait()
     g_c.wait_send(); g_x.wait_send(); g_y.wait_send()
     @pl.when(z < 3)
     def _(): g_u.wait_send()
@@ -1076,7 +1081,7 @@
             @pl.when(s < z)
             def _(): zd(a, s).wait_send()
 
-def weight_grads(a1, dattn, dq, dk, dv, mixed, gains, cid):
+def weight_grads(a1, dattn, dq, dk, dv, mixed, gains, out_half, tok_half, cid):
     toks, width = a1.shape
     hw = dq.shape[1]
     depth = width // 16
@@ -1087,17 +1092,17 @@
     V = lambda *shape, t=bf16: pltpu.VMEM(shape, t)
     return pl.pallas_call(
         weight_grad_kernel,
-        out_shape=[S((depth, hw), f32)] * 4 + [S((8, 128), f32)],
-        in_specs=[vm] * 7,
-        out_specs=[vm] * 5,
+        out_shape=[S((depth, hw), f32)] * 4 + [S((8, 128), f32)] + [S((2,) + out_half.shape, bf16)] * 2,
+        in_specs=[vm] * 9,
+        out_specs=[vm] * 7,
         scratch_shapes=[
             V(4, 16, depth, hw), V(4, 8, depth, hw), V(4, 4, depth, hw), V(4, 4, depth, hw), V(4, 4, depth, hw),
             V(2, 4, 8, 128, t=f32), V(4, 8, 128, t=f32), V(2, 4, 8, 128, t=f32), V(2, 4, 8, 128, t=f32), V(2, 8, 128, t=f32), V(2, 4, 8, 128, t=f32),
-            D((4, 8)), D((4, 8)), D((4, 4)), D((4, 4)), D((4, 4)), D((4, 4)), D((4, 4)), D((4, 4)), D((5,)), D((5,)),
+            D((4, 8)), D((4, 8)), D((4, 4)), D((4, 4)), D((4, 4)), D((4, 4)), D((4, 4)), D((4, 4)), D((5,)), D((5,)), D((4,)),
         ],
         compiler_params=pltpu.CompilerParams(collective_id=cid, has_side_effects=True, vmem_limit_bytes=60 << 20),
         name="weight_grads",
-    )(a1, dattn, dq, dk, dv, mixed, gains)
+    )(a1, dattn, dq, dk, dv, mixed, gains, out_half, tok_half)
 
 
 def expert_grads_kernel(deg, deu, eh, dsgu, hs, rows, deo, act, dy, e_gate, e_up, e_down, gu, down):
@@ -1147,7 +1152,8 @@
     n = len(outs)
     def pos(s, xx, cc): return (s * 2 + xx) * 2 + cc
     owns = [pltpu.make_async_copy(ins[a], outs[a].at[expert], lsem.at[a]) for a in range(n)]
-    owns.append(pltpu.make_async_copy(dy_in, dy_all.at[blk(z, x, y, c)], lsem.at[n]))
+    own_rows = pl.ds(pl.multiple_of(y * rows, rows), rows)
+    owns.append(pltpu.make_async_copy(dy_in.at[own_rows], dy_all.at[blk(z, x, y, c)], lsem.at[n]))
     for o in owns:
         o.start()
     w_down = pltpu.make_async_copy(wd_h, wd, wsem.at[3])
@@ -1162,18 +1168,23 @@
     def wc(a, s, xx):
         r = outs[a].at[pos(s, xx, c)]
         return rcopy(r, r, cs.at[a, s * 2 + xx], cr.at[a, s * 2 + xx], cn)
-    def gz(s, up):
-        r = dy_all.at[blk(s, x, y, c)]
-        return rcopy(r, r, gzs.at[s, up], gzr.at[s], dev(z + 2 * up - 1, x, y, c))
-    def gx(s):
-        r = dy_all.at[blk(s, x, y, c)]
-        return rcopy(r, r, gxs.at[s], gxr.at[s], xn)
-    def gy(s, xx):
-        r = dy_all.at[blk(s, xx, y, c)]
-        return rcopy(r, r, gys.at[s, xx], gyr.at[s, xx], yn)
-    def gc(s, xx, yy):
-        r = dy_all.at[blk(s, xx, yy, c)]
-        return rcopy(r, r, gcs.at[s * 2 + xx, yy], gcr.at[s * 2 + xx, yy], cn)
+    half = rows - 48
+    halves = (pl.ds(0, half), pl.ds(half, rows - half))
+    def piece(s, xx, yy, p):
+        return dy_all.at[blk(s, xx, yy, c), halves[p]]
+    def gz(s, xx, p, up):
+        r = piece(s, xx, y, p)
+        i = 0 if p == 0 else 1 + xx
+        return rcopy(r, r, gzs.at[i, s, up], gzr.at[i, s], dev(z + 2 * up - 1, x, y, c))
+    def gx(s, p):
+        r = piece(s, x, y, p)
+        return rcopy(r, r, gxs.at[p, s], gxr.at[p, s], xn)
+    def gy(s, xx, p):
+        r = piece(s, xx, y, p)
+        return rcopy(r, r, gys.at[p, s, xx], gyr.at[p, s, xx], yn)
+    def gc(s, xx, yy, p):
+        r = piece(s, xx, yy, p)
+        return rcopy(r, r, gcs.at[p, s * 2 + xx, yy], gcr.at[p, s * 2 + xx, yy], cn)
 
     def column(s):
         for a in range(n):
@@ -1182,15 +1193,17 @@
         s = nearest(z, g)
         for a in range(n):
             wx(a, s).wait_recv(); wc(a, s, 1 - x).start()
-    def gcolumn(s):
-        gx(s).start(); gy(s, x).start(); gc(s, x, y).start()
+    def gspread(s, xx, p):
+        gy(s, xx, p).start(); gc(s, xx, y, p).start()
     def gmiddle(g):
         s = nearest(z, g)
-        gx(s).wait_recv(); gy(s, 1 - x).start(); gc(s, 1 - x, y).start()
+        gx(s, 0).wait_recv()
+        gspread(s, 1 - x, 0)
     def glast(g):
         s = nearest(z, g)
         for q in (0, 1):
-            gy(s, q).wait_recv(); gc(s, q, 1 - y).start()
+            for p in (0, 1):
+                gy(s, q, p).wait_recv(); gc(s, q, 1 - y, p).start()
     def launch(fn):
         @pl.when(z < 3)
         def _(): fn(1)
@@ -1210,10 +1223,13 @@
         column(s)
     def garrive(g):
         s, up, more = towards(g)
-        gz(s, up).wait_recv()
-        @pl.when(more)
-        def _(): gz(s, up).start()
-        gcolumn(s)
+        for xx, p in ((x, 0), (x, 1), (1 - x, 1)):
+            gz(s, xx, p, up).wait_recv()
+            @pl.when(more)
+            def _(): gz(s, xx, p, up).start()
+            if p == 0:
+                gx(s, 0).start()
+            gspread(s, xx, p)
 
     def project(g):
         s = nearest(z, g)
@@ -1269,7 +1285,8 @@
         ranks_of(g)
         for xx in (0, 1):
             for yy in (0, 1):
-                gc(s, xx, yy).wait_recv()
+                for p in (0, 1):
+                    gc(s, xx, yy, p).wait_recv()
         @pl.loop(0, 2)
         def _(xx):
             base = (s * 2 + xx) * 2
@@ -1300,10 +1317,13 @@
 
     for o in owns:
         o.wait()
+    gx(z, 1).start()
     launch(lambda up: [wz(a, z, up).start() for a in range(n)])
     column(z)
-    launch(lambda up: gz(z, up).start())
-    gcolumn(z)
+    launch(lambda up: gz(z, x, 0, up).start())
+    launch(lambda up: gz(z, x, 1, up).start())
+    gx(z, 0).start()
+    gspread(z, x, 0); gspread(z, x, 1)
     @pl.loop(0, toks // 16)
     def _(r):
         q = pl.ds(pl.multiple_of(r * 16, 16), 16)
@@ -1311,6 +1331,9 @@
         inv[q] = lax.rsqrt(jnp.sum(v * v, axis=1, keepdims=True) * (1.0 / width) + EPS)
     gm[...] = jnp.zeros_like(gm)
     w_down.wait()
+    gx(z, 1).wait_recv()
+    launch(lambda up: gz(z, 1 - x, 1, up).start())
+    gspread(z, 1 - x, 1)
     arrive(1); middle(0); project(0)
     garrive(1); gmiddle(0)
     arrive(2); middle(1); project(1)
@@ -1367,24 +1390,28 @@
     for copy in stores(3, 1):
         copy.wait()
     swap.wait_send()
+    gx(z, 1).wait_send()
     for s in range(4):
         for a in range(n):
             wx(a, s).wait_send()
             for q in (0, 1):
                 wc(a, s, q).wait_send()
-        gx(s).wait_send()
+        gx(s, 0).wait_send()
         for q in (0, 1):
-            gy(s, q).wait_send()
-            for r in (0, 1):
-                gc(s, q, r).wait_send()
+            for p in (0, 1):
+                gy(s, q, p).wait_send()
+                for r in (0, 1):
+                    gc(s, q, r, p).wait_send()
         @pl.when((z < 3) & (s <= z))
         def _():
-            gz(s, 1).wait_send()
+            for xx, p in ((x, 0), (x, 1), (1 - x, 1)):
+                gz(s, xx, p, 1).wait_send()
             for a in range(n):
                 wz(a, s, 1).wait_send()
         @pl.when((z > 0) & (s >= z))
         def _():
-            gz(s, 0).wait_send()
+            for xx, p in ((x, 0), (x, 1), (1 - x, 1)):
+                gz(s, xx, p, 0).wait_send()
             for a in range(n):
                 wz(a, s, 0).wait_send()
 
@@ -1417,7 +1444,7 @@
             V(8, toks, t=f32), V(2, 2, rows, width), V(2, cap, width), V(2 * cap, hidden, t=f32),
             D((4,)), D((n + 1,)), D((2,)), D((2, 2)), D((2,)),
             D((n, 4, 2)), D((n, 4)), D((n, 4)), D((n, 4)), D((n, 8)), D((n, 8)),
-            D((4, 2)), D((4,)), D((4,)), D((4,)), D((4, 2)), D((4, 2)), D((8, 2)), D((8, 2)),
+            D((3, 4, 2)), D((3, 4)), D((2, 4)), D((2, 4)), D((2, 4, 2)), D((2, 4, 2)), D((2, 8, 2)), D((2, 8, 2)),
         ],
         compiler_params=pltpu.CompilerParams(collective_id=cid, has_side_effects=True, vmem_limit_bytes=60 << 20),
         name="attention_layer",
@@ -1446,8 +1473,6 @@
     rows_dev, width = tokens.shape
     topk = route_ids.shape[1]
     experts = lax.axis_size("dp")
-    half = rows_dev // lax.axis_size("tensor")
-    mine = lax.axis_index("tensor") * half
     capacity = rows_dev * topk * 4 // (3 * experts)
     slots = experts * capacity
     positions = jnp.arange(rows_dev, dtype=f32)
@@ -1455,7 +1480,6 @@
     angles = positions[:, None] * freqs[None, :]
     cosine = jnp.concatenate([jnp.cos(angles)] * 2, axis=1)
     sine = jnp.concatenate([-jnp.sin(angles), jnp.sin(angles)], axis=1)
-    grad_half = lax.dynamic_slice_in_dim(cotangent, mine, half, axis=0)
     chosen = route_ids[:, :, None] == jnp.arange(experts, dtype=jnp.int32)[None, None, :]
     table = jnp.sum(jnp.where(chosen, route_gates[:, :, None], 0.0), axis=1)
     gains = jnp.concatenate([gain_first[None], gain_second[None], jnp.zeros((14, gain_first.shape[0]), bf16)])
@@ -1480,7 +1504,7 @@
         query_whole, key_whole, value_whole, output_whole, grad_all, act_one, query_rot, key_rot, value_low, mixed,
         x_mid, act_two, gain_rows, rank_row, rank_col, slot_gate, rows_out_grad, hidden_rows_grad,
     ) = attention_layer(
-        tokens, (w_query, w_key, w_value, w_output), gains, table.T, grad_half, exp_down, cosine, sine, capacity, 0
+        tokens, (w_query, w_key, w_value, w_output), gains, table.T, cotangent, exp_down, cosine, sine, capacity, 0
     )
     weights = [w.reshape(width, -1) for w in (query_whole, key_whole, value_whole, output_whole)]
 
@@ -1513,8 +1537,8 @@
         ffn,
         total_grad,
         x_mid,
-        grad_half,
-        lax.dynamic_slice_in_dim(tokens, mine, half, axis=0),
+        cotangent,
+        tokens,
         gain_rows[0:1],
         gain_rows[1:2],
         weights,
@@ -1527,8 +1551,8 @@
     )
     gains = jnp.concatenate([gain_one_grad, gain_two_grad, jnp.zeros((6, width), f32)])
     gains = gains.reshape(8, 4, 2, 2, width // 16).transpose(3, 2, 1, 0, 4)
-    query_sum, key_sum, value_sum, output_sum, gain_grads = weight_grads(
-        act_one, attn_grad.reshape(rows_dev, width), query_grad, key_grad, value_grad, mixed, gains, 4
+    query_sum, key_sum, value_sum, output_sum, gain_grads, layer_out, tokens_grad = weight_grads(
+        act_one, attn_grad.reshape(rows_dev, width), query_grad, key_grad, value_grad, mixed, gains, layer_out, tokens_grad, 4
     )
     return (
         layer_out.reshape(rows_dev, width),

time: 824 us -> 785 us (0.953)
  Pallas kernels: 753 us -> 723 us
    pallas_call x1, Pallas kernels: 154 us -> 128 us  [attention_back(): pl.pallas_call(attention_back_kernel, out_shape=[S((rows, width), bf16),...]
    pallas_call x1, Pallas kernels: 216 us -> 208 us  [attention_layer(): pl.pallas_call(attention_kernel, out_shape=[S((16, depth, hw), bf16)] * 4...]
  transfers between devices with their start and end apart: 2 -> 2, of which waited for: 0 -> 0; matrix products, arithmetic and copies ran while one was open for 1% -> 1% of each run, Pallas kernels for 58% -> 57%
where the time goes in v4:
time: 785 us; the launch traced here: 774 us
  Pallas kernels  723 us (92%)
  local copies, waits for them, and re-layouts  23.6 us (3%)
  starting transfers between devices  18.5 us (2%)
    pallas_call x1, Pallas kernels, expert_layer(): pl.pallas_call(expert_kernel, out_shape=[S((rows, width), f32), S((32, ro...  234 us
    pallas_call x1, Pallas kernels, attention_layer(): pl.pallas_call(attention_kernel, out_shape=[S((16, depth, hw), bf16)] * 4...  208 us
    pallas_call x1, Pallas kernels, attention_back(): pl.pallas_call(attention_back_kernel, out_shape=[S((rows, width), bf16),...  128 us
    pallas_call x1, Pallas kernels, weight_grads(): pl.pallas_call(weight_grad_kernel, out_shape=[S((depth, hw), f32)] * 4 +...  107 us
    pallas_call x1, Pallas kernels, expert_grads(): pl.pallas_call(expert_grads_kernel, grid=(width // 256,), out_shape=[S((h...  47 us
  transfers between devices with their start and end apart: 2, of which 0 were waited for; matrix products, arithmetic and copies ran while one was open for 1% of the time, Pallas kernels for 57%

profile of v4, /device:TPU:0, one launch (start us, length us, event | category | flops | bytes accessed | tf_op | source)
XLA Modules:
  0.0 774.0 jit_solution(9383768046695450502)
XLA Ops:
  0.6 1.2 copy.66
  1.8 1.2 copy.67
  3.1 1.2 copy.68
  4.4 1.1 copy.69
  5.5 7.5 all-to-all-start
  14.3 0.9 pad_maximum_fusion.1
  15.2 0.7 maximum_maximum_fusion.1.gain_in
  15.9 207.8 %attention_layer.1 = (bf16[16,128,1024]{2,1,0:T(8,128)(2,1)}, bf16[16,128,1024]{2,1,0:T(8,128)(2,1)}, bf16[16,128,1024]{2,1,0:T(8,128)(2,1)}, bf16[16,128,1024]{...) custom-call(bf16[320,2048]{1,0:T(8,128)(2,1)} %x_in.3, ...), custom_call_target="tpu_custom_call" | custom-call | tf_op jit(solution)/shard_map/attention_layer/pallas_call | solution.py:1430
  224.7 1.0 fusion.9
  225.9 1.0 copy.73.sdt_h
  226.8 1.4 fusion.2.sgu_h
  228.2 234.4 %expert_layer.1 = (f32[160,2048]{1,0:T(8,128)}, bf16[32,160,2048]{2,1,0:T(8,128)(2,1)}, bf16[16,160,2048]{2,1,0:T(8,128)(2,1)}, bf16[16,160,704]{2,1,0:T(8,128)(...) custom-call(bf16[160,2048]{1,0:T(8,128)(2,1)} %get-tuple-element.62., ...), custom_call_target="tpu_custom_call" | custom-call | tf_op jit(solution)/shard_map/expert_layer/pallas_call | solution.py:718
  462.6 47.0 %expert_grads.1 = (f32[704,2048]{1,0:T(8,128)}, f32[704,2048]{1,0:T(8,128)}, f32[704,2048]{1,0:T(8,128)}, bf16[2048,256]{1,0:T(8,128)(2,1)}, bf16[2048,128]{1,0:T(8,128)(2,1)}) custom-call(bf16[2560,704]{1,0:T(8,128)(2,1)} %bitcast.73, bf16[2560,704]{1,0:T(8,128)(2,1)} %bitcast.74, bf16[2560,704]{1,0:T(8,128)(2,1)} %bitcast.72, bf16[5120,256]{1,0:T(8,128)(2,1)} %bitcast.80, ...), custom_call_target="tpu_custom_call" | custom-call | tf_op jit(solution)/shard_map/expert_grads/pallas_call | solution.py:1124
  509.6 1.6 fusion.8
  511.4 0.8 pad_maximum_fusion
  512.2 1.5 copy.75
  513.8 11.0 %all-to-all-start.1 = ((bf16[16,128,264]{1,2,0:T(8,128)(2,1)}), bf16[16,128,264]{1,2,0:T(8,128)(2,1)}, u32[]{:S(2)}, u32[]{:S(2)}) async-start(bf16[16,128,264]{1,2,0:T(8,128)(2,1)} %copy.75), calls=%async_computation.1 | async-start | bytes 2162688 | tf_op jit(solution)/shard_map/all_to_all | solution.py:1532
  524.9 1.5 fusion.10
  526.4 127.6 %attention_back.1 = (bf16[160,2048]{1,0:T(8,128)(2,1)}, bf16[160,2048]{1,0:T(8,128)(2,1)}, bf16[2,160,2048]{2,1,0:T(8,128)(2,1)}, bf16[320,1024]{1,0:T(8,128)(2,...) custom-call(bf16[32,160,2048]{2,1,0:T(8,128)(2,1)} %get-tuple-element.68.part, ...), custom_call_target="tpu_custom_call" | custom-call | tf_op jit(solution)/shard_map/attention_back/pallas_call | solution.py:943
  654.0 0.8 maximum_maximum_fusion
  655.4 106.7 %weight_grads.1 = (f32[128,1024]{1,0:T(8,128)}, f32[128,1024]{1,0:T(8,128)}, f32[128,1024]{1,0:T(8,128)}, f32[128,1024]{1,0:T(8,128)}, f32[8,128]{1,0:T(8,128)},...) custom-call(bf16[320,2048]{1,0:T(8,128)(2,1)} %get-tuple-element.61.a1, bf16[320,2048]{1,0:T(8,128)(2,1)} %bitcast.87, ...), custom_call_target="tpu_custom_call" | custom-call | tf_op jit(solution)/shard_map/weight_grads/pallas_call | solution.py:1093
  762.1 1.3 slice_bitcast_fusion
  763.4 1.4 convert_bitcast_fusion
  764.9 1.1 copy.78
  766.0 1.1 copy.77
  767.2 1.1 copy.76
  768.3 1.1 copy.87
  769.4 1.1 copy.88
  770.4 0.8 copy.89
  771.2 0.8 copy.90
  772.0 0.8 copy.91
  772.8 0.8 copy.92
  (40 shorter events, 3.7 us)
Async XLA Ops:
  4.4 8.7 %copy-start.7 = (f32[320,6]{0,1:T(8,128)S(1)}, f32[320,6]{0,1:T(8,128)}, u32[]{:S(2)}) copy-start(f32[320,6]{0,1:T(8,128)} %param.19) | copy-start | bytes 23044
  4.4 8.7 %copy-start.8 = (s32[320,6]{0,1:T(8,128)S(1)}, s32[320,6]{0,1:T(8,128)}, u32[]{:S(2)}) copy-start(s32[320,6]{0,1:T(8,128)} %param.18) | copy-start | bytes 23044
  5.5 9.7 %copy-start.9 = (bf16[128]{0:T(256)(128)(2,1)S(1)}, bf16[128]{0:T(256)(128)(2,1)}, u32[]{:S(2)}) copy-start(bf16[128]{0:T(256)(128)(2,1)} %param.25) | copy-start | bytes 772
  5.5 9.7 %copy-start.10 = (bf16[128]{0:T(256)(128)(2,1)S(1)}, bf16[128]{0:T(256)(128)(2,1)}, u32[]{:S(2)}) copy-start(bf16[128]{0:T(256)(128)(2,1)} %param.20) | copy-start | bytes 772
  5.5 218.2 %all-to-all-start = ((bf16[16,3,128,88]{2,3,1,0:T(8,128)(2,1)}), bf16[16,3,128,88]{2,3,1,0:T(8,128)(2,1)S(1)}, u32[]{:S(2)}, u32[]{:S(2)}) async-start(bf16[16,3,128,88]{2,3,1,0:T(8,128)(2,1)} %copy.69), calls=%async_computation | async-start | bytes 2162688 | tf_op jit(solution)/shard_map/all_to_all | solution.py:1492
  509.6 1.6 copy-start.6
  513.8 249.6 %all-to-all-start.1 = ((bf16[16,128,264]{1,2,0:T(8,128)(2,1)}), bf16[16,128,264]{1,2,0:T(8,128)(2,1)}, u32[]{:S(2)}, u32[]{:S(2)}) async-start(bf16[16,128,264]{1,2,0:T(8,128)(2,1)} %copy.75), calls=%async_computation.1 | async-start | bytes 2162688 | tf_op jit(solution)/shard_map/all_to_all | solution.py:1532
  764.9 3.4 copy-start.1
  767.2 2.2 copy-start
  768.3 2.1 copy-start.5
  769.4 1.9 copy-start.4
  769.4 2.7 copy-start.3
  770.4 2.4 copy-start.2

commit v5 on v4

--- a/solution.py
+++ b/solution.py
@@ -336,10 +336,10 @@
 
 def expert_kernel(
     a_in, deh, dy_all, rank_row, rank_col, gate, wg_h, wu_h, wd_h, sgu_h, sdt_h, sd_h,
-    total, act_all, rows_o, eh_o, deg_o, deu_o, hs_o, dsgu_o, part, ffn_part,
+    total, act_all, rows_o, eh_o, deg_o, deu_o, hs_o, dsgu_o, part, ffn_part, gu_o, down_o,
     wg, wu, wd, sgu, tail, acc, ic, iy0, ix0, ix1, iy1, iz,
-    eg, eu, dehb, ehb, degb, deub, sd, dhs, hsb, dsgub, eh2, hs2, ot,
-    wsem, usem, ssem, osem, psem, lsem,
+    eg, eu, dehb, ehb, degb, deub, sd, dhs, hsb, dsgub, eh2, hs2, ot, gub, downb,
+    wsem, usem, ssem, osem, psem, lsem, tsem, gsem, fsem,
     zs, zr, x0s, x0r, x1s, x1r, y0s, y0r, y1s, y1r, cs, cr,
     ls, rcs, rcr, ry0s, ry0r, rx0s, rx0r, rx1s, rx1r, ry1s, ry1r, rzs, rzr,
 ):
@@ -432,8 +432,8 @@
                 pltpu.make_async_copy(ehb.at[r], eh_o.at[j], ssem.at[k, 1]),
                 pltpu.make_async_copy(degb.at[r], deg_o.at[j], ssem.at[k, 2]),
                 pltpu.make_async_copy(deub.at[r], deu_o.at[j], ssem.at[k, 3]),
-                pltpu.make_async_copy(hsb.at[k], hs_o.at[j], ssem.at[k, 4]),
-                pltpu.make_async_copy(dsgub.at[k], dsgu_o.at[j], ssem.at[k, 5]),
+                pltpu.make_async_copy(hsb.at[pl.ds(2 * k, 2)], hs_o.at[pl.ds(2 * j, 2)], ssem.at[k, 4]),
+                pltpu.make_async_copy(dsgub.at[pl.ds(2 * k, 2)], dsgu_o.at[pl.ds(2 * j, 2)], ssem.at[k, 5]),
             ]
         return out
 
@@ -493,9 +493,9 @@
             gp, up = pre[:, :128], pre[:, 128:]
             dh = dhs[base + k]
             sig = jax.nn.sigmoid(gp)
-            hsb[k] = (gp * sig * up).astype(bf16)
-            dsgub[k, :, 0:128] = (dh * up * sig * (1.0 + gp * (1.0 - sig))).astype(bf16)
-            dsgub[k, :, 128:256] = (dh * gp * sig).astype(bf16)
+            hsb[2 * k:2 * k + 2] = (gp * sig * up).astype(bf16).reshape(2, rows, 128)
+            dsgub[2 * k:2 * k + 2, :, 0:128] = (dh * up * sig * (1.0 + gp * (1.0 - sig))).astype(bf16).reshape(2, rows, 128)
+            dsgub[2 * k:2 * k + 2, :, 128:256] = (dh * gp * sig).astype(bf16).reshape(2, rows, 128)
         picked = acc[0:2].reshape(2 * cap, width)
         eg[...] = nt(picked, wg[...])
         eu[...] = nt(picked, wu[...])
@@ -521,7 +521,7 @@
             left = jnp.concatenate([one, two], axis=1)[:, :cap].astype(bf16)
             for n in range(0, width, 512):
                 w = pl.ds(n, 512)
-                out = nn(left, acc[8 + k, :, w]) + nt(dsgub[k], sgu[w, :])
+                out = nn(left, acc[8 + k, :, w]) + nt(dsgub[2 * k:2 * k + 2].reshape(toks, 256), sgu[w, :])
                 out = out.astype(bf16)
                 acc[10 + 2 * k, :, w] = out[:rows]
                 acc[11 + 2 * k, :, w] = out[rows:]
@@ -634,7 +634,7 @@
     def out_loads(j, b):
         return [
             pltpu.make_async_copy(eh_o.at[j], eh2.at[b], osem.at[b, 0]),
-            pltpu.make_async_copy(hs_o.at[j], hs2.at[b], osem.at[b, 1]),
+            pltpu.make_async_copy(hs_o.at[pl.ds(2 * j, 2)], hs2.at[b], osem.at[b, 1]),
         ]
     def out_store(j, b):
         return pltpu.make_async_copy(ot.at[b], ffn_part.at[pl.ds(2 * j, 2)], psem.at[b])
@@ -654,7 +654,7 @@
             w = pl.ds(n, 512)
             tail[0:cap, w] = (nn(eh2[b], wd[:, w]) * weight).astype(bf16)
         one, two = spread_cols(j)
-        left = jnp.concatenate([one, two + hs2[b].astype(f32)], axis=1).astype(bf16)
+        left = jnp.concatenate([one, two + hs2[b].reshape(toks, 128).astype(f32)], axis=1).astype(bf16)
         for n in range(0, width, 512):
             w = pl.ds(n, 512)
             out = nn(left, tail[:, w]).astype(bf16)
@@ -667,14 +667,72 @@
 
     first(3); second(1)
     second(2); third(1)
-    @pl.loop(0, 16)
-    def _(j):
-        @pl.when(j == 4)
+    def tn(left, right):
+        return lax.dot_general(left, right, (((0,), (0,)), ((), ())), preferred_element_type=f32)
+    def flat(first, count):
+        return acc[:, :, first:first + count].reshape(16 * rows, count)
+    fixed = []
+    for q in (0, 1):
+        half = pl.ds(16 * q, 16)
+        fixed.append(pltpu.make_async_copy(dsgu_o.at[half], acc.at[:, :, pl.ds(256 * q, 256)], fsem.at[q]))
+        fixed.append(pltpu.make_async_copy(hs_o.at[half], acc.at[:, :, pl.ds(512 + 128 * q, 128)], fsem.at[2 + q]))
+    def feature(i, b):
+        return pl.ds(pl.multiple_of(lax.rem(2 * i + b, 8) * 256, 256), 256)
+    def tile_load(source, i, b):
+        return [
+            pltpu.make_async_copy(
+                source.at[pl.ds(16 * q, 16), :, feature(i, b)], acc.at[:, :, pl.ds(768 + 512 * b + 256 * q, 256)], tsem.at[b, q]
+            )
+            for q in (0, 1)
+        ]
+    def tile_start(i, b):
+        @pl.when(i < 4)
+        def _():
+            for copy in tile_load(act_all, i, b):
+                copy.start()
+        @pl.when((i >= 4) & (i < 8))
+        def _():
+            for copy in tile_load(dy_all, i, b):
+                copy.start()
+    def gu_store(i, b):
+        return pltpu.make_async_copy(gub.at[b], gu_o.at[feature(i, b)], gsem.at[0, b])
+    def down_store(i, b):
+        return pltpu.make_async_copy(downb.at[b], down_o.at[feature(i, b)], gsem.at[1, b])
+    for copy in fixed:
+        copy.start()
+    tile_start(0, 0)
+    for copy in fixed:
+        copy.wait()
+
+    @pl.loop(0, 8)
+    def _(i):
+        @pl.when(i == 2)
         def _():
             second(3); third(2)
-        @pl.when(j == 8)
+        @pl.when(i == 4)
         def _(): third(3)
-        forward_out(j)
+        for b in (0, 1):
+            tile_start(i + b, 1 - b)
+            forward_out(2 * i + b)
+            for copy in tile_load(act_all, i, b):
+                copy.wait()
+            base = 768 + 512 * b
+            @pl.when((i > 0) & (i < 5))
+            def _(): gu_store(i, b).wait()
+            @pl.when(i > 4)
+            def _(): down_store(i, b).wait()
+            @pl.when(i < 4)
+            def _():
+                out = tn(flat(base, 256), flat(0, 256)) + tn(flat(base + 256, 256), flat(256, 256))
+                gub[b] = out.astype(bf16)
+                gu_store(i, b).start()
+            @pl.when(i >= 4)
+            def _():
+                out = tn(flat(base, 256), flat(512, 128)) + tn(flat(base + 256, 256), flat(640, 128))
+                downb[b] = out.astype(bf16)
+                down_store(i, b).start()
+    for b in (0, 1):
+        down_store(7, b).wait()
     me = at(z, x, y)
     for g in (1, 2, 3):
         rz_wait(nearest(z, g))
@@ -720,20 +778,20 @@
         out_shape=[
             S((rows, width), f32), S((32, rows, width), bf16), S((16, cap, width), bf16),
             S((16, cap, hidden), bf16), S((16, cap, hidden), bf16), S((16, cap, hidden), bf16),
-            S((16, 2 * rows, 128), bf16), S((16, 2 * rows, 256), bf16),
-            S((16, rows, width), bf16), S((32, rows, width), bf16),
+            S((32, rows, 128), bf16), S((32, rows, 256), bf16),
+            S((16, rows, width), bf16), S((32, rows, width), bf16), S((width, 256), bf16), S((width, 128), bf16),
         ],
         in_specs=[vm, any_, any_, vm, vm, vm] + [any_] * 6,
-        out_specs=[vm] + [any_] * 9,
+        out_specs=[vm] + [any_] * 11,
         scratch_shapes=[
             V(*wg.shape), V(*wu.shape), V(*wd.shape), V(*sgu.shape), V(256, width),
             V(16, rows, width), V(16, rows, width), V(8, h, width), V(4, h, width), V(8, h, width), V(4, h, width),
             V(4, rows, width),
             V(2 * cap, hidden, t=f32), V(2 * cap, hidden, t=f32), V(2 * cap, hidden, t=f32),
             V(2 * cap, hidden), V(2 * cap, hidden), V(2 * cap, hidden),
-            V(*sd.shape), V(16, 2 * rows, 128, t=f32), V(2, 2 * rows, 128), V(2, 2 * rows, 256),
-            V(2, cap, hidden), V(2, 2 * rows, 128), V(2, 2, rows, width),
-            D((6,)), D((2, 3)), D((2, 7)), D((2, 2)), D((2,)), D,
+            V(*sd.shape), V(16, 2 * rows, 128, t=f32), V(4, rows, 128), V(4, rows, 256),
+            V(2, cap, hidden), V(2, 2, rows, 128), V(2, 2, rows, width), V(2, 256, 256), V(2, 256, 128),
+            D((6,)), D((2, 3)), D((2, 7)), D((2, 2)), D((2,)), D, D((2, 2)), D((2, 2)), D((4,)),
             D((4, 2)), D((4,)), D((4,)), D((4,)), D((4, 2)), D((4, 2)), D((4, 2)), D((4, 2)), D((4,)), D((4,)), D((16, 2)), D((16, 2)),
             D((4,)), D((16,)), D((16,)), D((4, 2)), D((4, 2)), D((4,)), D((4,)), D((4, 2)), D((4, 2)), D((4,)), D((4,)),
             D((4,)), D((4,)),
@@ -1105,31 +1163,28 @@
     )(a1, dattn, dq, dk, dv, mixed, gains, out_half, tok_half)
 
 
-def expert_grads_kernel(deg, deu, eh, dsgu, hs, rows, deo, act, dy, e_gate, e_up, e_down, gu, down):
+def expert_grads_kernel(deg, deu, eh, rows, deo, e_gate, e_up, e_down):
     def tn(left, right):
         return lax.dot_general(left, right, (((0,), (0,)), ((), ())), preferred_element_type=jnp.float32)
-    gu[...] = tn(act[...], dsgu[...]).astype(gu.dtype)
-    down[...] = tn(dy[...], hs[...]).astype(down.dtype)
     e_gate[...] = tn(deg[...], rows[...])
     e_up[...] = tn(deu[...], rows[...])
     e_down[...] = tn(eh[...], deo[...])
 
 
-def expert_grads(deg, deu, eh, dsgu, hs, rows, deo, act, dy):
+def expert_grads(deg, deu, eh, rows, deo):
     width = rows.shape[1]
-    S = jax.ShapeDtypeStruct
     whole = lambda a: pl.BlockSpec(a.shape, lambda i: (0, 0), pipeline_mode=pl.Buffered(1))
     tile = lambda n: pl.BlockSpec((n, 256), lambda i: (0, i))
     hidden = deg.shape[1]
     return pl.pallas_call(
         expert_grads_kernel,
         grid=(width // 256,),
-        out_shape=[S((hidden, width), jnp.float32)] * 3 + [S((width, 256), jnp.bfloat16), S((width, 128), jnp.bfloat16)],
-        in_specs=[whole(a) for a in (deg, deu, eh, dsgu, hs)] + [tile(a.shape[0]) for a in (rows, deo, act, dy)],
-        out_specs=[tile(hidden)] * 3 + [pl.BlockSpec((256, n), lambda i: (i, 0)) for n in (256, 128)],
+        out_shape=[jax.ShapeDtypeStruct((hidden, width), jnp.float32)] * 3,
+        in_specs=[whole(a) for a in (deg, deu, eh)] + [tile(a.shape[0]) for a in (rows, deo)],
+        out_specs=[tile(hidden)] * 3,
         compiler_params=pltpu.CompilerParams(vmem_limit_bytes=60 << 20),
         name="expert_grads",
-    )(deg, deu, eh, dsgu, hs, rows, deo, act, dy)
+    )(deg, deu, eh, rows, deo)
 
 
 def attention_kernel(
@@ -1508,22 +1563,20 @@
     )
     weights = [w.reshape(width, -1) for w in (query_whole, key_whole, value_whole, output_whole)]
 
-    total_grad, act_all, rows, hidden_rows, gate_rows_grad, up_rows_grad, common_hidden, common_gu_grad, unused, ffn = (
+    (
+        total_grad, unused_act, rows, hidden_rows, gate_rows_grad, up_rows_grad, unused_hidden, unused_grad, unused_part, ffn,
+        gu_grad, down_grad,
+    ) = (
         expert_layer(
             act_two, hidden_rows_grad, grad_all, rank_row, rank_col, slot_gate,
             exp_gate, exp_up, exp_down, common_gu, common_down.T[front:], common_down, 1,
         )
     )
-    act_all = act_all.reshape(-1, width)
-    grad_all = grad_all.reshape(-1, width)
     rows = rows.reshape(slots, width)
     rows_out_grad = rows_out_grad.reshape(slots, width)
     hidden_rows = hidden_rows.reshape(slots, -1)
-    common_hidden = common_hidden.reshape(-1, 128)
-    common_gu_grad = common_gu_grad.reshape(-1, 256)
-    expert_gate_grad, expert_up_grad, expert_down_grad, gu_grad, down_grad = expert_grads(
-        gate_rows_grad.reshape(slots, -1), up_rows_grad.reshape(slots, -1), hidden_rows,
-        common_gu_grad, common_hidden, rows, rows_out_grad, act_all, grad_all,
+    expert_gate_grad, expert_up_grad, expert_down_grad = expert_grads(
+        gate_rows_grad.reshape(slots, -1), up_rows_grad.reshape(slots, -1), hidden_rows, rows, rows_out_grad
     )
     common_w_grad = jnp.concatenate(
         [w[:, front : front + common_dev] for w in (gu_grad[:, :128], gu_grad[:, 128:], down_grad)], axis=1

time: 785 us -> 774 us (0.986)
  Pallas kernels: 723 us -> 714 us
    pallas_call x1, Pallas kernels: 47 us -> 32.5 us  [expert_grads(): pl.pallas_call(expert_grads_kernel, grid=(width // 256,), out_shape=[jax....]
  transfers between devices with their start and end apart: 2 -> 2, of which waited for: 0 -> 0; matrix products, arithmetic and copies ran while one was open for 1% -> 1% of each run, Pallas kernels for 57% -> 62%
where the time goes in v5:
time: 774 us; the launch traced here: 764 us
  Pallas kernels  714 us (92%)
  local copies, waits for them, and re-layouts  24.5 us (3%)
  starting transfers between devices  16.5 us (2%)
    pallas_call x1, Pallas kernels, expert_layer(): pl.pallas_call(expert_kernel, out_shape=[S((rows, width), f32), S((32, ro...  240 us
    pallas_call x1, Pallas kernels, attention_layer(): pl.pallas_call(attention_kernel, out_shape=[S((16, depth, hw), bf16)] * 4...  208 us
    pallas_call x1, Pallas kernels, attention_back(): pl.pallas_call(attention_back_kernel, out_shape=[S((rows, width), bf16),...  127 us
    pallas_call x1, Pallas kernels, weight_grads(): pl.pallas_call(weight_grad_kernel, out_shape=[S((depth, hw), f32)] * 4 +...  107 us
    pallas_call x1, Pallas kernels, expert_grads(): pl.pallas_call(expert_grads_kernel, grid=(width // 256,), out_shape=[jax....  32.5 us
  transfers between devices with their start and end apart: 2, of which 0 were waited for; matrix products, arithmetic and copies ran while one was open for 1% of the time, Pallas kernels for 62%

profile of v5, /device:TPU:0, one launch (start us, length us, event | category | flops | bytes accessed | tf_op | source)
XLA Modules:
  0.0 764.0 jit_solution(2138817802687830237)
XLA Ops:
  0.6 1.2 copy.66
  1.8 1.2 copy.67
  3.1 1.2 copy.68
  4.4 1.1 copy.69
  5.5 7.5 all-to-all-start
  14.3 0.9 pad_maximum_fusion.1
  15.9 207.8 %attention_layer.1 = (bf16[16,128,1024]{2,1,0:T(8,128)(2,1)}, bf16[16,128,1024]{2,1,0:T(8,128)(2,1)}, bf16[16,128,1024]{2,1,0:T(8,128)(2,1)}, bf16[16,128,1024]{...) custom-call(bf16[320,2048]{1,0:T(8,128)(2,1)} %x_in.3, ...), custom_call_target="tpu_custom_call" | custom-call | tf_op jit(solution)/shard_map/attention_layer/pallas_call | solution.py:1485
  224.7 1.0 fusion.9
  225.9 1.0 copy.73.sdt_h
  226.8 1.4 fusion.2.sgu_h
  228.2 240.0 %expert_layer.1 = (f32[160,2048]{1,0:T(8,128)}, bf16[32,160,2048]{2,1,0:T(8,128)(2,1)}, bf16[16,160,2048]{2,1,0:T(8,128)(2,1)}, bf16[16,160,704]{2,1,0:T(8,128)(...) custom-call(bf16[160,2048]{1,0:T(8,128)(2,1)} %get-tuple-element.59., ...), custom_call_target="tpu_custom_call" | custom-call | tf_op jit(solution)/shard_map/expert_layer/pallas_call | solution.py:776
  468.2 1.2 slice.62
  469.5 1.6 fusion.8
  471.0 0.8 pad_maximum_fusion
  471.8 1.5 copy.75
  473.4 9.0 %all-to-all-start.1 = ((bf16[16,128,264]{1,2,0:T(8,128)(2,1)}), bf16[16,128,264]{1,2,0:T(8,128)(2,1)}, u32[]{:S(2)}, u32[]{:S(2)}) async-start(bf16[16,128,264]{1,2,0:T(8,128)(2,1)} %copy.75), calls=%async_computation.1 | async-start | bytes 2162688 | tf_op jit(solution)/shard_map/all_to_all | solution.py:1585
  482.5 1.5 fusion.10
  484.0 127.5 %attention_back.1 = (bf16[160,2048]{1,0:T(8,128)(2,1)}, bf16[160,2048]{1,0:T(8,128)(2,1)}, bf16[2,160,2048]{2,1,0:T(8,128)(2,1)}, bf16[320,1024]{1,0:T(8,128)(2,...) custom-call(bf16[32,160,2048]{2,1,0:T(8,128)(2,1)} %get-tuple-element.65.part, ...), custom_call_target="tpu_custom_call" | custom-call | tf_op jit(solution)/shard_map/attention_back/pallas_call | solution.py:1001
  611.5 0.8 maximum_maximum_fusion
  612.9 106.6 %weight_grads.1 = (f32[128,1024]{1,0:T(8,128)}, f32[128,1024]{1,0:T(8,128)}, f32[128,1024]{1,0:T(8,128)}, f32[128,1024]{1,0:T(8,128)}, f32[8,128]{1,0:T(8,128)},...) custom-call(bf16[320,2048]{1,0:T(8,128)(2,1)} %get-tuple-element.58.a1, bf16[320,2048]{1,0:T(8,128)(2,1)} %bitcast.80, ...), custom_call_target="tpu_custom_call" | custom-call | tf_op jit(solution)/shard_map/weight_grads/pallas_call | solution.py:1151
  719.6 32.5 %expert_grads.1 = (f32[704,2048]{1,0:T(8,128)}, f32[704,2048]{1,0:T(8,128)}, f32[704,2048]{1,0:T(8,128)}) custom-call(bf16[2560,704]{1,0:T(8,128)(2,1)} %bitcast.67, bf16[2560,704]{1,0:T(8,128)(2,1)} %bitcast.68, bf16[2560,704]{1,0:T(8,128)(2,1)} %bitcast.66, bf16[2560,2048]{1,0:T(8,128)(2,1)} %bitcast.59, bf16[2560,2048]{1,0:T(8,128)(2,1)} %bitcast.58), custom_call_target="tpu_custom_call" | custom-call | tf_op jit(solution)/shard_map/expert_grads/pallas_call | solution.py:1179
  752.0 1.3 slice_bitcast_fusion
  753.3 1.4 convert_bitcast_fusion
  754.9 1.1 copy.78
  756.0 1.1 copy.77
  757.1 1.1 copy.76
  758.2 1.1 copy.87
  759.3 1.1 copy.88
  760.4 0.8 copy.89
  761.2 0.8 copy.90
  762.0 0.8 copy.91
  762.8 0.8 copy.92
  (38 shorter events, 4.2 us)
Async XLA Ops:
  4.4 8.7 %copy-start.6 = (f32[320,6]{0,1:T(8,128)S(1)}, f32[320,6]{0,1:T(8,128)}, u32[]{:S(2)}) copy-start(f32[320,6]{0,1:T(8,128)} %param.19) | copy-start | bytes 23044
  4.4 8.7 %copy-start.7 = (s32[320,6]{0,1:T(8,128)S(1)}, s32[320,6]{0,1:T(8,128)}, u32[]{:S(2)}) copy-start(s32[320,6]{0,1:T(8,128)} %param.18) | copy-start | bytes 23044
  5.5 9.7 %copy-start.8 = (bf16[128]{0:T(256)(128)(2,1)S(1)}, bf16[128]{0:T(256)(128)(2,1)}, u32[]{:S(2)}) copy-start(bf16[128]{0:T(256)(128)(2,1)} %param.25) | copy-start | bytes 772
  5.5 9.7 %copy-start.9 = (bf16[128]{0:T(256)(128)(2,1)S(1)}, bf16[128]{0:T(256)(128)(2,1)}, u32[]{:S(2)}) copy-start(bf16[128]{0:T(256)(128)(2,1)} %param.20) | copy-start | bytes 772
  5.5 218.2 %all-to-all-start = ((bf16[16,3,128,88]{2,3,1,0:T(8,128)(2,1)}), bf16[16,3,128,88]{2,3,1,0:T(8,128)(2,1)S(1)}, u32[]{:S(2)}, u32[]{:S(2)}) async-start(bf16[16,3,128,88]{2,3,1,0:T(8,128)(2,1)} %copy.69), calls=%async_computation | async-start | bytes 2162688 | tf_op jit(solution)/shard_map/all_to_all | solution.py:1547
  473.4 279.9 %all-to-all-start.1 = ((bf16[16,128,264]{1,2,0:T(8,128)(2,1)}), bf16[16,128,264]{1,2,0:T(8,128)(2,1)}, u32[]{:S(2)}, u32[]{:S(2)}) async-start(bf16[16,128,264]{1,2,0:T(8,128)(2,1)} %copy.75), calls=%async_computation.1 | async-start | bytes 2162688 | tf_op jit(solution)/shard_map/all_to_all | solution.py:1585
  754.8 3.4 copy-start.1
  757.1 2.2 copy-start
  758.2 2.1 copy-start.5
  759.3 1.9 copy-start.4
  759.3 2.7 copy-start.3
  760.4 2.4 copy-start.2

commit v6 on v5

--- a/solution.py
+++ b/solution.py
@@ -706,10 +706,10 @@
 
     @pl.loop(0, 8)
     def _(i):
-        @pl.when(i == 2)
+        @pl.when(i == 1)
         def _():
             second(3); third(2)
-        @pl.when(i == 4)
+        @pl.when(i == 3)
         def _(): third(3)
         for b in (0, 1):
             tile_start(i + b, 1 - b)

time: 774 us -> 771 us (level)
  no operation moved by 1% of the time
where the time goes in v6:
time: 771 us; the launch traced here: 760 us
  Pallas kernels  710 us (92%)
  local copies, waits for them, and re-layouts  24.5 us (3%)
  starting transfers between devices  16.9 us (2%)
    pallas_call x1, Pallas kernels, expert_layer(): pl.pallas_call(expert_kernel, out_shape=[S((rows, width), f32), S((32, ro...  236 us
    pallas_call x1, Pallas kernels, attention_layer(): pl.pallas_call(attention_kernel, out_shape=[S((16, depth, hw), bf16)] * 4...  208 us
    pallas_call x1, Pallas kernels, attention_back(): pl.pallas_call(attention_back_kernel, out_shape=[S((rows, width), bf16),...  127 us
    pallas_call x1, Pallas kernels, weight_grads(): pl.pallas_call(weight_grad_kernel, out_shape=[S((depth, hw), f32)] * 4 +...  107 us
    pallas_call x1, Pallas kernels, expert_grads(): pl.pallas_call(expert_grads_kernel, grid=(width // 256,), out_shape=[jax....  32.5 us
  transfers between devices with their start and end apart: 2, of which 0 were waited for; matrix products, arithmetic and copies ran while one was open for 1% of the time, Pallas kernels for 62%

profile of v6, /device:TPU:0, one launch (start us, length us, event | category | flops | bytes accessed | tf_op | source)
XLA Modules:
  0.0 760.5 jit_solution(6265134561112071982)
XLA Ops:
  0.6 1.2 copy.66
  1.8 1.2 copy.67
  3.1 1.2 copy.68
  4.4 1.1 copy.69
  5.5 7.5 all-to-all-start
  14.3 0.9 pad_maximum_fusion.1
  15.9 207.8 %attention_layer.1 = (bf16[16,128,1024]{2,1,0:T(8,128)(2,1)}, bf16[16,128,1024]{2,1,0:T(8,128)(2,1)}, bf16[16,128,1024]{2,1,0:T(8,128)(2,1)}, bf16[16,128,1024]{...) custom-call(bf16[320,2048]{1,0:T(8,128)(2,1)} %x_in.3, ...), custom_call_target="tpu_custom_call" | custom-call | tf_op jit(solution)/shard_map/attention_layer/pallas_call | solution.py:1485
  224.7 1.0 fusion.9
  225.9 1.0 copy.73.sdt_h
  226.8 1.4 fusion.2.sgu_h
  228.2 236.1 %expert_layer.1 = (f32[160,2048]{1,0:T(8,128)}, bf16[32,160,2048]{2,1,0:T(8,128)(2,1)}, bf16[16,160,2048]{2,1,0:T(8,128)(2,1)}, bf16[16,160,704]{2,1,0:T(8,128)(...) custom-call(bf16[160,2048]{1,0:T(8,128)(2,1)} %get-tuple-element.59., ...), custom_call_target="tpu_custom_call" | custom-call | tf_op jit(solution)/shard_map/expert_layer/pallas_call | solution.py:776
  464.3 1.2 slice.62
  465.5 1.6 fusion.8
  467.1 0.8 pad_maximum_fusion
  467.9 1.5 copy.75
  469.5 9.4 %all-to-all-start.1 = ((bf16[16,128,264]{1,2,0:T(8,128)(2,1)}), bf16[16,128,264]{1,2,0:T(8,128)(2,1)}, u32[]{:S(2)}, u32[]{:S(2)}) async-start(bf16[16,128,264]{1,2,0:T(8,128)(2,1)} %copy.75), calls=%async_computation.1 | async-start | bytes 2162688 | tf_op jit(solution)/shard_map/all_to_all | solution.py:1585
  479.0 1.5 fusion.10
  480.5 127.5 %attention_back.1 = (bf16[160,2048]{1,0:T(8,128)(2,1)}, bf16[160,2048]{1,0:T(8,128)(2,1)}, bf16[2,160,2048]{2,1,0:T(8,128)(2,1)}, bf16[320,1024]{1,0:T(8,128)(2,...) custom-call(bf16[32,160,2048]{2,1,0:T(8,128)(2,1)} %get-tuple-element.65.part, ...), custom_call_target="tpu_custom_call" | custom-call | tf_op jit(solution)/shard_map/attention_back/pallas_call | solution.py:1001
  608.0 0.8 maximum_maximum_fusion
  609.4 106.6 %weight_grads.1 = (f32[128,1024]{1,0:T(8,128)}, f32[128,1024]{1,0:T(8,128)}, f32[128,1024]{1,0:T(8,128)}, f32[128,1024]{1,0:T(8,128)}, f32[8,128]{1,0:T(8,128)},...) custom-call(bf16[320,2048]{1,0:T(8,128)(2,1)} %get-tuple-element.58.a1, bf16[320,2048]{1,0:T(8,128)(2,1)} %bitcast.80, ...), custom_call_target="tpu_custom_call" | custom-call | tf_op jit(solution)/shard_map/weight_grads/pallas_call | solution.py:1151
  716.1 32.5 %expert_grads.1 = (f32[704,2048]{1,0:T(8,128)}, f32[704,2048]{1,0:T(8,128)}, f32[704,2048]{1,0:T(8,128)}) custom-call(bf16[2560,704]{1,0:T(8,128)(2,1)} %bitcast.67, bf16[2560,704]{1,0:T(8,128)(2,1)} %bitcast.68, bf16[2560,704]{1,0:T(8,128)(2,1)} %bitcast.66, bf16[2560,2048]{1,0:T(8,128)(2,1)} %bitcast.59, bf16[2560,2048]{1,0:T(8,128)(2,1)} %bitcast.58), custom_call_target="tpu_custom_call" | custom-call | tf_op jit(solution)/shard_map/expert_grads/pallas_call | solution.py:1179
  748.5 1.3 slice_bitcast_fusion
  749.8 1.4 convert_bitcast_fusion
  751.4 1.1 copy.78
  752.5 1.1 copy.77
  753.6 1.1 copy.76
  754.7 1.1 copy.87
  755.8 1.1 copy.88
  756.9 0.8 copy.89
  757.7 0.8 copy.90
  758.5 0.8 copy.91
  759.3 0.8 copy.92
  (38 shorter events, 4.2 us)
Async XLA Ops:
  4.4 8.7 %copy-start.6 = (f32[320,6]{0,1:T(8,128)S(1)}, f32[320,6]{0,1:T(8,128)}, u32[]{:S(2)}) copy-start(f32[320,6]{0,1:T(8,128)} %param.19) | copy-start | bytes 23044
  4.4 8.7 %copy-start.7 = (s32[320,6]{0,1:T(8,128)S(1)}, s32[320,6]{0,1:T(8,128)}, u32[]{:S(2)}) copy-start(s32[320,6]{0,1:T(8,128)} %param.18) | copy-start | bytes 23044
  5.5 9.7 %copy-start.8 = (bf16[128]{0:T(256)(128)(2,1)S(1)}, bf16[128]{0:T(256)(128)(2,1)}, u32[]{:S(2)}) copy-start(bf16[128]{0:T(256)(128)(2,1)} %param.25) | copy-start | bytes 772
  5.5 9.7 %copy-start.9 = (bf16[128]{0:T(256)(128)(2,1)S(1)}, bf16[128]{0:T(256)(128)(2,1)}, u32[]{:S(2)}) copy-start(bf16[128]{0:T(256)(128)(2,1)} %param.20) | copy-start | bytes 772
  5.5 218.2 %all-to-all-start = ((bf16[16,3,128,88]{2,3,1,0:T(8,128)(2,1)}), bf16[16,3,128,88]{2,3,1,0:T(8,128)(2,1)S(1)}, u32[]{:S(2)}, u32[]{:S(2)}) async-start(bf16[16,3,128,88]{2,3,1,0:T(8,128)(2,1)} %copy.69), calls=%async_computation | async-start | bytes 2162688 | tf_op jit(solution)/shard_map/all_to_all | solution.py:1547
  469.5 280.4 %all-to-all-start.1 = ((bf16[16,128,264]{1,2,0:T(8,128)(2,1)}), bf16[16,128,264]{1,2,0:T(8,128)(2,1)}, u32[]{:S(2)}, u32[]{:S(2)}) async-start(bf16[16,128,264]{1,2,0:T(8,128)(2,1)} %copy.75), calls=%async_computation.1 | async-start | bytes 2162688 | tf_op jit(solution)/shard_map/all_to_all | solution.py:1585
  751.3 3.4 copy-start.1
  753.6 2.2 copy-start
  754.7 2.1 copy-start.5
  755.8 1.9 copy-start.4
  755.8 2.7 copy-start.3
  756.9 2.4 copy-start.2
